TPU v7x, 32 devices: a whole 2x2x4 slice. The times are simulated.
32 devices in a mesh: groups: 2 (over x), slab: 16 (over z, y, core).
Axes of the slice: x: 2, y: 2, z: 4, core: 2. Of those that a mesh axis runs over, the one named last changes fastest.
Arguments:
- mode_shapes: float32 [16384, 192], P(('groups', 'slab')), parts along dimension 0, may hold values from -6 to 6
- wall_coupling: float32 [16384, 15], P(('groups', 'slab')), parts along dimension 0, may hold values from -3.5 to 3.5
- owner_dev: int32 [16384, 1], P(('groups', 'slab')), parts along dimension 0, may hold values from 0 to 15; in each aligned block of 512 rows (0 to 511, 512 to 1023, ...) at most 64 rows name the same one
- owner_cell: int32 [16384], P(('groups', 'slab')), parts along dimension 0, may hold values from 0 to 2047
- neighbours: int32 [6, 65536], P(None, ('groups', 'slab')), parts along dimension 1, may hold values from -1 to 32767, as said below
- coupling_blocks: float32 [6, 5, 5, 65536], P(None, None, None, ('groups', 'slab')), parts along dimension 3, may hold values from -0.3 to 0.3
- inv_blocks: float32 [5, 5, 65536], P(None, None, ('groups', 'slab')), parts along dimension 2, may hold values from -0.9 to 3, as said below
Outputs:
- modes_basis: float32 [5, 64, 65536], P(None, None, ('groups', 'slab')), parts along dimension 2
- factor: float32 [128, 64], P('groups'), parts along dimension 0
There are 2 independent parts, one for each index of `groups`. A program takes and returns all parts, laid end to end along the dimension named above; each array names one. Nothing has to cross between parts.
Inputs may be any that keep to these rules, and one draw needn't show every extreme that they name: `owner_dev`: in the rows of one slab device at most 64 shell nodes name the same slab, a bound that some of them reach. `neighbours`: A filled slot of cell c names a cell whose number differs from c by 1 to 256. `inv_blocks`: each block has a positive diagonal entry shared by its five diagonal places and off-diagonal entries of at most 0.3 times it in magnitude.
All inputs are finite; a program needn't handle non-finite values.
Results may differ from a plain program's by a relative error of at most 0.0003.
Values sent between devices are 32-bit elements; how exact they have to be, the bound alone decides.
No kernel may reach another device: no remote copies, remote signals or barrier semaphores. Data moves between devices by JAX's collectives and lax.ppermute only.
A program may use at most 192 MiB of HBM per device.

v0:
```python
import math

import jax
import jax.numpy as jnp
from jax import lax
from jax.sharding import PartitionSpec as P

VARS = 5
NBR = 6
SWEEPS = 2


def with_halo(x, sides, width):
    for axis, dim in sides:
        count, length = (lax.axis_size(axis), x.shape[dim])
        up = [(i, (i + 1) % count) for i in range(count - 1)]
        down = [(j, i) for i, j in up]
        last = lax.slice_in_dim(x, length - width, length, axis=dim)
        first = lax.slice_in_dim(x, 0, width, axis=dim)
        before = lax.ppermute(last, axis, up)
        after = lax.ppermute(first, axis, down)
        x = jnp.concatenate([before, x, after], axis=dim)
    return x


def apply_blocks(blocks, field_in):
    rows_out = []
    for out_var in range(field_in.shape[0]):
        summed = blocks[out_var, 0][None, :] * field_in[0]
        for in_var in range(1, field_in.shape[0]):
            summed = summed + blocks[out_var, in_var][None, :] * field_in[in_var]
        rows_out.append(summed)
    return jnp.stack(rows_out)


def couple(weights, shapes):
    node_count = weights.shape[0]
    modes_total = shapes.shape[1] // 3
    weights_split = weights.reshape(node_count, -1, 3)
    shapes_split = shapes.reshape(node_count, 3, modes_total)
    summed = weights_split[:, :, 0, None] * shapes_split[:, None, 0, :]
    for component in range(1, 3):
        summed = summed + weights_split[:, :, component, None] * shapes_split[:, None, component, :]
    return summed.reshape(node_count, -1)


def gram_matrix(left_field, right_field):
    return jnp.einsum("vpc,vqc->pq", left_field, right_field, precision=lax.Precision.HIGHEST)


def combine(coeffs, field_in):
    return jnp.einsum("pq,vpc->vqc", coeffs, field_in, precision=lax.Precision.HIGHEST)


def cholesky_upper(gram):
    order = gram.shape[0]
    places = jnp.arange(order, dtype=jnp.int32)

    def column_step(column_at, lower):
        row_now = lax.dynamic_index_in_dim(lower, column_at, 0, keepdims=False)
        target = lax.dynamic_index_in_dim(gram, column_at, 1, keepdims=False)
        reduced = target - jnp.dot(lower, row_now, precision=lax.Precision.HIGHEST)
        pivot = jnp.sqrt(lax.dynamic_index_in_dim(reduced, column_at, 0, keepdims=False))
        column = jnp.where(
            places > column_at, reduced / pivot, jnp.where(places == column_at, pivot, 0.0)
        )
        return jnp.where(places[None, :] == column_at, column[:, None], lower)

    lower = lax.fori_loop(0, order, column_step, jnp.zeros((order, order), jnp.float32))
    return lower.T


def upper_inverse(upper):
    lower = upper.T
    order = lower.shape[0]
    places = jnp.arange(order, dtype=jnp.int32)
    identity = jnp.eye(order, dtype=jnp.float32)

    def row_step(row_at, inverse):
        lower_row = lax.dynamic_index_in_dim(lower, row_at, 0, keepdims=False)
        pivot = lax.dynamic_index_in_dim(lower_row, row_at, 0, keepdims=False)
        earlier = jnp.where(places < row_at, lower_row, 0.0)
        unit_row = lax.dynamic_index_in_dim(identity, row_at, 0, keepdims=False)
        new_row = (unit_row - jnp.dot(earlier, inverse, precision=lax.Precision.HIGHEST)) / pivot
        return jnp.where(places[:, None] == row_at, new_row[None, :], inverse)

    inverse = lax.fori_loop(0, order, row_step, jnp.zeros((order, order), jnp.float32))
    return inverse.T


def local(
    mode_shapes, wall_coupling, owner_dev, owner_cell, neighbours, coupling_blocks, inv_blocks
):
    devices_slab = lax.axis_size("slab")
    cell_count = inv_blocks.shape[2]
    node_count = mode_shapes.shape[0]
    modes_total = mode_shapes.shape[1] // 3
    capacity = max(2, 2 * node_count // devices_slab)
    destination = owner_dev[:, 0]
    onehot_dest = (
        destination[:, None] == jnp.arange(devices_slab, dtype=jnp.int32)[None, :]
    ).astype(jnp.int32)
    ranking = jnp.sum((jnp.cumsum(onehot_dest, axis=0) - 1) * onehot_dest, axis=1)
    slot_of = destination * capacity + ranking
    slot_total = devices_slab * capacity
    cell_tags = (
        jnp.full((slot_total,), -1.0, jnp.float32).at[slot_of].set(owner_cell.astype(jnp.float32))
    )
    contribution = couple(wall_coupling, mode_shapes)
    outgoing = (
        jnp.zeros((slot_total, contribution.shape[1]), jnp.float32).at[slot_of].set(contribution)
    )
    arrived, arrived_tags = (
        lax.all_to_all(outgoing, "slab", split_axis=0, concat_axis=0, tiled=True),
        lax.all_to_all(cell_tags, "slab", split_axis=0, concat_axis=0, tiled=True),
    )
    matches = (
        arrived_tags.astype(jnp.int32)[:, None] == jnp.arange(cell_count, dtype=jnp.int32)[None, :]
    ).astype(jnp.float32)
    forcing = lax.dot_general(
        arrived, matches, (((0,), (0,)), ((), ())), precision=lax.Precision.HIGHEST
    )
    forcing = forcing.reshape(VARS, modes_total, cell_count)
    rim_width = cell_count // 8
    first_cell = lax.axis_index("slab") * cell_count - rim_width
    local_ids = jnp.where(neighbours >= 0, neighbours - first_cell, cell_count + 2 * rim_width)
    state_field = apply_blocks(inv_blocks, forcing)
    for sweep_step in range(SWEEPS):
        widened = with_halo(state_field, (("slab", 2),), rim_width)
        padded = jnp.concatenate(
            [widened, jnp.zeros(widened.shape[:2] + (1,), jnp.float32)], axis=2
        )
        coupled = jnp.zeros_like(state_field)
        for slot_index in range(NBR):
            gathered = jnp.take(padded, local_ids[slot_index], axis=2)
            coupled = coupled + apply_blocks(coupling_blocks[slot_index], gathered)
        state_field = apply_blocks(inv_blocks, forcing - coupled)
    block_width = modes_total // 4
    factor = jnp.zeros((modes_total, modes_total), jnp.float32)
    basis_parts = []
    for block_index in range(4):
        start_col = block_index * block_width
        panel_cols = state_field[:, start_col : start_col + block_width, :]
        if block_index > 0:
            previous = jnp.concatenate(basis_parts, axis=1)
            projection = lax.psum(gram_matrix(previous, panel_cols), "slab")
            panel_cols = panel_cols - combine(projection, previous)
            factor = factor.at[:start_col, start_col : start_col + block_width].set(projection)
        diag_block = cholesky_upper(lax.psum(gram_matrix(panel_cols, panel_cols), "slab"))
        factor = factor.at[
            start_col : start_col + block_width, start_col : start_col + block_width
        ].set(diag_block)
        basis_parts.append(combine(upper_inverse(diag_block), panel_cols))
    basis_out = jnp.concatenate(basis_parts, axis=1)
    norm_scale = math.sqrt(VARS * cell_count * devices_slab)
    return (basis_out * norm_scale, factor / norm_scale)


def solution(mesh):
    in_specs = (
        P(("groups", "slab"), None),
        P(("groups", "slab"), None),
        P(("groups", "slab"), None),
        P(("groups", "slab")),
        P(None, ("groups", "slab")),
        P(None, None, None, ("groups", "slab")),
        P(None, None, ("groups", "slab")),
    )
    out_specs = (P(None, None, ("groups", "slab")), P("groups", None))
    return jax.shard_map(local, mesh=mesh, in_specs=in_specs, out_specs=out_specs, check_vma=False)
```

profile of v0, /device:TPU:0, one launch (start us, length us, event | category | flops | bytes accessed | tf_op | source)
XLA Modules:
  0.0 1054.8 jit_solution(16598022416229044817)
XLA Ops:
  8.1 7.4 all-to-all-start.1
  52.9 27.0 %all-to-all-done = f32[16,64,320]{2,1,0:T(8,128)S(1)} async-done(((f32[16,64,320]{2,1,0:T(8,128)}), f32[16,64,320]{2,1,0:T(8,128)S(1)}, u32[]{:S(2)}, u32[]{:S(2)}) %all-to-all-start) | async-done | bytes 1310752 | tf_op jit(solution)/shard_map/all_to_all | solution.py:114
  98.3 7.6 copy.130
  105.9 19.7 %gather_fusion.5 = f32[2048,5,64]{2,1,0:T(8,128)} fusion(f32[5,64,2561]{1,0,2:T(8,128)} %copy.130, s32[2048]{0:T(1024)} %get-tuple-element.1568), kind=kCustom, calls=%fused_computation.5.clone | custom fusion | bytes 5251072 | tf_op jit(solution)/shard_map/jit(_take)/gather | solution.py:135
  131.7 19.6 %gather_fusion.4 = f32[2048,5,64]{2,1,0:T(8,128)} fusion(f32[5,64,2561]{1,0,2:T(8,128)} %copy.130, s32[2048]{0:T(1024)S(1)} %copy-done.195), kind=kCustom, calls=%fused_computation.4.clone | custom fusion | bytes 5251072 | tf_op jit(solution)/shard_map/jit(_take)/gather | solution.py:135
  157.4 19.6 %gather_fusion.3 = f32[2048,5,64]{2,1,0:T(8,128)} fusion(f32[5,64,2561]{1,0,2:T(8,128)} %copy.130, s32[2048]{0:T(1024)S(1)} %copy-done.193), kind=kCustom, calls=%fused_computation.3.clone | custom fusion | bytes 5251072 | tf_op jit(solution)/shard_map/jit(_take)/gather | solution.py:135
  183.1 19.6 %gather_fusion.2 = f32[2048,5,64]{2,1,0:T(8,128)} fusion(f32[5,64,2561]{1,0,2:T(8,128)} %copy.130, s32[2048]{0:T(1024)S(1)} %copy-done.198), kind=kCustom, calls=%fused_computation.2.clone | custom fusion | bytes 5251072 | tf_op jit(solution)/shard_map/jit(_take)/gather | solution.py:135
  208.8 19.6 %gather_fusion.1 = f32[2048,5,64]{2,1,0:T(8,128)} fusion(f32[5,64,2561]{1,0,2:T(8,128)} %copy.130, s32[2048]{0:T(1024)S(1)} %copy-done.196), kind=kCustom, calls=%fused_computation.1.clone | custom fusion | bytes 5251072 | tf_op jit(solution)/shard_map/jit(_take)/gather | solution.py:135
  234.5 19.6 %gather_fusion = f32[2048,5,64]{2,1,0:T(8,128)} fusion(f32[5,64,2561]{1,0,2:T(8,128)} %copy.130, s32[2048]{0:T(1024)S(1)} %get-tuple-element.1569), kind=kCustom, calls=%fused_computation.clone | custom fusion | bytes 5251072 | tf_op jit(solution)/shard_map/jit(_take)/gather | solution.py:135
  291.8 7.3 collective-permute-start.2
  304.6 7.6 copy.147
  312.3 19.7 %gather_fusion.11 = f32[2048,5,64]{2,1,0:T(8,128)} fusion(f32[5,64,2561]{1,0,2:T(8,128)} %copy.147, s32[2048]{0:T(1024)} %get-tuple-element.1568), kind=kCustom, calls=%fused_computation.11.clone | custom fusion | bytes 5251072 | tf_op jit(solution)/shard_map/jit(_take)/gather | solution.py:135
  332.0 19.8 %gather_fusion.10 = f32[2048,5,64]{2,1,0:T(8,128)} fusion(f32[5,64,2561]{1,0,2:T(8,128)} %copy.147, s32[2048]{0:T(1024)} %get-tuple-element.1567), kind=kCustom, calls=%fused_computation.10.clone | custom fusion | bytes 5251072 | tf_op jit(solution)/shard_map/jit(_take)/gather | solution.py:135
  351.9 19.7 %gather_fusion.9 = f32[2048,5,64]{2,1,0:T(8,128)} fusion(f32[5,64,2561]{1,0,2:T(8,128)} %copy.147, s32[2048]{0:T(1024)S(1)} %copy-done.194), kind=kCustom, calls=%fused_computation.9.clone | custom fusion | bytes 5251072 | tf_op jit(solution)/shard_map/jit(_take)/gather | solution.py:135
  371.5 19.8 %gather_fusion.8 = f32[2048,5,64]{2,1,0:T(8,128)} fusion(f32[5,64,2561]{1,0,2:T(8,128)} %copy.147, s32[2048]{0:T(1024)} %get-tuple-element.1565), kind=kCustom, calls=%fused_computation.8.clone | custom fusion | bytes 5251072 | tf_op jit(solution)/shard_map/jit(_take)/gather | solution.py:135
  391.4 19.8 %gather_fusion.7 = f32[2048,5,64]{2,1,0:T(8,128)} fusion(f32[5,64,2561]{1,0,2:T(8,128)} %copy.147, s32[2048]{0:T(1024)S(1)} %copy-done.197), kind=kCustom, calls=%fused_computation.7.clone | custom fusion | bytes 5251072 | tf_op jit(solution)/shard_map/jit(_take)/gather | solution.py:135
  411.2 19.7 %gather_fusion.6 = f32[2048,5,64]{2,1,0:T(8,128)} fusion(f32[5,64,2561]{1,0,2:T(8,128)} %copy.147, s32[2048]{0:T(1024)} %copy-done.199), kind=kCustom, calls=%fused_computation.6.clone | custom fusion | bytes 5251072 | tf_op jit(solution)/shard_map/jit(_take)/gather | solution.py:135
  511.8 37.7 %psum.49 = f32[16,16]{1,0:T(8,128)S(1)} all-reduce(f32[16,16]{1,0:T(8,128)S(1)} %convolution_bitcast_fusion.20), channel_id=1, replica_groups=mesh['groups'=2,'slab'=16] {'slab'}, use_global_device_ids=true, to_apply=%region_5.7 | all-reduce | flops 256 | bytes 2048 | tf_op jit(solution)/shard_map/psum | solution.py:149
  549.6 24.4 %while.139 = (s32[]{:T(128)}, f32[16,16]{1,0:T(8,128)S(1)}, f32[16,16]{0,1:T(8,128)S(1)}, s32[]{:T(128)}, s32[]{:T(128)}) while((s32[]{:T(128)}, f32[16,16]{1,0:T(8,128)S(1)}, f32[16,16]{0,1:T(8,128)S(1)}, s32[]{:T(128)}, s32[]{:T(128)}) %tuple.552), condition=%wide.region_7.9_spmd.clone.clone, body=%wide.region_6.8_spmd.clone.clone.sunk | while | flops 3955 | bytes 14736 | solution.py:69
  574.0 34.1 %while.140 = (s32[]{:T(128)}, f32[16,16]{1,0:T(8,128)S(1)}, f32[16,16]{1,0:T(8,128)}, f32[16,16]{1,0:T(8,128)S(1)}, s32[]{:T(128)}, /*index=5*/s32[]{:T(128)}, s32[]{:T(128)}) while((s32[]{:T(128)}, f32[16,16]{1,0:T(8,128)S(1)}, f32[16,16]{1,0:T(8,128)}, f32[16,16]{1,0:T(8,128)S(1)}, s32[]{:T(128)}, ...), condition=%wide.region_9.11_spmd.clone.clone, body=%wide.region_8.10_spmd.clone.clone.sunk | while | flops 3924 | bytes 13155 | solution.py:87
  609.8 30.0 %psum.50 = f32[16,16]{1,0:T(8,128)S(1)} all-reduce(f32[16,16]{1,0:T(8,128)S(1)} %convolution_bitcast_fusion.19), channel_id=1, replica_groups=mesh['groups'=2,'slab'=16] {'slab'}, use_global_device_ids=true, to_apply=%region_10.12 | all-reduce | flops 256 | bytes 2048 | tf_op jit(solution)/shard_map/psum | solution.py:146
  642.6 30.0 %psum.51 = f32[16,16]{1,0:T(8,128)S(1)} all-reduce(f32[16,16]{1,0:T(8,128)S(1)} %convolution_bitcast_fusion.18), channel_id=1, replica_groups=mesh['groups'=2,'slab'=16] {'slab'}, use_global_device_ids=true, to_apply=%region_11.13 | all-reduce | flops 256 | bytes 2048 | tf_op jit(solution)/shard_map/psum | solution.py:149
  672.7 24.4 %while.141 = (s32[]{:T(128)}, f32[16,16]{1,0:T(8,128)S(1)}, f32[16,16]{0,1:T(8,128)S(1)}, s32[]{:T(128)}, s32[]{:T(128)}) while((s32[]{:T(128)}, f32[16,16]{1,0:T(8,128)S(1)}, f32[16,16]{0,1:T(8,128)S(1)}, s32[]{:T(128)}, s32[]{:T(128)}) %tuple.551), condition=%wide.region_13.15_spmd.clone.clone, body=%wide.region_12.14_spmd.clone.clone.sunk | while | flops 3955 | bytes 14736 | solution.py:69
  697.1 34.1 %while.142 = (s32[]{:T(128)}, f32[16,16]{1,0:T(8,128)S(1)}, f32[16,16]{1,0:T(8,128)}, f32[16,16]{1,0:T(8,128)S(1)}, s32[]{:T(128)}, /*index=5*/s32[]{:T(128)}, s32[]{:T(128)}) while((s32[]{:T(128)}, f32[16,16]{1,0:T(8,128)S(1)}, f32[16,16]{1,0:T(8,128)}, f32[16,16]{1,0:T(8,128)S(1)}, s32[]{:T(128)}, ...), condition=%wide.region_15.17_spmd.clone.clone, body=%wide.region_14.16_spmd.clone.clone.sunk | while | flops 3924 | bytes 13155 | solution.py:87
  734.2 57.9 %psum.52 = f32[32,16]{1,0:T(8,128)S(1)} all-reduce(f32[32,16]{1,0:T(8,128)S(1)} %convolution_bitcast_fusion.15), channel_id=1, replica_groups=mesh['groups'=2,'slab'=16] {'slab'}, use_global_device_ids=true, to_apply=%region_16.18 | all-reduce | flops 512 | bytes 4096 | tf_op jit(solution)/shard_map/psum | solution.py:146
  803.9 30.0 %psum.53 = f32[16,16]{1,0:T(8,128)S(1)} all-reduce(f32[16,16]{1,0:T(8,128)S(1)} %convolution_bitcast_fusion.17), channel_id=1, replica_groups=mesh['groups'=2,'slab'=16] {'slab'}, use_global_device_ids=true, to_apply=%region_17.19 | all-reduce | flops 256 | bytes 2048 | tf_op jit(solution)/shard_map/psum | solution.py:149
  834.0 24.4 %while.143 = (s32[]{:T(128)}, f32[16,16]{1,0:T(8,128)S(1)}, f32[16,16]{0,1:T(8,128)S(1)}, s32[]{:T(128)}, s32[]{:T(128)}) while((s32[]{:T(128)}, f32[16,16]{1,0:T(8,128)S(1)}, f32[16,16]{0,1:T(8,128)S(1)}, s32[]{:T(128)}, s32[]{:T(128)}) %tuple.550), condition=%wide.region_19.21_spmd.clone.clone, body=%wide.region_18.20_spmd.clone.clone.sunk | while | flops 3955 | bytes 14736 | solution.py:69
  858.4 34.1 %while.144 = (s32[]{:T(128)}, f32[16,16]{1,0:T(8,128)S(1)}, f32[16,16]{1,0:T(8,128)}, f32[16,16]{1,0:T(8,128)S(1)}, s32[]{:T(128)}, /*index=5*/s32[]{:T(128)}, s32[]{:T(128)}) while((s32[]{:T(128)}, f32[16,16]{1,0:T(8,128)S(1)}, f32[16,16]{1,0:T(8,128)}, f32[16,16]{1,0:T(8,128)S(1)}, s32[]{:T(128)}, ...), condition=%wide.region_21.23_spmd.clone.clone, body=%wide.region_20.22_spmd.clone.clone.sunk | while | flops 3924 | bytes 13155 | solution.py:87
  896.0 57.6 %psum.54 = f32[48,16]{1,0:T(8,128)S(1)} all-reduce(f32[48,16]{1,0:T(8,128)S(1)} %fusion.90), channel_id=1, replica_groups=mesh['groups'=2,'slab'=16] {'slab'}, use_global_device_ids=true, to_apply=%region_22.24 | all-reduce | flops 768 | bytes 6144 | tf_op jit(solution)/shard_map/psum | solution.py:146
  962.0 30.0 %psum.55 = f32[16,16]{1,0:T(8,128)S(1)} all-reduce(f32[16,16]{1,0:T(8,128)S(1)} %convolution_bitcast_fusion.16), channel_id=1, replica_groups=mesh['groups'=2,'slab'=16] {'slab'}, use_global_device_ids=true, to_apply=%region_23.25 | all-reduce | flops 256 | bytes 2048 | tf_op jit(solution)/shard_map/psum | solution.py:149
  992.1 24.4 %while.145 = (s32[]{:T(128)}, f32[16,16]{1,0:T(8,128)S(1)}, f32[16,16]{0,1:T(8,128)S(1)}, s32[]{:T(128)}, s32[]{:T(128)}) while((s32[]{:T(128)}, f32[16,16]{1,0:T(8,128)S(1)}, f32[16,16]{0,1:T(8,128)S(1)}, s32[]{:T(128)}, s32[]{:T(128)}) %tuple.549), condition=%wide.region_25.27_spmd.clone.clone, body=%wide.region_24.26_spmd.clone.clone.sunk | while | flops 3955 | bytes 14736 | solution.py:69
  1016.6 34.1 %while.146 = (s32[]{:T(128)}, f32[16,16]{1,0:T(8,128)S(1)}, f32[16,16]{1,0:T(8,128)}, f32[16,16]{1,0:T(8,128)S(1)}, s32[]{:T(128)}, /*index=5*/s32[]{:T(128)}, s32[]{:T(128)}) while((s32[]{:T(128)}, f32[16,16]{1,0:T(8,128)S(1)}, f32[16,16]{1,0:T(8,128)}, f32[16,16]{1,0:T(8,128)S(1)}, s32[]{:T(128)}, ...), condition=%wide.region_27.29_spmd.clone.clone, body=%wide.region_26.28_spmd.clone.clone.sunk | while | flops 3924 | bytes 13155 | solution.py:87
  (1295 shorter events, 438.7 us)
Async XLA Ops:
  8.1 33.1 %all-to-all-start.1 = ((f32[16,64,1]{1,2,0:T(1,128)}), f32[16,64,1]{1,2,0:T(1,128)S(1)}, u32[]{:S(2)}, u32[]{:S(2)}) async-start(f32[16,64,1]{1,2,0:T(1,128)} %bitcast.16), calls=%async_computation.1 | async-start | bytes 16384 | tf_op jit(solution)/shard_map/all_to_all | solution.py:115
  41.8 38.2 %all-to-all-start = ((f32[16,64,320]{2,1,0:T(8,128)}), f32[16,64,320]{2,1,0:T(8,128)S(1)}, u32[]{:S(2)}, u32[]{:S(2)}) async-start(f32[16,64,320]{2,1,0:T(8,128)} %bitcast.14), calls=%async_computation | async-start | bytes 3145728 | tf_op jit(solution)/shard_map/all_to_all | solution.py:114
  51.6 223.7 %copy-start.129 = (f32[1,1,2048]{2,1,0:T(1,128)}, f32[1,1,2048]{2,1,0:T(1,128)S(1)}, u32[]{:S(2)}) copy-start(f32[1,1,2048]{2,1,0:T(1,128)S(1)} %get-tuple-element.1472) | copy-start | bytes 24580
  51.8 224.3 %copy-start.121 = (f32[1,1,2048]{2,1,0:T(1,128)}, f32[1,1,2048]{2,1,0:T(1,128)S(1)}, u32[]{:S(2)}) copy-start(f32[1,1,2048]{2,1,0:T(1,128)S(1)} %get-tuple-element.1462) | copy-start | bytes 24580
  51.8 224.3 %copy-start.123 = (f32[1,1,2048]{2,1,0:T(1,128)}, f32[1,1,2048]{2,1,0:T(1,128)S(1)}, u32[]{:S(2)}) copy-start(f32[1,1,2048]{2,1,0:T(1,128)S(1)} %get-tuple-element.1463) | copy-start | bytes 24580
  51.8 224.3 %copy-start.125 = (f32[1,1,2048]{2,1,0:T(1,128)}, f32[1,1,2048]{2,1,0:T(1,128)S(1)}, u32[]{:S(2)}) copy-start(f32[1,1,2048]{2,1,0:T(1,128)S(1)} %get-tuple-element.1464) | copy-start | bytes 24580
  51.8 224.3 %copy-start.127 = (f32[1,1,2048]{2,1,0:T(1,128)}, f32[1,1,2048]{2,1,0:T(1,128)S(1)}, u32[]{:S(2)}) copy-start(f32[1,1,2048]{2,1,0:T(1,128)S(1)} %get-tuple-element.1465) | copy-start | bytes 24580
  51.8 224.5 %copy-start.111 = (f32[1,1,2048]{2,1,0:T(1,128)}, f32[1,1,2048]{2,1,0:T(1,128)S(1)}, u32[]{:S(2)}) copy-start(f32[1,1,2048]{2,1,0:T(1,128)S(1)} %get-tuple-element.1457) | copy-start | bytes 24580
  51.8 224.5 %copy-start.113 = (f32[1,1,2048]{2,1,0:T(1,128)}, f32[1,1,2048]{2,1,0:T(1,128)S(1)}, u32[]{:S(2)}) copy-start(f32[1,1,2048]{2,1,0:T(1,128)S(1)} %get-tuple-element.1458) | copy-start | bytes 24580
  51.8 224.5 %copy-start.115 = (f32[1,1,2048]{2,1,0:T(1,128)}, f32[1,1,2048]{2,1,0:T(1,128)S(1)}, u32[]{:S(2)}) copy-start(f32[1,1,2048]{2,1,0:T(1,128)S(1)} %get-tuple-element.1459) | copy-start | bytes 24580
  51.8 224.5 %copy-start.117 = (f32[1,1,2048]{2,1,0:T(1,128)}, f32[1,1,2048]{2,1,0:T(1,128)S(1)}, u32[]{:S(2)}) copy-start(f32[1,1,2048]{2,1,0:T(1,128)S(1)} %get-tuple-element.1460) | copy-start | bytes 24580
  51.8 224.5 %copy-start.119 = (f32[1,1,2048]{2,1,0:T(1,128)}, f32[1,1,2048]{2,1,0:T(1,128)S(1)}, u32[]{:S(2)}) copy-start(f32[1,1,2048]{2,1,0:T(1,128)S(1)} %get-tuple-element.1461) | copy-start | bytes 24580
  51.9 224.7 %copy-start.101 = (f32[1,1,2048]{2,1,0:T(1,128)}, f32[1,1,2048]{2,1,0:T(1,128)S(1)}, u32[]{:S(2)}) copy-start(f32[1,1,2048]{2,1,0:T(1,128)S(1)} %get-tuple-element.1452) | copy-start | bytes 24580
  51.9 224.7 %copy-start.103 = (f32[1,1,2048]{2,1,0:T(1,128)}, f32[1,1,2048]{2,1,0:T(1,128)S(1)}, u32[]{:S(2)}) copy-start(f32[1,1,2048]{2,1,0:T(1,128)S(1)} %get-tuple-element.1453) | copy-start | bytes 24580
  51.9 224.7 %copy-start.105 = (f32[1,1,2048]{2,1,0:T(1,128)}, f32[1,1,2048]{2,1,0:T(1,128)S(1)}, u32[]{:S(2)}) copy-start(f32[1,1,2048]{2,1,0:T(1,128)S(1)} %get-tuple-element.1454) | copy-start | bytes 24580
  51.9 224.7 %copy-start.107 = (f32[1,1,2048]{2,1,0:T(1,128)}, f32[1,1,2048]{2,1,0:T(1,128)S(1)}, u32[]{:S(2)}) copy-start(f32[1,1,2048]{2,1,0:T(1,128)S(1)} %get-tuple-element.1455) | copy-start | bytes 24580
  51.9 224.7 %copy-start.109 = (f32[1,1,2048]{2,1,0:T(1,128)}, f32[1,1,2048]{2,1,0:T(1,128)S(1)}, u32[]{:S(2)}) copy-start(f32[1,1,2048]{2,1,0:T(1,128)S(1)} %get-tuple-element.1456) | copy-start | bytes 24580
  51.9 225.0 %copy-start.91 = (f32[1,1,2048]{2,1,0:T(1,128)}, f32[1,1,2048]{2,1,0:T(1,128)S(1)}, u32[]{:S(2)}) copy-start(f32[1,1,2048]{2,1,0:T(1,128)S(1)} %get-tuple-element.1447) | copy-start | bytes 24580
  51.9 225.0 %copy-start.93 = (f32[1,1,2048]{2,1,0:T(1,128)}, f32[1,1,2048]{2,1,0:T(1,128)S(1)}, u32[]{:S(2)}) copy-start(f32[1,1,2048]{2,1,0:T(1,128)S(1)} %get-tuple-element.1448) | copy-start | bytes 24580
  51.9 225.0 %copy-start.95 = (f32[1,1,2048]{2,1,0:T(1,128)}, f32[1,1,2048]{2,1,0:T(1,128)S(1)}, u32[]{:S(2)}) copy-start(f32[1,1,2048]{2,1,0:T(1,128)S(1)} %get-tuple-element.1449) | copy-start | bytes 24580
  51.9 225.0 %copy-start.97 = (f32[1,1,2048]{2,1,0:T(1,128)}, f32[1,1,2048]{2,1,0:T(1,128)S(1)}, u32[]{:S(2)}) copy-start(f32[1,1,2048]{2,1,0:T(1,128)S(1)} %get-tuple-element.1450) | copy-start | bytes 24580
  51.9 225.0 %copy-start.99 = (f32[1,1,2048]{2,1,0:T(1,128)}, f32[1,1,2048]{2,1,0:T(1,128)S(1)}, u32[]{:S(2)}) copy-start(f32[1,1,2048]{2,1,0:T(1,128)S(1)} %get-tuple-element.1451) | copy-start | bytes 24580
  52.1 225.5 %copy-start.83 = (f32[1,1,2048]{2,1,0:T(1,128)}, f32[1,1,2048]{2,1,0:T(1,128)S(1)}, u32[]{:S(2)}) copy-start(f32[1,1,2048]{2,1,0:T(1,128)S(1)} %get-tuple-element.1437) | copy-start | bytes 24580
  52.1 225.5 %copy-start.85 = (f32[1,1,2048]{2,1,0:T(1,128)}, f32[1,1,2048]{2,1,0:T(1,128)S(1)}, u32[]{:S(2)}) copy-start(f32[1,1,2048]{2,1,0:T(1,128)S(1)} %get-tuple-element.1438) | copy-start | bytes 24580
  52.1 225.5 %copy-start.87 = (f32[1,1,2048]{2,1,0:T(1,128)}, f32[1,1,2048]{2,1,0:T(1,128)S(1)}, u32[]{:S(2)}) copy-start(f32[1,1,2048]{2,1,0:T(1,128)S(1)} %get-tuple-element.1439) | copy-start | bytes 24580
  52.1 225.5 %copy-start.89 = (f32[1,1,2048]{2,1,0:T(1,128)}, f32[1,1,2048]{2,1,0:T(1,128)S(1)}, u32[]{:S(2)}) copy-start(f32[1,1,2048]{2,1,0:T(1,128)S(1)} %get-tuple-element.1440) | copy-start | bytes 24580
  52.1 225.8 %copy-start.79 = (f32[1,1,2048]{2,1,0:T(1,128)}, f32[1,1,2048]{2,1,0:T(1,128)S(1)}, u32[]{:S(2)}) copy-start(f32[1,1,2048]{2,1,0:T(1,128)S(1)} %get-tuple-element.1435) | copy-start | bytes 24580
  52.1 225.8 %copy-start.81 = (f32[1,1,2048]{2,1,0:T(1,128)}, f32[1,1,2048]{2,1,0:T(1,128)S(1)}, u32[]{:S(2)}) copy-start(f32[1,1,2048]{2,1,0:T(1,128)S(1)} %get-tuple-element.1436) | copy-start | bytes 24580
  88.5 5.1 collective-permute-start
  91.2 5.0 collective-permute-start.1
  291.8 10.5 collective-permute-start.2
  299.1 3.5 collective-permute-start.3
  (193 other events, 4023.8 us)
where the time goes:
time: 1070 us; the launch traced here: 1050 us
  local copies, waits for them, and re-layouts  451 us (42%)
  blocking collectives  273 us (26%)
  matrix products  127 us (12%)
  other arithmetic  98.8 us (9%)
  loops' own time  45.6 us (4%)
  waiting for transfers between devices  30 us (3%)
  starting transfers between devices  26.2 us (2%)
    gather x24, local copies, waits for them, and re-layouts, local(): gathered = jnp.take(padded, local_ids[slot_index], axis=2)  310 us
    psum x3, blocking collectives, local(): projection = lax.psum(gram_matrix(previous, panel_cols), 'slab')  146 us
    psum x4, blocking collectives, local(): lax.psum(gram_matrix(panel_cols, panel_cols), 'slab')  128 us
    dot_general x64, matrix products, row_step(): jnp.dot(earlier, inverse, precision=lax.Precision.HIGHEST)  93.2 us
    another operation x4, loops' own time, cholesky_upper(): lax.fori_loop(0, order, column_step, jnp.zeros((order, order), jnp.float32))  45.1 us
    dynamic_slice x64, local copies, waits for them, and re-layouts, column_step(): lax.dynamic_index_in_dim(reduced, column_at, 0, keepdims=False)  38 us
    dynamic_slice x64, local copies, waits for them, and re-layouts, row_step(): pivot = lax.dynamic_index_in_dim(lower_row, row_at, 0, keepdims=False)  37.7 us
    unnamed x68, other arithmetic  29.4 us
  transfers between devices with their start and end apart: 6, of which 3 were waited for; matrix products, arithmetic and copies ran while one was open for 3% of the time, Pallas kernels for 0%

commit v1 on v0

v1 whole, which is shorter than its diff:
```python
import functools
import math

import jax
import jax.numpy as jnp
from jax import lax
from jax.experimental import pallas as pl
from jax.experimental.pallas import tpu as pltpu
from jax.sharding import PartitionSpec as P

VARS = 5
NBR = 6
BY_LANES = 2
F32, BF16, I32 = jnp.float32, jnp.bfloat16, jnp.int32
VMEM = pl.BlockSpec(memory_space=pltpu.VMEM)


def round_up(value, unit):
    return -(-value // unit) * unit


def split2(x):
    high = x.astype(BF16)
    return high, (x - high.astype(F32)).astype(BF16)


def dot(a, b):
    return jnp.dot(a, b, preferred_element_type=F32)


def call(body, out_shape, *args, name, scratch=(), limit=40, flops=0, **kw):
    return pl.pallas_call(
        body,
        out_shape=out_shape,
        in_specs=kw.pop("in_specs", [VMEM] * len(args)),
        out_specs=kw.pop("out_specs", jax.tree.map(lambda _: VMEM, out_shape)),
        scratch_shapes=list(scratch),
        name=name,
        compiler_params=pltpu.CompilerParams(vmem_limit_bytes=limit << 20),
        **kw,
    )(*args)


def pack_body(cap, groups, rows, shapes_ref, weights_ref, dev_ref, cell_ref, out_ref, rows_ref, lhs_ref):
    nodes, width = shapes_ref.shape
    devices = out_ref.shape[0] // rows
    rows16 = lhs_ref.shape[1] // 3
    used = width + weights_ref.shape[1]
    rows_ref[used - used % 8 :, :] = jnp.zeros((rows_ref.shape[0] - used + used % 8, nodes), F32)
    rows_ref[:width, :] = shapes_ref[...].T
    rows_ref[width:used, :] = weights_ref[...].T
    rows_ref[used : used + 1, :] = (cell_ref[...] + 1).astype(F32)
    for g in range(groups):
        x = rows_ref[g * rows : g * rows + rows16, :]
        high = x.astype(BF16)
        rest = x - high.astype(F32)
        mid = rest.astype(BF16)
        lhs_ref[g, :rows16, :] = high
        lhs_ref[g, rows16 : 2 * rows16, :] = mid
        lhs_ref[g, 2 * rows16 :, :] = (rest - mid.astype(F32)).astype(BF16)
    dest = dev_ref[...]
    named = jnp.where(dest == lax.broadcasted_iota(I32, (nodes, devices), 1), 1.0, 0.0)
    earlier = jnp.where(
        lax.broadcasted_iota(I32, (nodes, nodes), 0) > lax.broadcasted_iota(I32, (nodes, nodes), 1), 1.0, 0.0
    )
    before = dot(earlier.astype(BF16), named.astype(BF16))
    rank = jnp.sum(named * before, axis=1, keepdims=True).astype(I32)
    place = jnp.broadcast_to(dest * 128 + rank, (nodes, 128))
    lane = lax.broadcasted_iota(I32, (nodes, 128), 1)

    def pair(step, _):
        total = jnp.zeros((3 * rows16, 256), F32)
        for g in range(groups):
            hot = [
                jnp.where(place + g * cap == lane + (step * 2 + h) * 128, 1.0, 0.0).astype(BF16) for h in range(2)
            ]
            total = total + dot(lhs_ref[g], jnp.concatenate(hot, axis=1))
        total = total[:rows16] + total[rows16 : 2 * rows16] + total[2 * rows16 :]
        for h in range(2):
            at = pl.multiple_of((step * 2 + h) * rows, 8)
            out_ref[pl.ds(at, rows), :] = total[:rows, h * 128 : (h + 1) * 128]
        return 0

    lax.fori_loop(0, devices // 2, pair, 0)


def prepare_body(rim, near_ref, filled_ref, coupling_ref, inv_ref, blocks_ref, place_ref):
    cells = near_ref.shape[1]
    for j in range(NBR):
        filled = filled_ref[j : j + 1, :] != 0
        for v in range(VARS):
            total = inv_ref[v, 0:1, :] * coupling_ref[j, 0]
            for w in range(1, VARS):
                total = total + inv_ref[v, w : w + 1, :] * coupling_ref[j, w]
            blocks_ref[(j * VARS + v) * 8 : (j * VARS + v) * 8 + VARS, :] = jnp.where(filled, total, 0.0)
        base = lax.broadcasted_iota(I32, (1, cells), 1) // 256 * 256
        place_ref[j : j + 1, :] = jnp.where(filled, near_ref[j : j + 1, :] + rim - base, rim)


def forcing_body(cap, groups, rows, modes, arrived_ref, inv_ref, out_ref, table_ref, lhs_ref, tag_ref):
    devices = arrived_ref.shape[0] // rows
    slots = devices * cap
    cells = out_ref.shape[2]
    lane_group = lax.broadcasted_iota(I32, (rows, 128), 1) // cap
    for p in range(devices // groups):
        chunks = [arrived_ref[(p * groups + b) * rows : (p * groups + b + 1) * rows, :] for b in range(groups)]
        for g in range(groups):
            merged = chunks[g]
            for b in range(groups):
                if b != g:
                    turned = pltpu.roll(chunks[b], (b - g) * cap % 128, 1)
                    merged = jnp.where(lane_group == b, turned, merged)
            table_ref[g * rows : (g + 1) * rows, p * 128 : (p + 1) * 128] = merged
    at = 3 * modes
    tag_row = at + 3 * VARS
    tags = table_ref[tag_row // 8 * 8 : tag_row // 8 * 8 + 8, :].T
    tag_ref[...] = jnp.broadcast_to(tags[:, tag_row % 8 : tag_row % 8 + 1], (slots, 128))
    for v in range(VARS):
        load = table_ref[at + 3 * v : at + 3 * v + 1, :] * table_ref[:modes, :]
        for k in range(1, 3):
            load = load + table_ref[at + 3 * v + k : at + 3 * v + k + 1, :] * table_ref[k * modes : (k + 1) * modes, :]
        high, low = split2(load)
        lhs_ref[v * 2 * modes : v * 2 * modes + modes, :] = high
        lhs_ref[v * 2 * modes + modes : (v + 1) * 2 * modes, :] = low
    lane = lax.broadcasted_iota(I32, (slots, 128), 1) + 1

    def tile(t, _):
        lo = pl.multiple_of(t * 256, 256)
        hot = [jnp.where(tag_ref[...] == (lane + (lo + h * 128)).astype(F32), 1.0, 0.0).astype(BF16) for h in range(2)]
        both = dot(lhs_ref[...], jnp.concatenate(hot, axis=1))
        forcing = [both[u * 2 * modes : u * 2 * modes + modes] + both[u * 2 * modes + modes : (u + 1) * 2 * modes] for u in range(VARS)]
        for v in range(VARS):
            total = inv_ref[v, 0:1, pl.ds(lo, 256)] * forcing[0]
            for u in range(1, VARS):
                total = total + inv_ref[v, u : u + 1, pl.ds(lo, 256)] * forcing[u]
            out_ref[v, :, pl.ds(lo, 256)] = total
        return 0

    lax.fori_loop(0, cells // 256, tile, 0)


def sweep_body(last, x_ref, before_ref, after_ref, start_ref, place_ref, blocks_ref, *refs):
    if last:
        out_ref, gram_ref, ext_ref, two_ref, sum_ref = refs
    else:
        out_ref, ext_ref, two_ref = refs
    modes, cells = x_ref.shape[1:]
    rim = before_ref.shape[2]
    by_matmul = NBR - BY_LANES

    def put(x, u, at):
        ext_ref[u, :, pl.ds(at, 256)] = x
        high, low = split2(x)
        two_ref[u * 2 * modes : u * 2 * modes + modes, pl.ds(at, 256)] = high
        two_ref[u * 2 * modes + modes : (u + 1) * 2 * modes, pl.ds(at, 256)] = low

    for u in range(VARS):
        put(before_ref[u], u, 0)
        put(after_ref[u], u, cells + rim)

    def widen(t, _):
        lo = pl.multiple_of(t * 256, 256)
        for u in range(VARS):
            put(x_ref[u, :, pl.ds(lo, 256)], u, pl.multiple_of(lo + rim, 256))
        return 0

    lax.fori_loop(0, cells // 256, widen, 0)
    if last:
        sum_ref[...] = jnp.zeros_like(sum_ref)
    window = lax.broadcasted_iota(I32, (256 + 2 * rim, 256), 0)

    def tile(t, _):
        lo = pl.multiple_of(t * 256, 256)
        fetched = []
        for j in range(by_matmul):
            hot = jnp.where(window == place_ref[j : j + 1, pl.ds(lo, 256)], 1.0, 0.0).astype(BF16)
            fetched.append(dot(two_ref[:, pl.ds(lo, 256 + 2 * rim)], hot))
        results = [[None] * 2 for _ in range(modes // 8)]
        for m in range(0, modes, 8):
            for h in range(2):
                at = pl.multiple_of(lo + h * 128, 128)
                acc = [start_ref[v, m : m + 8, pl.ds(at, 128)] for v in range(VARS)]

                def subtract(j, u, value):
                    for v in range(VARS):
                        row = (j * VARS + v) * 8 + u
                        acc[v] = acc[v] - blocks_ref[row : row + 1, pl.ds(at, 128)] * value

                around = (128 + 2 * rim) // 128
                source = [[ext_ref[u, m : m + 8, pl.ds(at + s * 128, 128)] for s in range(around)] for u in range(VARS)]
                for j in range(by_matmul, NBR):
                    place = jnp.broadcast_to(place_ref[j : j + 1, pl.ds(at, 128)] - h * 128, (8, 128))
                    lane, block = place & 127, place >> 7
                    for u in range(VARS):
                        value = jnp.take_along_axis(source[u][0], lane, axis=1, mode="promise_in_bounds")
                        for s in range(1, around):
                            there = jnp.take_along_axis(source[u][s], lane, axis=1, mode="promise_in_bounds")
                            value = jnp.where(block == s, there, value)
                        subtract(j, u, value)
                for j in range(by_matmul):
                    for u in range(VARS):
                        r = u * 2 * modes + m
                        both = fetched[j][:, h * 128 : (h + 1) * 128]
                        subtract(j, u, both[r : r + 8] + both[r + modes : r + modes + 8])
                for v in range(VARS):
                    ext_out(v, m, h, at, acc[v])
        if last:
            for v in range(VARS):
                high, low = split2(sum_ref[v, :, :256])
                pair = jnp.concatenate([high, low], axis=0)
                out_ref[v, :, pl.ds(lo, 256)] = pair
                gram_add(pair)
        return 0

    def ext_out(v, m, h, at, value):
        if last:
            sum_ref[v, m : m + 8, h * 128 : (h + 1) * 128] = value
        else:
            out_ref[v, m : m + 8, pl.ds(at, 128)] = value

    def gram_add(pair):
        sum_ref[0, :, 256:384] += lax.dot_general(
            pair[:modes], pair, (((1,), (1,)), ((), ())), preferred_element_type=F32
        )
        sum_ref[1, :, 256:384] += lax.dot_general(
            pair[modes:], pair, (((1,), (1,)), ((), ())), preferred_element_type=F32
        )

    lax.fori_loop(0, cells // 256, tile, 0)
    if last:
        gram = sum_ref[0, :, 256:384] + sum_ref[1, :, 256:384]
        gram = gram + pltpu.roll(gram, modes, 1)
        gram_ref[...] = jnp.where(lax.broadcasted_iota(I32, gram.shape, 1) < modes, gram, 0.0)


def basis_body(norm, gram_ref, field_ref, out_ref, factor_ref, lhs_ref):
    modes = factor_ref.shape[0]

    @pl.when(pl.program_id(0) == 0)
    def _():
        row = lax.broadcasted_iota(I32, (modes, 2 * modes), 0)
        lane = lax.broadcasted_iota(I32, (modes, 2 * modes), 1)
        a = jnp.where(lane == row + modes, 1.0, gram_ref[...])
        for k in range(modes - 1):
            pivot_row = a[k : k + 1, :]
            scale = a[:, k : k + 1] / a[k : k + 1, k : k + 1]
            a = a - jnp.where(row > k, scale, 0.0) * pivot_row
        diagonal = jnp.sum(jnp.where(lane == row, a, 0.0), axis=1, keepdims=True)
        a = a / jnp.sqrt(diagonal)
        factor_ref[...] = jnp.where(lane >= row, a / norm, 0.0)[:, :modes]
        inverse = a * norm
        inverse = jnp.where(lane < modes, pltpu.roll(inverse, modes, 1), inverse)
        high, low = split2(inverse)
        lhs_ref[:modes, :] = high
        lhs_ref[modes:, :] = low

    both = dot(lhs_ref[...], field_ref[0])
    out_ref[0] = both[:modes] + both[modes:]


def local(mode_shapes, wall_coupling, owner_dev, owner_cell, neighbours, coupling_blocks, inv_blocks):
    devices = lax.axis_size("slab")
    cells = inv_blocks.shape[2]
    nodes, modes = mode_shapes.shape[0], mode_shapes.shape[1] // 3
    cap = max(2, 2 * nodes // devices)
    rim = cells // 8
    groups = 128 // cap
    columns = 3 * modes + 3 * VARS + 1
    rows = round_up(-(-columns // groups), 8)
    rows16 = round_up(rows, 16)
    packed = call(
        functools.partial(pack_body, cap, groups, rows),
        jax.ShapeDtypeStruct((devices * rows, 128), F32),
        mode_shapes, wall_coupling, owner_dev, owner_cell[None, :],
        scratch=[pltpu.VMEM(((groups - 1) * rows + rows16, nodes), F32), pltpu.VMEM((groups, 3 * rows16, nodes), BF16)],
        name="pack",
    )
    arrived = lax.all_to_all(packed, "slab", split_axis=0, concat_axis=0, tiled=True)
    near = neighbours - lax.axis_index("slab") * cells
    blocks, place = call(
        functools.partial(prepare_body, rim),
        (jax.ShapeDtypeStruct((NBR * VARS * 8, cells), F32), jax.ShapeDtypeStruct((8, cells), I32)),
        near, (neighbours >= 0).astype(I32), coupling_blocks, inv_blocks,
        name="prepare",
    )
    start = call(
        functools.partial(forcing_body, cap, groups, rows, modes),
        jax.ShapeDtypeStruct((VARS, modes, cells), F32),
        arrived, inv_blocks,
        scratch=[
            pltpu.VMEM((groups * rows, devices * cap), F32),
            pltpu.VMEM((VARS * 2 * modes, devices * cap), BF16),
            pltpu.VMEM((devices * cap, 128), F32),
        ],
        name="forcing",
    )
    up = [(i, i + 1) for i in range(devices - 1)]
    down = [(j, i) for i, j in up]
    x = start
    for last in (False, True):
        before = lax.ppermute(x[:, :, cells - rim :], "slab", up)
        after = lax.ppermute(x[:, :, :rim], "slab", down)
        shapes = jax.ShapeDtypeStruct((VARS, modes, cells), F32)
        scratch = [pltpu.VMEM((VARS, modes, cells + 2 * rim), F32), pltpu.VMEM((VARS * 2 * modes, cells + 2 * rim), BF16)]
        if last:
            shapes = (jax.ShapeDtypeStruct((VARS, 2 * modes, cells), BF16), jax.ShapeDtypeStruct((modes, 2 * modes), F32))
            scratch.append(pltpu.VMEM((VARS, modes, 384), F32))
        x = call(
            functools.partial(sweep_body, last), shapes, x, before, after, start, place, blocks,
            scratch=scratch, name="sweep_last" if last else "sweep",
        )
    field, gram = x
    reach = 1
    while reach < devices:
        gram = gram + lax.ppermute(gram, "slab", [(i, i ^ reach) for i in range(devices)])
        reach *= 2
    norm = math.sqrt(VARS * cells * devices)
    return call(
        functools.partial(basis_body, norm),
        (jax.ShapeDtypeStruct((VARS, modes, cells), F32), jax.ShapeDtypeStruct((modes, modes), F32)),
        gram, field,
        grid=(VARS,),
        in_specs=[
            pl.BlockSpec((modes, 2 * modes), lambda v: (0, 0)),
            pl.BlockSpec((1, 2 * modes, cells), lambda v: (v, 0, 0)),
        ],
        out_specs=(
            pl.BlockSpec((1, modes, cells), lambda v: (v, 0, 0)),
            pl.BlockSpec((modes, modes), lambda v: (0, 0)),
        ),
        scratch=[pltpu.VMEM((2 * modes, 2 * modes), BF16)],
        name="basis",
    )


def solution(mesh):
    in_specs = (
        P(("groups", "slab"), None),
        P(("groups", "slab"), None),
        P(("groups", "slab"), None),
        P(("groups", "slab")),
        P(None, ("groups", "slab")),
        P(None, None, None, ("groups", "slab")),
        P(None, None, ("groups", "slab")),
    )
    out_specs = (P(None, None, ("groups", "slab")), P("groups", None))
    return jax.shard_map(local, mesh=mesh, in_specs=in_specs, out_specs=out_specs, check_vma=False)
```

time: 1070 us -> 124 us (0.12); the launches traced: 1050 us -> 123 us
  local copies, waits for them, and re-layouts: 451 us -> 5.91 us
  blocking collectives: 273 us -> 0 us
  matrix products: 127 us -> 0 us
  other arithmetic: 98.8 us -> 0.04 us
  Pallas kernels: 0 us -> 53.5 us
  loops' own time: 45.6 us -> 0 us
    gather x24 -> x0, local copies, waits for them, and re-layouts: 310 us -> none  [local(): gathered = jnp.take(padded, local_ids[slot_index], axis=2)]
    psum x7 -> x0, blocking collectives: 273 us -> none  [the longest x3 146 us: local(): projection = lax.psum(gram_matrix(previous, panel_cols), 'slab')]
    dot_general x143 -> x0, matrix products: 127 us -> none  [the longest x64 93.2 us: row_step(): jnp.dot(earlier, inverse, precision=lax.Precision.HIGHEST)]
    dynamic_slice x128 -> x0, local copies, waits for them, and re-layouts: 75.7 us -> none  [the longest x64 38 us: column_step(): lax.dynamic_index_in_dim(reduced, column_at, 0, keepdims=False)]
    pallas_call x0 -> x6, Pallas kernels: none -> 53.5 us  [call(): pl.pallas_call(body, out_shape=out_shape, in_specs=kw.pop('in_specs', [VM...]
    another operation x8 -> x0, loops' own time: 45.6 us -> none  [the longest x4 45.1 us: cholesky_upper(): lax.fori_loop(0, order, column_step, jnp.zeros((order, order), jnp.float32))]
    unnamed x68 -> x0, other arithmetic: 29.4 us -> none
    select_n x206 -> x0, other arithmetic: 25.2 us -> none  [the longest x12 13.8 us: local(): gathered = jnp.take(padded, local_ids[slot_index], axis=2)]
  transfers between devices with their start and end apart: 6 -> 9, of which waited for: 3 -> 6; matrix products, arithmetic and copies ran while one was open for 3% -> 2% of each run, Pallas kernels for 0% -> 1%
where the time goes in v1:
time: 124 us; the launch traced here: 123 us
  Pallas kernels  53.5 us (43%)
  starting transfers between devices  36.8 us (30%)
  waiting for transfers between devices  26.2 us (21%)
  local copies, waits for them, and re-layouts  5.91 us (5%)
    pallas_call x6, Pallas kernels, call(): pl.pallas_call(body, out_shape=out_shape, in_specs=kw.pop('in_specs', [VM...  53.5 us
    all_to_all x1, waiting for transfers between devices, local(): lax.all_to_all(packed, 'slab', split_axis=0, concat_axis=0, tiled=True)  17.5 us
    ppermute x4, starting transfers between devices, local(): lax.ppermute(gram, 'slab', [(i, i ^ reach) for i in range(devices)])  14.1 us
    ppermute x2, starting transfers between devices, local(): before = lax.ppermute(x[:, :, cells - rim:], 'slab', up)  12.6 us
    all_to_all x1, starting transfers between devices, local(): lax.all_to_all(packed, 'slab', split_axis=0, concat_axis=0, tiled=True)  7.52 us
    ppermute x4, waiting for transfers between devices, local(): lax.ppermute(gram, 'slab', [(i, i ^ reach) for i in range(devices)])  7.42 us
    unnamed x10, local copies, waits for them, and re-layouts  5.79 us
    ppermute x2, starting transfers between devices, local(): after = lax.ppermute(x[:, :, :rim], 'slab', down)  2.58 us
  transfers between devices with their start and end apart: 9, of which 6 were waited for; matrix products, arithmetic and copies ran while one was open for 2% of the time, Pallas kernels for 1%

profile of v1, /device:TPU:0, one launch (start us, length us, event | category | flops | bytes accessed | tf_op | source)
XLA Modules:
  0.0 123.2 jit_solution(13281187741813195914)
XLA Ops:
  0.6 0.9 copy.10.weights_ref
  1.5 0.8 copy.11.dev_ref
  2.4 1.2 copy.9.shapes_ref
  3.6 0.0 copy-start.1
  3.6 0.7 copy-done.1
  4.2 4.5 %pack.1 = f32[1664,128]{1,0:T(8,128)} custom-call(f32[512,192]{1,0:T(8,128)S(1)} %copy.9.shapes_ref, f32[512,15]{1,0:T(8,128)S(1)} %copy.10.weights_ref, s32[512,1]{1,0:T(8,128)S(1)} %copy.11.dev_ref, s32[1,512]{1,0:T(1,128)S(1)} %bitcast.4), custom_call_target="tpu_custom_call" | custom-call | tf_op jit(solution)/shard_map/pack/pallas_call | solution.py:32
  8.7 7.5 %all-to-all-start = ((f32[16,104,128]{2,1,0:T(8,128)}), f32[16,104,128]{2,1,0:T(8,128)S(1)}, u32[]{:S(2)}, u32[]{:S(2)}) async-start(f32[16,104,128]{2,1,0:T(8,128)} %bitcast.1), calls=%async_computation | async-start | bytes 1703936 | tf_op jit(solution)/shard_map/all_to_all | solution.py:278
  16.2 2.2 %copy.12.coupling_ref = f32[6,5,5,2048]{3,2,1,0:T(8,128)S(1)} copy(f32[6,5,5,2048]{3,0,2,1:T(8,128)} %param.12) | data formatting | bytes 2457600 | tf_op args[5]
  18.5 17.5 %all-to-all-done = f32[16,104,128]{2,1,0:T(8,128)S(1)} async-done(((f32[16,104,128]{2,1,0:T(8,128)}), f32[16,104,128]{2,1,0:T(8,128)S(1)}, u32[]{:S(2)}, u32[]{:S(2)}) %all-to-all-start) | async-done | bytes 852000 | tf_op jit(solution)/shard_map/all_to_all | solution.py:278
  36.0 5.3 %forcing.1.x_ref.start_ref = f32[5,64,2048]{2,1,0:T(8,128)S(1)} custom-call(f32[1664,128]{1,0:T(8,128)S(1)} %bitcast.3, f32[5,5,2048]{2,1,0:T(8,128)S(1)} %copy-done), custom_call_target="tpu_custom_call" | custom-call | tf_op jit(solution)/shard_map/forcing/pallas_call | solution.py:32
  41.3 0.1 fusion.1
  41.4 1.3 %collective-permute-start.1 = (f32[5,64,256]{2,1,0:T(8,128)S(1)}, f32[5,64,256]{2,1,0:T(8,128)S(1)}, u32[]{:S(2)}, u32[]{:S(2)}) collective-permute-start(f32[5,64,256]{2,1,0:T(8,128)S(1)} %get-tuple-element.12), channel_id=1, source_target_pairs={{1,0},{2,1},{3,2},{4,3},{5,4},{6,5},{7,6},{8,7},{9,8},{10,9},{11,1... | collective-permute-start | bytes 983048 | tf_op jit(solution)/shard_map/ppermute | solution.py:302
  42.7 3.1 %collective-permute-start = (f32[5,64,256]{2,1,0:T(8,128)S(1)}, f32[5,64,256]{2,1,0:T(8,128)S(1)}, u32[]{:S(2)}, u32[]{:S(2)}) collective-permute-start(f32[5,64,256]{2,1,0:T(8,128)S(1)} %get-tuple-element.13), channel_id=1, source_target_pairs={{0,1},{1,2},{2,3},{3,4},{4,5},{5,6},{6,7},{7,8},{8,9},{9,10},{10,1... | collective-permute-start | bytes 983048 | tf_op jit(solution)/shard_map/ppermute | solution.py:301
  45.8 1.2 %prepare.1 = (f32[240,2048]{1,0:T(8,128)S(1)}, s32[8,2048]{1,0:T(8,128)S(1)}) custom-call(s32[6,2048]{1,0:T(8,128)S(1)} %broadcast_subtract_fusion.near_ref, s32[6,2048]{1,0:T(8,128)S(1)} %compare_convert_fusion.filled_ref, f32[6,5,5,2048]{3,2,1,0:T(8,128)S(1)} %copy.12.coupling_ref, f32[5,5,2048]{2,1,0:T(8,128)S(1)} %copy-done), custom_call_target="tpu_custom_call" | custom-call | tf_op jit(solution)/shard_map/prepare/pallas_call | solution.py:32
  47.0 0.0 collective-permute-done.1.after_ref
  47.0 0.0 collective-permute-done.before_ref
  47.0 15.0 %sweep.1.x_ref = f32[5,64,2048]{2,1,0:T(8,128)S(1)} custom-call(f32[5,64,2048]{2,1,0:T(8,128)S(1)} %forcing.1.x_ref.start_ref, f32[5,64,256]{2,1,0:T(8,128)S(1)} %collective-permute-done.before_ref, f32[5,64,256]{2,1,0:T(8,128)S(1)} %collective-permute-done.1.after_ref, f32[5,64,2048]{2,1,0:T(8,128)S(1)} %forcing.1.x_ref.start_ref, ...), custom_call_target="tpu_custom_call" | custom-call | tf_op jit(solution)/shard_map/sweep/pallas_call | solution.py:32
  62.0 0.1 fusion
  62.1 1.3 %collective-permute-start.3 = (f32[5,64,256]{2,1,0:T(8,128)S(1)}, f32[5,64,256]{2,1,0:T(8,128)S(1)}, u32[]{:S(2)}, u32[]{:S(2)}) collective-permute-start(f32[5,64,256]{2,1,0:T(8,128)S(1)} %get-tuple-element.10), channel_id=1, source_target_pairs={{1,0},{2,1},{3,2},{4,3},{5,4},{6,5},{7,6},{8,7},{9,8},{10,9},{11,1... | collective-permute-start | bytes 983048 | tf_op jit(solution)/shard_map/ppermute | solution.py:302
  63.4 9.6 %collective-permute-start.2 = (f32[5,64,256]{2,1,0:T(8,128)S(1)}, f32[5,64,256]{2,1,0:T(8,128)S(1)}, u32[]{:S(2)}, u32[]{:S(2)}) collective-permute-start(f32[5,64,256]{2,1,0:T(8,128)S(1)} %get-tuple-element.11), channel_id=1, source_target_pairs={{0,1},{1,2},{2,3},{3,4},{4,5},{5,6},{6,7},{7,8},{8,9},{9,10},{10,1... | collective-permute-start | bytes 983048 | tf_op jit(solution)/shard_map/ppermute | solution.py:301
  72.9 0.0 collective-permute-done.3.after_ref
  73.0 1.2 collective-permute-done.2.before_ref
  74.2 18.9 %sweep_last.1 = (bf16[5,128,2048]{2,1,0:T(8,128)(2,1)S(1)}, f32[64,128]{1,0:T(8,128)S(1)}) custom-call(f32[5,64,2048]{2,1,0:T(8,128)S(1)} %sweep.1.x_ref, f32[5,64,256]{2,1,0:T(8,128)S(1)} %collective-permute-done.2.before_ref, f32[5,64,256]{2,1,0:T(8,128)S(1)} %collective-permute-done.3.after_ref, f32[5,64,2048]{2,1,0:T(8,128)S(1)} %forcing.1.x_ref.start_ref, ...), custom_call_target="tpu_custom_call" | custom-call | tf_op jit(solution)/shard_map/sweep_last/pallas_call | solution.py:32
  93.0 6.3 %collective-permute-start.4 = (f32[64,128]{1,0:T(8,128)S(1)}, f32[64,128]{1,0:T(8,128)S(1)}, u32[]{:S(2)}, u32[]{:S(2)}) collective-permute-start(f32[64,128]{1,0:T(8,128)S(1)} %get-tuple-element.8), channel_id=1, source_target_pairs={{0,1},{1,0},{2,3},{3,2},{4,5},{5,4},{6,7},{7,6},{8,9},{9,8},{10,11... | collective-permute-start | bytes 98312 | tf_op jit(solution)/shard_map/ppermute | solution.py:315
  99.3 0.9 collective-permute-done.4
  100.2 2.7 %collective-permute-start.5 = (f32[64,128]{1,0:T(8,128)S(1)}, f32[64,128]{1,0:T(8,128)S(1)}, u32[]{:S(2)}, u32[]{:S(2)}) collective-permute-start(f32[64,128]{1,0:T(8,128)S(1)} %add.12), channel_id=1, source_target_pairs={{0,2},{1,3},{2,0},{3,1},{4,6},{5,7},{6,4},{7,5},{8,10},{9,11},{10,... | collective-permute-start | bytes 98312 | tf_op jit(solution)/shard_map/ppermute | solution.py:315
  102.9 1.9 %collective-permute-done.5 = f32[64,128]{1,0:T(8,128)S(1)} collective-permute-done((f32[64,128]{1,0:T(8,128)S(1)}, f32[64,128]{1,0:T(8,128)S(1)}, u32[]{:S(2)}, u32[]{:S(2)}) %collective-permute-start.5) | collective-permute-done | bytes 32800 | tf_op jit(solution)/shard_map/ppermute | solution.py:315
  104.8 3.0 %collective-permute-start.6 = (f32[64,128]{1,0:T(8,128)S(1)}, f32[64,128]{1,0:T(8,128)S(1)}, u32[]{:S(2)}, u32[]{:S(2)}) collective-permute-start(f32[64,128]{1,0:T(8,128)S(1)} %add.13), channel_id=1, source_target_pairs={{0,4},{1,5},{2,6},{3,7},{4,0},{5,1},{6,2},{7,3},{8,12},{9,13},{10,... | collective-permute-start | bytes 98312 | tf_op jit(solution)/shard_map/ppermute | solution.py:315
  107.8 1.9 %collective-permute-done.6 = f32[64,128]{1,0:T(8,128)S(1)} collective-permute-done((f32[64,128]{1,0:T(8,128)S(1)}, f32[64,128]{1,0:T(8,128)S(1)}, u32[]{:S(2)}, u32[]{:S(2)}) %collective-permute-start.6) | collective-permute-done | bytes 32800 | tf_op jit(solution)/shard_map/ppermute | solution.py:315
  109.7 2.0 %collective-permute-start.7 = (f32[64,128]{1,0:T(8,128)S(1)}, f32[64,128]{1,0:T(8,128)S(1)}, u32[]{:S(2)}, u32[]{:S(2)}) collective-permute-start(f32[64,128]{1,0:T(8,128)S(1)} %add.14), channel_id=1, source_target_pairs={{0,8},{1,9},{2,10},{3,11},{4,12},{5,13},{6,14},{7,15},{8,0},{9,1},... | collective-permute-start | bytes 98312 | tf_op jit(solution)/shard_map/ppermute | solution.py:315
  111.8 2.8 %collective-permute-done.7 = f32[64,128]{1,0:T(8,128)S(1)} collective-permute-done((f32[64,128]{1,0:T(8,128)S(1)}, f32[64,128]{1,0:T(8,128)S(1)}, u32[]{:S(2)}, u32[]{:S(2)}) %collective-permute-start.7) | collective-permute-done | bytes 32800 | tf_op jit(solution)/shard_map/ppermute | solution.py:315
  114.6 8.6 %basis.1 = (f32[5,64,2048]{2,1,0:T(8,128)}, f32[64,64]{1,0:T(8,128)}) custom-call(f32[64,128]{1,0:T(8,128)S(1)} %add.15.gram_ref, bf16[5,128,2048]{2,1,0:T(8,128)(2,1)S(1)} %get-tuple-element.9.field_ref), custom_call_target="tpu_custom_call" | custom-call | tf_op jit(solution)/shard_map/basis/pallas_call | solution.py:32
  (10 shorter events, 0.0 us)
Async XLA Ops:
  3.6 0.7 copy-start.1
  8.7 9.7 %copy-start.2 = (s32[6,2048]{1,0:T(8,128)S(1)}, s32[6,2048]{1,0:T(8,128)}, u32[]{:S(2)}) copy-start(s32[6,2048]{1,0:T(8,128)} %param.11) | copy-start | bytes 147460
  8.7 27.3 %copy-start = (f32[5,5,2048]{2,1,0:T(8,128)S(1)}, f32[5,5,2048]{2,1,0:T(8,128)}, u32[]{:S(2)}) copy-start(f32[5,5,2048]{2,1,0:T(8,128)} %inv_ref.3) | copy-start | bytes 614404
  8.7 27.3 %all-to-all-start = ((f32[16,104,128]{2,1,0:T(8,128)}), f32[16,104,128]{2,1,0:T(8,128)S(1)}, u32[]{:S(2)}, u32[]{:S(2)}) async-start(f32[16,104,128]{2,1,0:T(8,128)} %bitcast.1), calls=%async_computation | async-start | bytes 1703936 | tf_op jit(solution)/shard_map/all_to_all | solution.py:278
  41.4 5.6 %collective-permute-start.1 = (f32[5,64,256]{2,1,0:T(8,128)S(1)}, f32[5,64,256]{2,1,0:T(8,128)S(1)}, u32[]{:S(2)}, u32[]{:S(2)}) collective-permute-start(f32[5,64,256]{2,1,0:T(8,128)S(1)} %get-tuple-element.12), channel_id=1, source_target_pairs={{1,0},{2,1},{3,2},{4,3},{5,4},{6,5},{7,6},{8,7},{9,8},{10,9},{11,1... | collective-permute-start | bytes 983048 | tf_op jit(solution)/shard_map/ppermute | solution.py:302
  42.7 4.3 %collective-permute-start = (f32[5,64,256]{2,1,0:T(8,128)S(1)}, f32[5,64,256]{2,1,0:T(8,128)S(1)}, u32[]{:S(2)}, u32[]{:S(2)}) collective-permute-start(f32[5,64,256]{2,1,0:T(8,128)S(1)} %get-tuple-element.13), channel_id=1, source_target_pairs={{0,1},{1,2},{2,3},{3,4},{4,5},{5,6},{6,7},{7,8},{8,9},{9,10},{10,1... | collective-permute-start | bytes 983048 | tf_op jit(solution)/shard_map/ppermute | solution.py:301
  62.1 10.9 %collective-permute-start.3 = (f32[5,64,256]{2,1,0:T(8,128)S(1)}, f32[5,64,256]{2,1,0:T(8,128)S(1)}, u32[]{:S(2)}, u32[]{:S(2)}) collective-permute-start(f32[5,64,256]{2,1,0:T(8,128)S(1)} %get-tuple-element.10), channel_id=1, source_target_pairs={{1,0},{2,1},{3,2},{4,3},{5,4},{6,5},{7,6},{8,7},{9,8},{10,9},{11,1... | collective-permute-start | bytes 983048 | tf_op jit(solution)/shard_map/ppermute | solution.py:302
  63.4 10.8 %collective-permute-start.2 = (f32[5,64,256]{2,1,0:T(8,128)S(1)}, f32[5,64,256]{2,1,0:T(8,128)S(1)}, u32[]{:S(2)}, u32[]{:S(2)}) collective-permute-start(f32[5,64,256]{2,1,0:T(8,128)S(1)} %get-tuple-element.11), channel_id=1, source_target_pairs={{0,1},{1,2},{2,3},{3,4},{4,5},{5,6},{6,7},{7,8},{8,9},{9,10},{10,1... | collective-permute-start | bytes 983048 | tf_op jit(solution)/shard_map/ppermute | solution.py:301
  93.0 7.2 %collective-permute-start.4 = (f32[64,128]{1,0:T(8,128)S(1)}, f32[64,128]{1,0:T(8,128)S(1)}, u32[]{:S(2)}, u32[]{:S(2)}) collective-permute-start(f32[64,128]{1,0:T(8,128)S(1)} %get-tuple-element.8), channel_id=1, source_target_pairs={{0,1},{1,0},{2,3},{3,2},{4,5},{5,4},{6,7},{7,6},{8,9},{9,8},{10,11... | collective-permute-start | bytes 98312 | tf_op jit(solution)/shard_map/ppermute | solution.py:315
  100.2 4.6 %collective-permute-start.5 = (f32[64,128]{1,0:T(8,128)S(1)}, f32[64,128]{1,0:T(8,128)S(1)}, u32[]{:S(2)}, u32[]{:S(2)}) collective-permute-start(f32[64,128]{1,0:T(8,128)S(1)} %add.12), channel_id=1, source_target_pairs={{0,2},{1,3},{2,0},{3,1},{4,6},{5,7},{6,4},{7,5},{8,10},{9,11},{10,... | collective-permute-start | bytes 98312 | tf_op jit(solution)/shard_map/ppermute | solution.py:315
  104.8 4.9 %collective-permute-start.6 = (f32[64,128]{1,0:T(8,128)S(1)}, f32[64,128]{1,0:T(8,128)S(1)}, u32[]{:S(2)}, u32[]{:S(2)}) collective-permute-start(f32[64,128]{1,0:T(8,128)S(1)} %add.13), channel_id=1, source_target_pairs={{0,4},{1,5},{2,6},{3,7},{4,0},{5,1},{6,2},{7,3},{8,12},{9,13},{10,... | collective-permute-start | bytes 98312 | tf_op jit(solution)/shard_map/ppermute | solution.py:315
  109.7 4.8 %collective-permute-start.7 = (f32[64,128]{1,0:T(8,128)S(1)}, f32[64,128]{1,0:T(8,128)S(1)}, u32[]{:S(2)}, u32[]{:S(2)}) collective-permute-start(f32[64,128]{1,0:T(8,128)S(1)} %add.14), channel_id=1, source_target_pairs={{0,8},{1,9},{2,10},{3,11},{4,12},{5,13},{6,14},{7,15},{8,0},{9,1},... | collective-permute-start | bytes 98312 | tf_op jit(solution)/shard_map/ppermute | solution.py:315

commit v2 on v1

v2 whole, which is shorter than its diff:
```python
import functools
import math

import jax
import jax.numpy as jnp
from jax import lax
from jax.experimental import pallas as pl
from jax.experimental.pallas import tpu as pltpu
from jax.sharding import PartitionSpec as P

VARS = 5
NBR = 6
BY_LANES = 2
ROWS = 16
TOGETHER = 4
MANY = 4
STEP = 8
F32, BF16, I32 = jnp.float32, jnp.bfloat16, jnp.int32
VMEM = pl.BlockSpec(memory_space=pltpu.VMEM)


def round_up(value, unit):
    return -(-value // unit) * unit


def split2(x):
    high = x.astype(BF16)
    return high, (x - high.astype(F32)).astype(BF16)


def dot(a, b):
    return jnp.dot(a, b, preferred_element_type=F32)


def call(body, out_shape, *args, name, scratch=(), limit=40, flops=0, **kw):
    return pl.pallas_call(
        body,
        out_shape=out_shape,
        in_specs=kw.pop("in_specs", [VMEM] * len(args)),
        out_specs=kw.pop("out_specs", jax.tree.map(lambda _: VMEM, out_shape)),
        scratch_shapes=list(scratch),
        name=name,
        compiler_params=pltpu.CompilerParams(vmem_limit_bytes=limit << 20),
        **kw,
    )(*args)


def pack_body(cap, groups, rows, shapes_ref, weights_ref, dev_ref, cell_ref, out_ref, rows_ref, lhs_ref):
    width, nodes = shapes_ref.shape
    devices = out_ref.shape[0] // rows
    rows16 = lhs_ref.shape[1] // 3
    used = width + weights_ref.shape[0]
    rows_ref[used - used % 8 :, :] = jnp.zeros((rows_ref.shape[0] - used + used % 8, nodes), F32)
    rows_ref[:width, :] = shapes_ref[...]
    rows_ref[width:used, :] = weights_ref[...]
    rows_ref[used : used + 1, :] = (cell_ref[...] + 1).astype(F32)
    for g in range(groups):
        x = rows_ref[g * rows : g * rows + rows16, :]
        high = x.astype(BF16)
        rest = x - high.astype(F32)
        mid = rest.astype(BF16)
        lhs_ref[g, :rows16, :] = high
        lhs_ref[g, rows16 : 2 * rows16, :] = mid
        lhs_ref[g, 2 * rows16 :, :] = (rest - mid.astype(F32)).astype(BF16)
    dest = dev_ref[...]
    named = jnp.where(dest == lax.broadcasted_iota(I32, (devices, nodes), 0), 1.0, 0.0)
    earlier = jnp.where(
        lax.broadcasted_iota(I32, (nodes, nodes), 0) < lax.broadcasted_iota(I32, (nodes, nodes), 1), 1.0, 0.0
    )
    rank = jnp.sum(named * dot(named.astype(BF16), earlier.astype(BF16)), axis=0, keepdims=True).astype(I32)
    place = dest * 128 + rank
    slot = lax.broadcasted_iota(I32, (128 * MANY, nodes), 0)

    def several(step, _):
        total = jnp.zeros((3 * rows16, 128 * MANY), F32)
        for g in range(groups):
            hot = jnp.where(place + (g * cap - step * 128 * MANY) == slot, 1.0, 0.0).astype(BF16)
            total = total + lax.dot_general(lhs_ref[g], hot, (((1,), (1,)), ((), ())), preferred_element_type=F32)
        total = total[:rows16] + total[rows16 : 2 * rows16] + total[2 * rows16 :]
        for h in range(MANY):
            at = pl.multiple_of((step * MANY + h) * rows, 8)
            out_ref[pl.ds(at, rows), :] = total[:rows, h * 128 : (h + 1) * 128]
        return 0

    lax.fori_loop(0, devices // MANY, several, 0)


def prepare_body(rim, first_ref, neighbours_ref, coupling_ref, inv_ref, blocks_ref, place_ref):
    cells = neighbours_ref.shape[1]
    near = neighbours_ref[...]
    filled = near >= 0
    for u in range(VARS):
        for v in range(VARS):
            total = inv_ref[v, 0:1, :] * coupling_ref[0, u]
            for w in range(1, VARS):
                total = total + inv_ref[v, w : w + 1, :] * coupling_ref[w, u]
            blocks_ref[(v * VARS + u) * 8 : (v * VARS + u) * 8 + NBR, :] = jnp.where(filled, total, 0.0)
    base = lax.broadcasted_iota(I32, (NBR, cells), 1) // 256 * 256 + first_ref[0]
    place_ref[:NBR, :] = jnp.where(filled, near + rim - base, rim)


def forcing_body(cap, groups, rows, modes, rim, arrived_ref, inv_ref, out_ref, two_ref, first_ref, last_ref, table_ref, lhs_ref, tag_ref):
    devices = arrived_ref.shape[0] // rows
    slots = devices * cap
    cells = out_ref.shape[2]
    lane_group = lax.broadcasted_iota(I32, (rows, 128), 1) // cap
    for p in range(devices // groups):
        chunks = [arrived_ref[(p * groups + b) * rows : (p * groups + b + 1) * rows, :] for b in range(groups)]
        for g in range(groups):
            merged = chunks[g]
            for b in range(groups):
                if b != g:
                    turned = pltpu.roll(chunks[b], (b - g) * cap % 128, 1)
                    merged = jnp.where(lane_group == b, turned, merged)
            table_ref[g * rows : (g + 1) * rows, p * 128 : (p + 1) * 128] = merged
    at = 3 * modes
    tag_row = at + 3 * VARS
    tags = table_ref[tag_row // 8 * 8 : tag_row // 8 * 8 + 8, :].T
    tag_ref[...] = jnp.broadcast_to(tags[:, tag_row % 8 : tag_row % 8 + 1], (slots, 128))
    for v in range(VARS):
        load = table_ref[at + 3 * v : at + 3 * v + 1, :] * table_ref[:modes, :]
        for k in range(1, 3):
            load = load + table_ref[at + 3 * v + k : at + 3 * v + k + 1, :] * table_ref[k * modes : (k + 1) * modes, :]
        high, low = split2(load)
        lhs_ref[v * 2 * modes : v * 2 * modes + modes, :] = high
        lhs_ref[v * 2 * modes + modes : (v + 1) * 2 * modes, :] = low
    lane = lax.broadcasted_iota(I32, (slots, 128), 1) + 1

    def tile(t, _):
        lo = pl.multiple_of(t * 512, 512)
        hot = [jnp.where(tag_ref[...] == (lane + (lo + h * 128)).astype(F32), 1.0, 0.0).astype(BF16) for h in range(4)]
        both = dot(lhs_ref[...], jnp.concatenate(hot, axis=1))
        forcing = [both[u * 2 * modes : u * 2 * modes + modes] + both[u * 2 * modes + modes : (u + 1) * 2 * modes] for u in range(VARS)]
        for v in range(VARS):
            total = inv_ref[v, 0:1, pl.ds(lo, 512)] * forcing[0]
            for u in range(1, VARS):
                total = total + inv_ref[v, u : u + 1, pl.ds(lo, 512)] * forcing[u]
            out_ref[v, :, pl.ds(lo, 512)] = total
            high, low = split2(total)
            two_ref[2 * v * modes : (2 * v + 1) * modes, pl.ds(lo, 512)] = high
            two_ref[(2 * v + 1) * modes : (2 * v + 2) * modes, pl.ds(lo, 512)] = low
        return 0

    lax.fori_loop(0, cells // 512, tile, 0)
    first_ref[...] = out_ref[:, :, :rim]
    last_ref[...] = out_ref[:, :, cells - rim :]


def fetch(out_ref, windows, place_ref, lo):
    def step(slots):
        total, at = None, 0
        for two, start, width in windows:
            row = lax.broadcasted_iota(I32, (width, 256), 0) + at
            hot = [jnp.where(row == place_ref[j : j + 1, pl.ds(lo, 256)], 1.0, 0.0).astype(BF16) for j in slots]
            part = dot(two[:, pl.ds(start, width)], jnp.concatenate(hot, axis=1))
            total = part if total is None else total + part
            at += width
        out_ref[:, slots[0] * 256 : (slots[-1] + 1) * 256] = total

    slots = list(range(NBR - BY_LANES))
    return [functools.partial(step, slots[j : j + TOGETHER]) for j in range(0, len(slots), TOGETHER)]


def relax(fetched_ref, source, start_ref, place_ref, blocks_ref, lo, store):
    modes = start_ref.shape[1]
    by_matmul = NBR - BY_LANES
    rows = range(0, ROWS, 8)

    def step(m, h):
        at = pl.multiple_of(lo + h * 128, 128)
        acc = [[start_ref[v, m + i : m + i + 8, pl.ds(at, 128)] for i in rows] for v in range(VARS)]

        def subtract(j, u, values):
            for v in range(VARS):
                row = (v * VARS + u) * 8 + j
                block = blocks_ref[row : row + 1, pl.ds(at, 128)]
                acc[v] = [a - block * value for a, value in zip(acc[v], values)]

        lanes, wheres = [], []
        for j in range(by_matmul, NBR):
            place = jnp.broadcast_to(place_ref[j : j + 1, pl.ds(at, 128)] - h * 128, (8, 128))
            lanes.append(place & 127)
            wheres.append(place >> 7)
        def by_lanes(u):
            around = [[source(u, m + i, h + s) for s in range(5)] for i in rows]
            taken = [
                [[jnp.take_along_axis(x, lane, axis=1, mode="promise_in_bounds") for x in blocks] for blocks in around]
                for lane in lanes
            ]
            for n, where in enumerate(wheres):
                values = []
                for x in taken[n]:
                    value = x[0]
                    for s in range(1, 5):
                        value = jnp.where(where == s, x[s], value)
                    values.append(value)
                subtract(by_matmul + n, u, values)

        def by_dots(u):
            for j in range(by_matmul):
                values = []
                for i in rows:
                    r, c = u * 2 * modes + m + i, j * 256 + h * 128
                    values.append(
                        fetched_ref[r : r + 8, c : c + 128] + fetched_ref[r + modes : r + modes + 8, c : c + 128]
                    )
                subtract(j, u, values)

        for u in range(VARS):
            by_lanes(u)
        for u in range(VARS):
            by_dots(u)
        for v in range(VARS):
            store(v, m, h, jnp.concatenate(acc[v], axis=0))

    return [functools.partial(step, m, h) for m in range(0, modes, ROWS) for h in range(2)]


def run(steps):
    for step in steps:
        step()


def put_two(two_ref, modes, v, m, at, high, low):
    value_rows = high.shape[0]
    two_ref[2 * v * modes + m : 2 * v * modes + m + value_rows, at] = high
    two_ref[(2 * v + 1) * modes + m : (2 * v + 1) * modes + m + value_rows, at] = low


def inner_body(rim, last, x_ref, two_ref, start_ref, place_ref, blocks_ref, *refs):
    if last:
        mid_two_ref, fetched_ref = refs
    else:
        mid_ref, mid_two_ref, fetched_ref = refs
    modes, cells = x_ref.shape[1:]
    tiles = (cells - 2 * rim) // 256

    def load(t, ref):
        lo = pl.multiple_of(rim + t * 256, 256)
        return fetch(ref, [(two_ref, pl.multiple_of(lo - rim, 256), 256 + 2 * rim)], place_ref, lo)

    def work(t, ref):
        lo = pl.multiple_of(rim + t * 256, 256)

        def store(v, m, h, value):
            at = pl.ds(pl.multiple_of(t * 256 + h * 128, 128), 128)
            if not last:
                mid_ref[v, m : m + ROWS, at] = value
            put_two(mid_two_ref, modes, v, m, at, *split2(value))

        def source(u, m, s):
            return x_ref[u, m : m + 8, pl.ds(pl.multiple_of(lo - rim + s * 128, 128), 128)]

        return relax(ref, source, start_ref, place_ref, blocks_ref, lo, store)

    def one_tile(t, _):
        run(load(t, fetched_ref) + work(t, fetched_ref))
        return 0

    lax.fori_loop(0, tiles, one_tile, 0)


def outer_body(rim, last, x_ref, two_ref, before_ref, after_ref, start_ref, place_ref, blocks_ref, *refs):
    if last:
        mid_two_ref, out_two_ref, gram_ref, window_ref, window_two_ref, fetched_ref = refs
    else:
        mid_ref, mid_two_ref, out_ref, out_two_ref, first_ref, last_ref, window_ref, window_two_ref, fetched_ref = refs
    modes, cells = x_ref.shape[1:]
    ends = cells - rim
    near = 256 + rim
    window_ref[0, :, :, :rim] = before_ref[...]
    window_ref[0, :, :, rim:] = x_ref[:, :, :near]
    window_ref[1, :, :, :near] = x_ref[:, :, cells - near :]
    window_ref[1, :, :, near:] = after_ref[...]
    window_two_ref[0, :, rim:] = two_ref[:, :near]
    window_two_ref[1, :, :near] = two_ref[:, cells - near :]
    for side, (ref, at) in enumerate(((before_ref, 0), (after_ref, near))):
        for u in range(VARS):
            high, low = split2(ref[u])
            window_two_ref[side, 2 * u * modes : (2 * u + 1) * modes, at : at + rim] = high
            window_two_ref[side, (2 * u + 1) * modes : (2 * u + 2) * modes, at : at + rim] = low
    out_two_ref[:, rim:ends] = mid_two_ref[...]
    if not last:
        out_ref[:, :, rim:ends] = mid_ref[...]

    def one_side(t, _):
        lo = pl.multiple_of(t * ends, 256)

        def source(u, m, s):
            return window_ref[t, u, m : m + 8, s * 128 : (s + 1) * 128]

        def store(v, m, h, value):
            at = pl.ds(pl.multiple_of(lo + h * 128, 128), 128)
            if not last:
                out_ref[v, m : m + ROWS, at] = value
            put_two(out_two_ref, modes, v, m, at, *split2(value))

        run(
            fetch(fetched_ref, [(window_two_ref.at[t], 0, near + rim)], place_ref, lo)
            + relax(fetched_ref, source, start_ref, place_ref, blocks_ref, lo, store)
        )
        return 0

    lax.fori_loop(0, 2, one_side, 0)
    if not last:
        first_ref[...] = out_ref[:, :, :rim]
        last_ref[...] = out_ref[:, :, ends:]
    if last:
        gram = jnp.zeros((2 * modes, 2 * modes), F32)
        for v in range(VARS):
            both = out_two_ref[2 * v * modes : (2 * v + 2) * modes, :]
            gram = gram + lax.dot_general(both, both, (((1,), (1,)), ((), ())), preferred_element_type=F32)
        gram = gram[:modes] + gram[modes:]
        gram = gram + pltpu.roll(gram, modes, 1)
        gram_ref[...] = jnp.where(lax.broadcasted_iota(I32, gram.shape, 1) < modes, gram, 0.0)


def basis_body(norm, gram_ref, field_ref, out_ref, factor_ref, lhs_ref, inverse_ref):
    modes = factor_ref.shape[0]

    @pl.when(pl.program_id(0) == 0)
    def _():
        row = lax.broadcasted_iota(I32, (8, 2 * modes), 0)
        lane = lax.broadcasted_iota(I32, (8, 2 * modes), 1)
        parts = [jnp.where(lane == row + (i + modes), 1.0, gram_ref[i : i + 8, :]) for i in range(0, modes, 8)]
        pivots = []
        for k in range(0, modes, STEP):
            g, r = k // 8, k % 8
            steps = range(STEP)
            rows = [parts[g][r + i : r + i + 1, :] for i in steps]
            block = [[jnp.broadcast_to(x[:, k + i : k + i + 1], x.shape) for i in steps] for x in rows]
            inverses = []
            for i in steps:
                inverses.append(1.0 / block[i][i])
                for j in range(i + 1, STEP):
                    ratio = block[j][i] * inverses[i]
                    block[j] = [x - ratio * y for x, y in zip(block[j], block[i])]
                    rows[j] = rows[j] - ratio * rows[i]
                pivots.append(block[i][i])
            scaled = [x * inverse for x, inverse in zip(rows, inverses)]
            for n in range(g, modes // 8):
                part = parts[n]
                columns = [jnp.broadcast_to(part[:, k + i : k + i + 1], part.shape) for i in steps]
                for i in steps:
                    for j in range(i + 1, STEP):
                        columns[j] = columns[j] - columns[i] * (block[i][j] * inverses[i])
                for i in steps:
                    column = jnp.where(row >= r + STEP, columns[i], 0.0) if n == g else columns[i]
                    part = part - column * scaled[i]
                if n == g:
                    for i in steps:
                        part = jnp.where(row == r + i, rows[i], part)
                parts[n] = part
        for i in range(modes // 8):
            scale = 1.0 / jnp.sqrt(jnp.concatenate(pivots[i * 8 : (i + 1) * 8], axis=0))
            part = parts[i] * scale
            upper = jnp.where(lane >= row + i * 8, part / norm, 0.0)
            factor_ref[i * 8 : (i + 1) * 8, :] = upper[:, :modes]
            part = part * norm
            inverse_ref[i * 8 : (i + 1) * 8, :] = jnp.where(lane < modes, pltpu.roll(part, modes, 1), part)
        inverse = inverse_ref[...]
        high, low = split2(inverse)
        lhs_ref[:modes, :] = high
        lhs_ref[modes:, :] = low

    both = dot(lhs_ref[...], field_ref[0])
    out_ref[0] = both[:modes] + both[modes:]


def local(mode_shapes, wall_coupling, owner_dev, owner_cell, neighbours, coupling_blocks, inv_blocks):
    devices = lax.axis_size("slab")
    cells = inv_blocks.shape[2]
    nodes, modes = mode_shapes.shape[0], mode_shapes.shape[1] // 3
    cap = max(2, 2 * nodes // devices)
    rim = cells // 8
    groups = 128 // cap
    columns = 3 * modes + 3 * VARS + 1
    rows = round_up(-(-columns // groups), 8)
    rows16 = round_up(rows, 16)
    packed = call(
        functools.partial(pack_body, cap, groups, rows),
        jax.ShapeDtypeStruct((devices * rows, 128), F32),
        mode_shapes.T, wall_coupling.T, owner_dev.T, owner_cell[None, :],
        grid=(1,),
        in_specs=[pl.BlockSpec((n, nodes), lambda i: (0, 0)) for n in (3 * modes, 3 * VARS, 1, 1)],
        out_specs=pl.BlockSpec((devices * rows, 128), lambda i: (0, 0)),
        scratch=[pltpu.VMEM(((groups - 1) * rows + rows16, nodes), F32), pltpu.VMEM((groups, 3 * rows16, nodes), BF16)],
        name="pack", limit=60,
    )
    arrived = lax.all_to_all(packed, "slab", split_axis=0, concat_axis=0, tiled=True)
    field = jax.ShapeDtypeStruct((VARS, modes, cells), F32)
    field_two = jax.ShapeDtypeStruct((VARS * 2 * modes, cells), BF16)
    edge = jax.ShapeDtypeStruct((VARS, modes, rim), F32)
    blocks, place = call(
        functools.partial(prepare_body, rim),
        (jax.ShapeDtypeStruct((VARS * VARS * 8, cells), F32), jax.ShapeDtypeStruct((8, cells), I32)),
        (lax.axis_index("slab") * cells).astype(I32)[None], neighbours, coupling_blocks.transpose(1, 2, 0, 3), inv_blocks,
        in_specs=[pl.BlockSpec(memory_space=pltpu.SMEM)] + [VMEM] * 3,
        cost_estimate=pl.CostEstimate(flops=10**9, bytes_accessed=10**7, transcendentals=0),
        name="prepare",
    )
    start, two, first, final = call(
        functools.partial(forcing_body, cap, groups, rows, modes, rim),
        (field, field_two, edge, edge),
        arrived, inv_blocks,
        scratch=[
            pltpu.VMEM((groups * rows, devices * cap), F32),
            pltpu.VMEM((VARS * 2 * modes, devices * cap), BF16),
            pltpu.VMEM((devices * cap, 128), F32),
        ],
        name="forcing",
    )
    up = [(i, i + 1) for i in range(devices - 1)]
    down = [(j, i) for i, j in up]
    x = start
    inner = cells - 2 * rim
    mid = jax.ShapeDtypeStruct((VARS, modes, inner), F32)
    mid_two = jax.ShapeDtypeStruct((VARS * 2 * modes, inner), BF16)
    fetched = [pltpu.VMEM((VARS * 2 * modes, (NBR - BY_LANES) * 256), F32)]
    cost = pl.CostEstimate(flops=10**10, bytes_accessed=3 * 10**7, transcendentals=0)
    for last in (False, True):
        before = lax.ppermute(final, "slab", up)
        after = lax.ppermute(first, "slab", down)
        middle = call(
            functools.partial(inner_body, rim, last), (mid_two,) if last else (mid, mid_two),
            x, two, start, place, blocks, scratch=fetched, cost_estimate=cost, name="inner_last" if last else "inner",
        )
        windows = [
            pltpu.VMEM((2, VARS, modes, 256 + 2 * rim), F32), pltpu.VMEM((2, VARS * 2 * modes, 256 + 2 * rim), BF16)
        ]
        if last:
            two, gram = call(
                functools.partial(outer_body, rim, last), (field_two, jax.ShapeDtypeStruct((modes, 2 * modes), F32)),
                x, two, before, after, start, place, blocks, *middle,
                scratch=windows + fetched, name="outer_last",
            )
        else:
            x, two, first, final = call(
                functools.partial(outer_body, rim, last), (field, field_two, edge, edge),
                x, two, before, after, start, place, blocks, *middle, scratch=windows + fetched, name="outer",
            )
    field = two.reshape(VARS, 2 * modes, cells)
    reach = 1
    while reach < devices:
        gram = gram + lax.ppermute(gram, "slab", [(i, i ^ reach) for i in range(devices)])
        reach *= 2
    norm = math.sqrt(VARS * cells * devices)
    return call(
        functools.partial(basis_body, norm),
        (jax.ShapeDtypeStruct((VARS, modes, cells), F32), jax.ShapeDtypeStruct((modes, modes), F32)),
        gram, field,
        grid=(VARS,),
        in_specs=[
            pl.BlockSpec((modes, 2 * modes), lambda v: (0, 0)),
            pl.BlockSpec((1, 2 * modes, cells), lambda v: (v, 0, 0)),
        ],
        out_specs=(
            pl.BlockSpec((1, modes, cells), lambda v: (v, 0, 0)),
            pl.BlockSpec((modes, modes), lambda v: (0, 0)),
        ),
        scratch=[pltpu.VMEM((2 * modes, 2 * modes), BF16), pltpu.VMEM((modes, 2 * modes), F32)],
        name="basis",
    )


def solution(mesh):
    in_specs = (
        P(("groups", "slab"), None),
        P(("groups", "slab"), None),
        P(("groups", "slab"), None),
        P(("groups", "slab")),
        P(None, ("groups", "slab")),
        P(None, None, None, ("groups", "slab")),
        P(None, None, ("groups", "slab")),
    )
    out_specs = (P(None, None, ("groups", "slab")), P("groups", None))
    return jax.shard_map(local, mesh=mesh, in_specs=in_specs, out_specs=out_specs, check_vma=False)
```

time: 124 us -> 107 us (0.86)
  starting transfers between devices: 36.8 us -> 29.2 us
  local copies, waits for them, and re-layouts: 5.91 us -> 1.45 us
  waiting for transfers between devices: 26.2 us -> 23.9 us
  Pallas kernels: 53.5 us -> 51.4 us
    ppermute x4, starting transfers between devices: 15.2 us -> 8.61 us  [the longest x2 5.85 us: local(): before = lax.ppermute(final, 'slab', up)]
    unnamed x10 -> x12, local copies, waits for them, and re-layouts: 5.79 us -> 1.45 us
    pallas_call x6 -> x8, Pallas kernels: 53.5 us -> 51.4 us  [call(): pl.pallas_call(body, out_shape=out_shape, in_specs=kw.pop('in_specs', [VM...]
  transfers between devices with their start and end apart: 9 -> 9, of which waited for: 6 -> 5; matrix products, arithmetic and copies ran while one was open for 2% -> 0% of each run, Pallas kernels for 1% -> 21%
where the time goes in v2:
time: 107 us
  Pallas kernels  51.4 us (48%)
  starting transfers between devices  29.2 us (27%)
  waiting for transfers between devices  23.9 us (22%)
  local copies, waits for them, and re-layouts  1.45 us (1%)
    pallas_call x8, Pallas kernels, call(): pl.pallas_call(body, out_shape=out_shape, in_specs=kw.pop('in_specs', [VM...  51.4 us
    all_to_all x1, waiting for transfers between devices, local(): lax.all_to_all(packed, 'slab', split_axis=0, concat_axis=0, tiled=True)  17.3 us
    ppermute x4, starting transfers between devices, local(): lax.ppermute(gram, 'slab', [(i, i ^ reach) for i in range(devices)])  13.2 us
    all_to_all x1, starting transfers between devices, local(): lax.all_to_all(packed, 'slab', split_axis=0, concat_axis=0, tiled=True)  7.39 us
    ppermute x4, waiting for transfers between devices, local(): lax.ppermute(gram, 'slab', [(i, i ^ reach) for i in range(devices)])  6.54 us
    ppermute x2, starting transfers between devices, local(): before = lax.ppermute(final, 'slab', up)  5.85 us
    ppermute x2, starting transfers between devices, local(): after = lax.ppermute(first, 'slab', down)  2.76 us
  transfers between devices with their start and end apart: 9, of which 5 were waited for; matrix products, arithmetic and copies ran while one was open for 0% of the time, Pallas kernels for 21%

profile of v2, /device:TPU:0, one launch (start us, length us, event | category | flops | bytes accessed | tf_op | source)
XLA Modules:
  0.0 106.8 jit_solution(2188156350686780375)
XLA Ops:
  0.6 0.0 copy-start.3
  0.6 0.0 copy-start.5
  0.7 4.5 %pack.1 = f32[1664,128]{1,0:T(8,128)} custom-call(f32[192,512]{1,0:T(8,128)} %bitcast.13, f32[15,512]{1,0:T(8,128)} %bitcast.14, s32[1,512]{1,0:T(1,128)} %bitcast.15, s32[1,512]{1,0:T(1,128)} %bitcast.16), custom_call_target="tpu_custom_call" | custom-call | tf_op jit(solution)/shard_map/pack/pallas_call | solution.py:36
  5.2 7.4 %all-to-all-start = ((f32[16,104,128]{2,1,0:T(8,128)}), f32[16,104,128]{2,1,0:T(8,128)S(1)}, u32[]{:S(2)}, u32[]{:S(2)}) async-start(f32[16,104,128]{2,1,0:T(8,128)} %bitcast.12), calls=%async_computation | async-start | bytes 1703936 | tf_op jit(solution)/shard_map/all_to_all | solution.py:390
  12.6 0.0 copy-start.4
  12.6 1.4 %copy-done.4 = f32[6,5,5,2048]{3,0,2,1:T(8,128)S(1)} copy-done((f32[6,5,5,2048]{3,0,2,1:T(8,128)S(1)}, f32[6,5,5,2048]{3,0,2,1:T(8,128)}, u32[]{:S(2)}) %copy-start.4) | copy-done | bytes 1228824
  14.0 1.0 prepare.1
  15.0 17.3 %all-to-all-done = f32[16,104,128]{2,1,0:T(8,128)S(1)} async-done(((f32[16,104,128]{2,1,0:T(8,128)}), f32[16,104,128]{2,1,0:T(8,128)S(1)}, u32[]{:S(2)}, u32[]{:S(2)}) %all-to-all-start) | async-done | bytes 852000 | tf_op jit(solution)/shard_map/all_to_all | solution.py:390
  32.3 5.3 %forcing.1 = (f32[5,64,2048]{2,1,0:T(8,128)S(1)}, bf16[640,2048]{1,0:T(8,128)(2,1)S(1)}, f32[5,64,256]{2,1,0:T(8,128)S(1)}, f32[5,64,256]{2,1,0:T(8,128)S(1)}) custom-call(f32[1664,128]{1,0:T(8,128)S(1)} %bitcast.9, f32[5,5,2048]{2,1,0:T(8,128)S(1)} %copy-done.3), custom_call_target="tpu_custom_call" | custom-call | tf_op jit(solution)/shard_map/forcing/pallas_call | solution.py:36
  37.7 0.0 copy-start
  37.7 2.3 %collective-permute-start = (f32[5,64,256]{2,1,0:T(8,128)S(1)}, f32[5,64,256]{2,1,0:T(8,128)S(1)}, u32[]{:S(2)}, u32[]{:S(2)}) collective-permute-start(f32[5,64,256]{2,1,0:T(8,128)S(1)} %get-tuple-element.18), channel_id=1, source_target_pairs={{0,1},{1,2},{2,3},{3,4},{4,5},{5,6},{6,7},{7,8},{8,9},{9,10},{10,1... | collective-permute-start | bytes 983048 | tf_op jit(solution)/shard_map/ppermute | solution.py:422
  40.0 1.3 %collective-permute-start.1 = (f32[5,64,256]{2,1,0:T(8,128)S(1)}, f32[5,64,256]{2,1,0:T(8,128)S(1)}, u32[]{:S(2)}, u32[]{:S(2)}) collective-permute-start(f32[5,64,256]{2,1,0:T(8,128)S(1)} %get-tuple-element.19), channel_id=1, source_target_pairs={{1,0},{2,1},{3,2},{4,3},{5,4},{6,5},{7,6},{8,7},{9,8},{10,9},{11,1... | collective-permute-start | bytes 983048 | tf_op jit(solution)/shard_map/ppermute | solution.py:423
  41.3 10.8 %inner.1 = (f32[5,64,1536]{2,1,0:T(8,128)S(1)}, bf16[640,1536]{1,0:T(8,128)(2,1)S(1)}) custom-call(f32[5,64,2048]{2,1,0:T(8,128)S(1)} %get-tuple-element.16.x_ref.start_ref, bf16[640,2048]{1,0:T(8,128)(2,1)S(1)} %get-tuple-element.17.two_ref, f32[5,64,2048]{2,1,0:T(8,128)S(1)} %get-tuple-element.16.x_ref.start_ref, ...), custom_call_target="tpu_custom_call" | custom-call | flops 10000000000 | bytes 30000000 | tf_op jit(solution)/shard_map/inner/pallas_call | solution.py:36
  52.1 0.0 collective-permute-done.before_ref
  52.1 0.0 collective-permute-done.1.after_ref
  52.1 0.0 copy-start.1
  52.1 7.6 %outer.1 = (f32[5,64,2048]{2,1,0:T(8,128)S(1)}, bf16[640,2048]{1,0:T(8,128)(2,1)S(1)}, f32[5,64,256]{2,1,0:T(8,128)S(1)}, f32[5,64,256]{2,1,0:T(8,128)S(1)}) custom-call(f32[5,64,2048]{2,1,0:T(8,128)} %copy-done, bf16[640,2048]{1,0:T(8,128)(2,1)} %copy-done.2, f32[5,64,256]{2,1,0:T(8,128)S(1)} %collective-permute-done.before_ref, ...), custom_call_target="tpu_custom_call" | custom-call | tf_op jit(solution)/shard_map/outer/pallas_call | solution.py:36
  59.7 3.6 %collective-permute-start.2 = (f32[5,64,256]{2,1,0:T(8,128)S(1)}, f32[5,64,256]{2,1,0:T(8,128)S(1)}, u32[]{:S(2)}, u32[]{:S(2)}) collective-permute-start(f32[5,64,256]{2,1,0:T(8,128)S(1)} %get-tuple-element.26), channel_id=1, source_target_pairs={{0,1},{1,2},{2,3},{3,4},{4,5},{5,6},{6,7},{7,8},{8,9},{9,10},{10,1... | collective-permute-start | bytes 983048 | tf_op jit(solution)/shard_map/ppermute | solution.py:422
  63.3 1.5 %collective-permute-start.3 = (f32[5,64,256]{2,1,0:T(8,128)S(1)}, f32[5,64,256]{2,1,0:T(8,128)S(1)}, u32[]{:S(2)}, u32[]{:S(2)}) collective-permute-start(f32[5,64,256]{2,1,0:T(8,128)S(1)} %get-tuple-element.27), channel_id=1, source_target_pairs={{1,0},{2,1},{3,2},{4,3},{5,4},{6,5},{7,6},{8,7},{9,8},{10,9},{11,1... | collective-permute-start | bytes 983048 | tf_op jit(solution)/shard_map/ppermute | solution.py:423
  64.8 10.7 %inner_last.1.refs_0_ = bf16[640,1536]{1,0:T(8,128)(2,1)S(1)} custom-call(f32[5,64,2048]{2,1,0:T(8,128)S(1)} %get-tuple-element.24.x_ref, bf16[640,2048]{1,0:T(8,128)(2,1)S(1)} %get-tuple-element.25.two_ref, f32[5,64,2048]{2,1,0:T(8,128)S(1)} %copy-done.1, s32[8,2048]{1,0:T(8,128)S(1)} %get-tuple-element.20.place_ref, ...), custom_call_target="tpu_custom_call" | custom-call | flops 10000000000 | bytes 30000000 | tf_op jit(solution)/shard_map/inner_last/pallas_call | solution.py:36
  75.5 0.0 collective-permute-done.2.before_ref
  75.5 0.0 collective-permute-done.3.after_ref
  75.5 6.6 %outer_last.1 = (bf16[640,2048]{1,0:T(8,128)(2,1)S(1)}, f32[64,128]{1,0:T(8,128)S(1)}) custom-call(f32[5,64,2048]{2,1,0:T(8,128)S(1)} %get-tuple-element.24.x_ref, bf16[640,2048]{1,0:T(8,128)(2,1)S(1)} %get-tuple-element.25.two_ref, f32[5,64,256]{2,1,0:T(8,128)S(1)} %collective-permute-done.2.before_ref, f32[5,64,256]{2,1,0:T(8,128)S(1)} %collective-permute-done.3.after_ref, ...), custom_call_target="tpu_custom_call" | custom-call | tf_op jit(solution)/shard_map/outer_last/pallas_call | solution.py:36
  82.1 2.4 %collective-permute-start.4 = (f32[64,128]{1,0:T(8,128)S(1)}, f32[64,128]{1,0:T(8,128)S(1)}, u32[]{:S(2)}, u32[]{:S(2)}) collective-permute-start(f32[64,128]{1,0:T(8,128)S(1)} %get-tuple-element.28), channel_id=1, source_target_pairs={{0,1},{1,0},{2,3},{3,2},{4,5},{5,4},{6,7},{7,6},{8,9},{9,8},{10,11... | collective-permute-start | bytes 98312 | tf_op jit(solution)/shard_map/ppermute | solution.py:445
  84.5 0.9 collective-permute-done.4
  85.4 3.5 %collective-permute-start.5 = (f32[64,128]{1,0:T(8,128)S(1)}, f32[64,128]{1,0:T(8,128)S(1)}, u32[]{:S(2)}, u32[]{:S(2)}) collective-permute-start(f32[64,128]{1,0:T(8,128)S(1)} %add.12), channel_id=1, source_target_pairs={{0,2},{1,3},{2,0},{3,1},{4,6},{5,7},{6,4},{7,5},{8,10},{9,11},{10,... | collective-permute-start | bytes 98312 | tf_op jit(solution)/shard_map/ppermute | solution.py:445
  88.9 1.9 %collective-permute-done.5 = f32[64,128]{1,0:T(8,128)S(1)} collective-permute-done((f32[64,128]{1,0:T(8,128)S(1)}, f32[64,128]{1,0:T(8,128)S(1)}, u32[]{:S(2)}, u32[]{:S(2)}) %collective-permute-start.5) | collective-permute-done | bytes 32800 | tf_op jit(solution)/shard_map/ppermute | solution.py:445
  90.8 3.4 %collective-permute-start.6 = (f32[64,128]{1,0:T(8,128)S(1)}, f32[64,128]{1,0:T(8,128)S(1)}, u32[]{:S(2)}, u32[]{:S(2)}) collective-permute-start(f32[64,128]{1,0:T(8,128)S(1)} %add.13), channel_id=1, source_target_pairs={{0,4},{1,5},{2,6},{3,7},{4,0},{5,1},{6,2},{7,3},{8,12},{9,13},{10,... | collective-permute-start | bytes 98312 | tf_op jit(solution)/shard_map/ppermute | solution.py:445
  94.2 1.9 %collective-permute-done.6 = f32[64,128]{1,0:T(8,128)S(1)} collective-permute-done((f32[64,128]{1,0:T(8,128)S(1)}, f32[64,128]{1,0:T(8,128)S(1)}, u32[]{:S(2)}, u32[]{:S(2)}) %collective-permute-start.6) | collective-permute-done | bytes 32800 | tf_op jit(solution)/shard_map/ppermute | solution.py:445
  96.1 3.9 %collective-permute-start.7 = (f32[64,128]{1,0:T(8,128)S(1)}, f32[64,128]{1,0:T(8,128)S(1)}, u32[]{:S(2)}, u32[]{:S(2)}) collective-permute-start(f32[64,128]{1,0:T(8,128)S(1)} %add.14), channel_id=1, source_target_pairs={{0,8},{1,9},{2,10},{3,11},{4,12},{5,13},{6,14},{7,15},{8,0},{9,1},... | collective-permute-start | bytes 98312 | tf_op jit(solution)/shard_map/ppermute | solution.py:445
  100.0 1.9 %collective-permute-done.7 = f32[64,128]{1,0:T(8,128)S(1)} collective-permute-done((f32[64,128]{1,0:T(8,128)S(1)}, f32[64,128]{1,0:T(8,128)S(1)}, u32[]{:S(2)}, u32[]{:S(2)}) %collective-permute-start.7) | collective-permute-done | bytes 32800 | tf_op jit(solution)/shard_map/ppermute | solution.py:445
  101.9 4.9 %basis.1 = (f32[5,64,2048]{2,1,0:T(8,128)}, f32[64,64]{1,0:T(8,128)}) custom-call(f32[64,128]{1,0:T(8,128)S(1)} %add.15.gram_ref, bf16[5,128,2048]{2,1,0:T(8,128)(2,1)S(1)} %bitcast.10), custom_call_target="tpu_custom_call" | custom-call | tf_op jit(solution)/shard_map/basis/pallas_call | solution.py:36
  (10 shorter events, 0.0 us)
Async XLA Ops:
  0.6 11.9 %copy-start.3 = (f32[5,5,2048]{2,1,0:T(8,128)S(1)}, f32[5,5,2048]{2,1,0:T(8,128)}, u32[]{:S(2)}) copy-start(f32[5,5,2048]{2,1,0:T(8,128)} %inv_ref.3) | copy-start | bytes 614404
  0.6 11.9 %copy-start.5 = (s32[6,2048]{1,0:T(8,128)S(1)}, s32[6,2048]{1,0:T(8,128)}, u32[]{:S(2)}) copy-start(s32[6,2048]{1,0:T(8,128)} %neighbours_ref.1) | copy-start | bytes 147460
  5.2 27.2 %all-to-all-start = ((f32[16,104,128]{2,1,0:T(8,128)}), f32[16,104,128]{2,1,0:T(8,128)S(1)}, u32[]{:S(2)}, u32[]{:S(2)}) async-start(f32[16,104,128]{2,1,0:T(8,128)} %bitcast.12), calls=%async_computation | async-start | bytes 1703936 | tf_op jit(solution)/shard_map/all_to_all | solution.py:390
  12.6 1.4 %copy-start.4 = (f32[6,5,5,2048]{3,0,2,1:T(8,128)S(1)}, f32[6,5,5,2048]{3,0,2,1:T(8,128)}, u32[]{:S(2)}) copy-start(f32[6,5,5,2048]{3,0,2,1:T(8,128)} %param.12) | copy-start | bytes 3686404
  37.7 14.4 %copy-start = (f32[5,64,2048]{2,1,0:T(8,128)}, f32[5,64,2048]{2,1,0:T(8,128)S(1)}, u32[]{:S(2)}) copy-start(f32[5,64,2048]{2,1,0:T(8,128)S(1)} %get-tuple-element.16.x_ref.start_ref) | copy-start | bytes 7864324
  37.7 14.4 %copy-start.2 = (bf16[640,2048]{1,0:T(8,128)(2,1)}, bf16[640,2048]{1,0:T(8,128)(2,1)S(1)}, u32[]{:S(2)}) copy-start(bf16[640,2048]{1,0:T(8,128)(2,1)S(1)} %get-tuple-element.17.two_ref) | copy-start | bytes 7864324
  37.7 14.4 %collective-permute-start = (f32[5,64,256]{2,1,0:T(8,128)S(1)}, f32[5,64,256]{2,1,0:T(8,128)S(1)}, u32[]{:S(2)}, u32[]{:S(2)}) collective-permute-start(f32[5,64,256]{2,1,0:T(8,128)S(1)} %get-tuple-element.18), channel_id=1, source_target_pairs={{0,1},{1,2},{2,3},{3,4},{4,5},{5,6},{6,7},{7,8},{8,9},{9,10},{10,1... | collective-permute-start | bytes 983048 | tf_op jit(solution)/shard_map/ppermute | solution.py:422
  40.0 12.1 %collective-permute-start.1 = (f32[5,64,256]{2,1,0:T(8,128)S(1)}, f32[5,64,256]{2,1,0:T(8,128)S(1)}, u32[]{:S(2)}, u32[]{:S(2)}) collective-permute-start(f32[5,64,256]{2,1,0:T(8,128)S(1)} %get-tuple-element.19), channel_id=1, source_target_pairs={{1,0},{2,1},{3,2},{4,3},{5,4},{6,5},{7,6},{8,7},{9,8},{10,9},{11,1... | collective-permute-start | bytes 983048 | tf_op jit(solution)/shard_map/ppermute | solution.py:423
  52.1 12.7 %copy-start.1 = (f32[5,64,2048]{2,1,0:T(8,128)S(1)}, f32[5,64,2048]{2,1,0:T(8,128)}, u32[]{:S(2)}) copy-start(f32[5,64,2048]{2,1,0:T(8,128)} %copy-done) | copy-start | bytes 7864324
  59.7 15.8 %collective-permute-start.2 = (f32[5,64,256]{2,1,0:T(8,128)S(1)}, f32[5,64,256]{2,1,0:T(8,128)S(1)}, u32[]{:S(2)}, u32[]{:S(2)}) collective-permute-start(f32[5,64,256]{2,1,0:T(8,128)S(1)} %get-tuple-element.26), channel_id=1, source_target_pairs={{0,1},{1,2},{2,3},{3,4},{4,5},{5,6},{6,7},{7,8},{8,9},{9,10},{10,1... | collective-permute-start | bytes 983048 | tf_op jit(solution)/shard_map/ppermute | solution.py:422
  63.3 12.2 %collective-permute-start.3 = (f32[5,64,256]{2,1,0:T(8,128)S(1)}, f32[5,64,256]{2,1,0:T(8,128)S(1)}, u32[]{:S(2)}, u32[]{:S(2)}) collective-permute-start(f32[5,64,256]{2,1,0:T(8,128)S(1)} %get-tuple-element.27), channel_id=1, source_target_pairs={{1,0},{2,1},{3,2},{4,3},{5,4},{6,5},{7,6},{8,7},{9,8},{10,9},{11,1... | collective-permute-start | bytes 983048 | tf_op jit(solution)/shard_map/ppermute | solution.py:423
  82.1 3.3 %collective-permute-start.4 = (f32[64,128]{1,0:T(8,128)S(1)}, f32[64,128]{1,0:T(8,128)S(1)}, u32[]{:S(2)}, u32[]{:S(2)}) collective-permute-start(f32[64,128]{1,0:T(8,128)S(1)} %get-tuple-element.28), channel_id=1, source_target_pairs={{0,1},{1,0},{2,3},{3,2},{4,5},{5,4},{6,7},{7,6},{8,9},{9,8},{10,11... | collective-permute-start | bytes 98312 | tf_op jit(solution)/shard_map/ppermute | solution.py:445
  85.4 5.4 %collective-permute-start.5 = (f32[64,128]{1,0:T(8,128)S(1)}, f32[64,128]{1,0:T(8,128)S(1)}, u32[]{:S(2)}, u32[]{:S(2)}) collective-permute-start(f32[64,128]{1,0:T(8,128)S(1)} %add.12), channel_id=1, source_target_pairs={{0,2},{1,3},{2,0},{3,1},{4,6},{5,7},{6,4},{7,5},{8,10},{9,11},{10,... | collective-permute-start | bytes 98312 | tf_op jit(solution)/shard_map/ppermute | solution.py:445
  90.8 5.3 %collective-permute-start.6 = (f32[64,128]{1,0:T(8,128)S(1)}, f32[64,128]{1,0:T(8,128)S(1)}, u32[]{:S(2)}, u32[]{:S(2)}) collective-permute-start(f32[64,128]{1,0:T(8,128)S(1)} %add.13), channel_id=1, source_target_pairs={{0,4},{1,5},{2,6},{3,7},{4,0},{5,1},{6,2},{7,3},{8,12},{9,13},{10,... | collective-permute-start | bytes 98312 | tf_op jit(solution)/shard_map/ppermute | solution.py:445
  96.1 5.8 %collective-permute-start.7 = (f32[64,128]{1,0:T(8,128)S(1)}, f32[64,128]{1,0:T(8,128)S(1)}, u32[]{:S(2)}, u32[]{:S(2)}) collective-permute-start(f32[64,128]{1,0:T(8,128)S(1)} %add.14), channel_id=1, source_target_pairs={{0,8},{1,9},{2,10},{3,11},{4,12},{5,13},{6,14},{7,15},{8,0},{9,1},... | collective-permute-start | bytes 98312 | tf_op jit(solution)/shard_map/ppermute | solution.py:445

commit v3 on v2

--- a/solution.py
+++ b/solution.py
@@ -13,6 +13,7 @@
 BY_LANES = 2
 ROWS = 16
 TOGETHER = 4
+LIMIT = 16
 MANY = 4
 STEP = 8
 F32, BF16, I32 = jnp.float32, jnp.bfloat16, jnp.int32
@@ -32,7 +33,7 @@
     return jnp.dot(a, b, preferred_element_type=F32)
 
 
-def call(body, out_shape, *args, name, scratch=(), limit=40, flops=0, **kw):
+def call(body, out_shape, *args, name, scratch=(), limit=LIMIT, flops=0, **kw):
     return pl.pallas_call(
         body,
         out_shape=out_shape,
@@ -312,59 +313,63 @@
             gram = gram + lax.dot_general(both, both, (((1,), (1,)), ((), ())), preferred_element_type=F32)
         gram = gram[:modes] + gram[modes:]
         gram = gram + pltpu.roll(gram, modes, 1)
-        gram_ref[...] = jnp.where(lax.broadcasted_iota(I32, gram.shape, 1) < modes, gram, 0.0)
-
-
-def basis_body(norm, gram_ref, field_ref, out_ref, factor_ref, lhs_ref, inverse_ref):
+        half = modes // 2
+        gram_ref[...] = jnp.where(lax.broadcasted_iota(I32, (half, 2 * modes), 1) < modes, gram[:half], gram[half:])
+
+
+def basis_body(norm, gram_ref, field_ref, out_ref, factor_ref, inverse_ref, held_ref, done_ref):
     modes = factor_ref.shape[0]
-
-    @pl.when(pl.program_id(0) == 0)
-    def _():
-        row = lax.broadcasted_iota(I32, (8, 2 * modes), 0)
-        lane = lax.broadcasted_iota(I32, (8, 2 * modes), 1)
-        parts = [jnp.where(lane == row + (i + modes), 1.0, gram_ref[i : i + 8, :]) for i in range(0, modes, 8)]
-        pivots = []
-        for k in range(0, modes, STEP):
-            g, r = k // 8, k % 8
-            steps = range(STEP)
-            rows = [parts[g][r + i : r + i + 1, :] for i in steps]
-            block = [[jnp.broadcast_to(x[:, k + i : k + i + 1], x.shape) for i in steps] for x in rows]
-            inverses = []
+    row = lax.broadcasted_iota(I32, (8, 2 * modes), 0)
+    lane = lax.broadcasted_iota(I32, (8, 2 * modes), 1)
+    parts = []
+    for i in range(0, modes, 8):
+        x = gram_ref[i % (modes // 2) : i % (modes // 2) + 8, :]
+        x = x if i < modes // 2 else pltpu.roll(x, modes, 1)
+        parts.append(jnp.where(lane < modes, x, jnp.where(lane == row + (i + modes), 1.0, 0.0)))
+    pivots = []
+    for k in range(0, modes, STEP):
+        g, r = k // 8, k % 8
+        steps = range(STEP)
+        rows = [parts[g][r + i : r + i + 1, :] for i in steps]
+        block = [[jnp.broadcast_to(x[:, k + i : k + i + 1], x.shape) for i in steps] for x in rows]
+        inverses = []
+        for i in steps:
+            inverses.append(1.0 / block[i][i])
+            for j in range(i + 1, STEP):
+                ratio = block[j][i] * inverses[i]
+                block[j] = [x - ratio * y for x, y in zip(block[j], block[i])]
+                rows[j] = rows[j] - ratio * rows[i]
+            pivots.append(block[i][i])
+        scaled = [x * inverse for x, inverse in zip(rows, inverses)]
+        for n in range(g, modes // 8):
+            part = parts[n]
+            columns = [jnp.broadcast_to(part[:, k + i : k + i + 1], part.shape) for i in steps]
             for i in steps:
-                inverses.append(1.0 / block[i][i])
                 for j in range(i + 1, STEP):
-                    ratio = block[j][i] * inverses[i]
-                    block[j] = [x - ratio * y for x, y in zip(block[j], block[i])]
-                    rows[j] = rows[j] - ratio * rows[i]
-                pivots.append(block[i][i])
-            scaled = [x * inverse for x, inverse in zip(rows, inverses)]
-            for n in range(g, modes // 8):
-                part = parts[n]
-                columns = [jnp.broadcast_to(part[:, k + i : k + i + 1], part.shape) for i in steps]
+                    columns[j] = columns[j] - columns[i] * (block[i][j] * inverses[i])
+            for i in steps:
+                column = jnp.where(row >= r + STEP, columns[i], 0.0) if n == g else columns[i]
+                part = part - column * scaled[i]
+            if n == g:
                 for i in steps:
-                    for j in range(i + 1, STEP):
-                        columns[j] = columns[j] - columns[i] * (block[i][j] * inverses[i])
-                for i in steps:
-                    column = jnp.where(row >= r + STEP, columns[i], 0.0) if n == g else columns[i]
-                    part = part - column * scaled[i]
-                if n == g:
-                    for i in steps:
-                        part = jnp.where(row == r + i, rows[i], part)
-                parts[n] = part
-        for i in range(modes // 8):
-            scale = 1.0 / jnp.sqrt(jnp.concatenate(pivots[i * 8 : (i + 1) * 8], axis=0))
-            part = parts[i] * scale
-            upper = jnp.where(lane >= row + i * 8, part / norm, 0.0)
-            factor_ref[i * 8 : (i + 1) * 8, :] = upper[:, :modes]
-            part = part * norm
-            inverse_ref[i * 8 : (i + 1) * 8, :] = jnp.where(lane < modes, pltpu.roll(part, modes, 1), part)
-        inverse = inverse_ref[...]
-        high, low = split2(inverse)
-        lhs_ref[:modes, :] = high
-        lhs_ref[modes:, :] = low
-
-    both = dot(lhs_ref[...], field_ref[0])
-    out_ref[0] = both[:modes] + both[modes:]
+                    part = jnp.where(row == r + i, rows[i], part)
+            parts[n] = part
+    for i in range(modes // 8):
+        scale = 1.0 / jnp.sqrt(jnp.concatenate(pivots[i * 8 : (i + 1) * 8], axis=0))
+        part = parts[i] * scale
+        upper = jnp.where(lane >= row + i * 8, part / norm, 0.0)
+        factor_ref[i * 8 : (i + 1) * 8, :] = upper[:, :modes]
+        part = part * norm
+        inverse_ref[i * 8 : (i + 1) * 8, :] = jnp.where(lane < modes, pltpu.roll(part, modes, 1), part)
+    lhs = jnp.concatenate(split2(inverse_ref[...]), axis=0)
+    copies = []
+    for v in range(VARS):
+        both = dot(lhs, field_ref[2 * v * modes : (2 * v + 2) * modes, :])
+        held_ref[v] = both[:modes] + both[modes:]
+        copies.append(pltpu.make_async_copy(held_ref.at[v], out_ref.at[v], done_ref.at[v]))
+        copies[-1].start()
+    for copy in copies:
+        copy.wait()
 
 
 def local(mode_shapes, wall_coupling, owner_dev, owner_cell, neighbours, coupling_blocks, inv_blocks):
@@ -430,7 +435,7 @@
         ]
         if last:
             two, gram = call(
-                functools.partial(outer_body, rim, last), (field_two, jax.ShapeDtypeStruct((modes, 2 * modes), F32)),
+                functools.partial(outer_body, rim, last), (field_two, jax.ShapeDtypeStruct((modes // 2, 2 * modes), F32)),
                 x, two, before, after, start, place, blocks, *middle,
                 scratch=windows + fetched, name="outer_last",
             )
@@ -439,7 +444,6 @@
                 functools.partial(outer_body, rim, last), (field, field_two, edge, edge),
                 x, two, before, after, start, place, blocks, *middle, scratch=windows + fetched, name="outer",
             )
-    field = two.reshape(VARS, 2 * modes, cells)
     reach = 1
     while reach < devices:
         gram = gram + lax.ppermute(gram, "slab", [(i, i ^ reach) for i in range(devices)])
@@ -448,17 +452,11 @@
     return call(
         functools.partial(basis_body, norm),
         (jax.ShapeDtypeStruct((VARS, modes, cells), F32), jax.ShapeDtypeStruct((modes, modes), F32)),
-        gram, field,
-        grid=(VARS,),
-        in_specs=[
-            pl.BlockSpec((modes, 2 * modes), lambda v: (0, 0)),
-            pl.BlockSpec((1, 2 * modes, cells), lambda v: (v, 0, 0)),
+        gram, two,
+        out_specs=(pl.BlockSpec(memory_space=pl.ANY), VMEM),
+        scratch=[
+            pltpu.VMEM((modes, 2 * modes), F32), pltpu.VMEM((VARS, modes, cells), F32), pltpu.SemaphoreType.DMA((VARS,))
         ],
-        out_specs=(
-            pl.BlockSpec((1, modes, cells), lambda v: (v, 0, 0)),
-            pl.BlockSpec((modes, modes), lambda v: (0, 0)),
-        ),
-        scratch=[pltpu.VMEM((2 * modes, 2 * modes), BF16), pltpu.VMEM((modes, 2 * modes), F32)],
         name="basis",
     )
 

time: 107 us -> 100 us (0.935)
  Pallas kernels: 51.4 us -> 45.4 us
    pallas_call x8, Pallas kernels: 51.4 us -> 45.4 us  [call(): pl.pallas_call(body, out_shape=out_shape, in_specs=kw.pop('in_specs', [VM...]
  transfers between devices with their start and end apart: 9 -> 9, of which waited for: 5 -> 5; matrix products, arithmetic and copies ran while one was open for 0% -> 0% of each run, Pallas kernels for 21% -> 22%
where the time goes in v3:
time: 100 us
  Pallas kernels  45.4 us (45%)
  starting transfers between devices  29.1 us (29%)
  waiting for transfers between devices  23.3 us (23%)
  local copies, waits for them, and re-layouts  1.43 us (1%)
    pallas_call x8, Pallas kernels, call(): pl.pallas_call(body, out_shape=out_shape, in_specs=kw.pop('in_specs', [VM...  45.4 us
    all_to_all x1, waiting for transfers between devices, local(): lax.all_to_all(packed, 'slab', split_axis=0, concat_axis=0, tiled=True)  17.3 us
    ppermute x4, starting transfers between devices, local(): lax.ppermute(gram, 'slab', [(i, i ^ reach) for i in range(devices)])  13.1 us
    all_to_all x1, starting transfers between devices, local(): lax.all_to_all(packed, 'slab', split_axis=0, concat_axis=0, tiled=True)  7.39 us
    ppermute x4, waiting for transfers between devices, local(): lax.ppermute(gram, 'slab', [(i, i ^ reach) for i in range(devices)])  5.99 us
    ppermute x2, starting transfers between devices, local(): before = lax.ppermute(final, 'slab', up)  5.85 us
    ppermute x2, starting transfers between devices, local(): after = lax.ppermute(first, 'slab', down)  2.76 us
  transfers between devices with their start and end apart: 9, of which 5 were waited for; matrix products, arithmetic and copies ran while one was open for 0% of the time, Pallas kernels for 22%

profile of v3, /device:TPU:0, one launch (start us, length us, event | category | flops | bytes accessed | tf_op | source)
XLA Modules:
  0.0 100.1 jit_solution(1773795192227976486)
XLA Ops:
  0.6 0.0 copy-start
  0.6 0.0 copy-start.2
  0.7 4.5 %pack.1 = f32[1664,128]{1,0:T(8,128)} custom-call(f32[192,512]{1,0:T(8,128)} %bitcast.11, f32[15,512]{1,0:T(8,128)} %bitcast.12, s32[1,512]{1,0:T(1,128)} %bitcast.13, s32[1,512]{1,0:T(1,128)} %bitcast.14), custom_call_target="tpu_custom_call" | custom-call | tf_op jit(solution)/shard_map/pack/pallas_call | solution.py:37
  5.2 7.4 %all-to-all-start = ((f32[16,104,128]{2,1,0:T(8,128)}), f32[16,104,128]{2,1,0:T(8,128)S(1)}, u32[]{:S(2)}, u32[]{:S(2)}) async-start(f32[16,104,128]{2,1,0:T(8,128)} %bitcast.10), calls=%async_computation | async-start | bytes 1703936 | tf_op jit(solution)/shard_map/all_to_all | solution.py:395
  12.6 0.0 copy-done
  12.6 0.0 copy-done.2
  12.6 0.0 copy-start.1
  12.6 1.4 %copy-done.1 = f32[6,5,5,2048]{3,0,2,1:T(8,128)S(1)} copy-done((f32[6,5,5,2048]{3,0,2,1:T(8,128)S(1)}, f32[6,5,5,2048]{3,0,2,1:T(8,128)}, u32[]{:S(2)}) %copy-start.1) | copy-done | bytes 1228824
  14.0 1.0 %prepare.1 = (f32[200,2048]{1,0:T(8,128)S(1)}, s32[8,2048]{1,0:T(8,128)S(1)}) custom-call(s32[1]{0:T(128)} %bitcast.6.first_ref, s32[6,2048]{1,0:T(8,128)S(1)} %copy-done.2, f32[5,5,6,2048]{3,2,1,0:T(8,128)S(1)} %bitcast.9, f32[5,5,2048]{2,1,0:T(8,128)S(1)} %copy-done), custom_call_target="tpu_custom_call" | custom-call | flops 1000000000 | bytes 10000000 | tf_op jit(solution)/shard_map/prepare/pallas_call | solution.py:37
  15.0 17.3 %all-to-all-done = f32[16,104,128]{2,1,0:T(8,128)S(1)} async-done(((f32[16,104,128]{2,1,0:T(8,128)}), f32[16,104,128]{2,1,0:T(8,128)S(1)}, u32[]{:S(2)}, u32[]{:S(2)}) %all-to-all-start) | async-done | bytes 852000 | tf_op jit(solution)/shard_map/all_to_all | solution.py:395
  32.3 5.3 %forcing.1 = (f32[5,64,2048]{2,1,0:T(8,128)S(1)}, bf16[640,2048]{1,0:T(8,128)(2,1)S(1)}, f32[5,64,256]{2,1,0:T(8,128)S(1)}, f32[5,64,256]{2,1,0:T(8,128)S(1)}) custom-call(f32[1664,128]{1,0:T(8,128)S(1)} %bitcast.8, f32[5,5,2048]{2,1,0:T(8,128)S(1)} %copy-done), custom_call_target="tpu_custom_call" | custom-call | tf_op jit(solution)/shard_map/forcing/pallas_call | solution.py:37
  37.7 2.3 %collective-permute-start = (f32[5,64,256]{2,1,0:T(8,128)S(1)}, f32[5,64,256]{2,1,0:T(8,128)S(1)}, u32[]{:S(2)}, u32[]{:S(2)}) collective-permute-start(f32[5,64,256]{2,1,0:T(8,128)S(1)} %get-tuple-element.18), channel_id=1, source_target_pairs={{0,1},{1,2},{2,3},{3,4},{4,5},{5,6},{6,7},{7,8},{8,9},{9,10},{10,1... | collective-permute-start | bytes 983048 | tf_op jit(solution)/shard_map/ppermute | solution.py:427
  39.9 1.3 %collective-permute-start.1 = (f32[5,64,256]{2,1,0:T(8,128)S(1)}, f32[5,64,256]{2,1,0:T(8,128)S(1)}, u32[]{:S(2)}, u32[]{:S(2)}) collective-permute-start(f32[5,64,256]{2,1,0:T(8,128)S(1)} %get-tuple-element.19), channel_id=1, source_target_pairs={{1,0},{2,1},{3,2},{4,3},{5,4},{6,5},{7,6},{8,7},{9,8},{10,9},{11,1... | collective-permute-start | bytes 983048 | tf_op jit(solution)/shard_map/ppermute | solution.py:428
  41.2 10.8 %inner.1 = (f32[5,64,1536]{2,1,0:T(8,128)S(1)}, bf16[640,1536]{1,0:T(8,128)(2,1)S(1)}) custom-call(f32[5,64,2048]{2,1,0:T(8,128)S(1)} %get-tuple-element.16.x_ref.start_ref, bf16[640,2048]{1,0:T(8,128)(2,1)S(1)} %get-tuple-element.17.two_ref, f32[5,64,2048]{2,1,0:T(8,128)S(1)} %get-tuple-element.16.x_ref.start_ref, ...), custom_call_target="tpu_custom_call" | custom-call | flops 10000000000 | bytes 30000000 | tf_op jit(solution)/shard_map/inner/pallas_call | solution.py:37
  52.0 0.0 collective-permute-done.before_ref
  52.0 0.0 collective-permute-done.1.after_ref
  52.0 4.1 %outer.1 = (f32[5,64,2048]{2,1,0:T(8,128)S(1)}, bf16[640,2048]{1,0:T(8,128)(2,1)S(1)}, f32[5,64,256]{2,1,0:T(8,128)S(1)}, f32[5,64,256]{2,1,0:T(8,128)S(1)}) custom-call(f32[5,64,2048]{2,1,0:T(8,128)S(1)} %get-tuple-element.16.x_ref.start_ref, bf16[640,2048]{1,0:T(8,128)(2,1)S(1)} %get-tuple-element.17.two_ref, ...), custom_call_target="tpu_custom_call" | custom-call | tf_op jit(solution)/shard_map/outer/pallas_call | solution.py:37
  56.2 3.6 %collective-permute-start.2 = (f32[5,64,256]{2,1,0:T(8,128)S(1)}, f32[5,64,256]{2,1,0:T(8,128)S(1)}, u32[]{:S(2)}, u32[]{:S(2)}) collective-permute-start(f32[5,64,256]{2,1,0:T(8,128)S(1)} %get-tuple-element.26), channel_id=1, source_target_pairs={{0,1},{1,2},{2,3},{3,4},{4,5},{5,6},{6,7},{7,8},{8,9},{9,10},{10,1... | collective-permute-start | bytes 983048 | tf_op jit(solution)/shard_map/ppermute | solution.py:427
  59.8 1.5 %collective-permute-start.3 = (f32[5,64,256]{2,1,0:T(8,128)S(1)}, f32[5,64,256]{2,1,0:T(8,128)S(1)}, u32[]{:S(2)}, u32[]{:S(2)}) collective-permute-start(f32[5,64,256]{2,1,0:T(8,128)S(1)} %get-tuple-element.27), channel_id=1, source_target_pairs={{1,0},{2,1},{3,2},{4,3},{5,4},{6,5},{7,6},{8,7},{9,8},{10,9},{11,1... | collective-permute-start | bytes 983048 | tf_op jit(solution)/shard_map/ppermute | solution.py:428
  61.2 10.7 %inner_last.1.refs_0_ = bf16[640,1536]{1,0:T(8,128)(2,1)S(1)} custom-call(f32[5,64,2048]{2,1,0:T(8,128)S(1)} %get-tuple-element.24.x_ref, bf16[640,2048]{1,0:T(8,128)(2,1)S(1)} %get-tuple-element.25.two_ref, f32[5,64,2048]{2,1,0:T(8,128)S(1)} %get-tuple-element.16.x_ref.start_ref, s32[8,2048]{1,0:T(8,128)S(1)} %get-tuple-element.20.place_ref, ...), custom_call_target="tpu_custom_call" | custom-call | flops 10000000000 | bytes 30000000 | tf_op jit(solution)/shard_map/inner_last/pallas_call | solution.py:37
  72.0 0.0 collective-permute-done.2.before_ref
  72.0 0.0 collective-permute-done.3.after_ref
  72.0 4.8 %outer_last.1 = (bf16[640,2048]{1,0:T(8,128)(2,1)S(1)}, f32[32,128]{1,0:T(8,128)S(1)}) custom-call(f32[5,64,2048]{2,1,0:T(8,128)S(1)} %get-tuple-element.24.x_ref, bf16[640,2048]{1,0:T(8,128)(2,1)S(1)} %get-tuple-element.25.two_ref, f32[5,64,256]{2,1,0:T(8,128)S(1)} %collective-permute-done.2.before_ref, f32[5,64,256]{2,1,0:T(8,128)S(1)} %collective-permute-done.3.after_ref, ...), custom_call_target="tpu_custom_call" | custom-call | tf_op jit(solution)/shard_map/outer_last/pallas_call | solution.py:37
  76.8 2.4 %collective-permute-start.4 = (f32[32,128]{1,0:T(8,128)S(1)}, f32[32,128]{1,0:T(8,128)S(1)}, u32[]{:S(2)}, u32[]{:S(2)}) collective-permute-start(f32[32,128]{1,0:T(8,128)S(1)} %get-tuple-element.28), channel_id=1, source_target_pairs={{0,1},{1,0},{2,3},{3,2},{4,5},{5,4},{6,7},{7,6},{8,9},{9,8},{10,11... | collective-permute-start | bytes 49160 | tf_op jit(solution)/shard_map/ppermute | solution.py:449
  79.2 0.8 collective-permute-done.4
  80.1 3.5 %collective-permute-start.5 = (f32[32,128]{1,0:T(8,128)S(1)}, f32[32,128]{1,0:T(8,128)S(1)}, u32[]{:S(2)}, u32[]{:S(2)}) collective-permute-start(f32[32,128]{1,0:T(8,128)S(1)} %add.12), channel_id=1, source_target_pairs={{0,2},{1,3},{2,0},{3,1},{4,6},{5,7},{6,4},{7,5},{8,10},{9,11},{10,... | collective-permute-start | bytes 49160 | tf_op jit(solution)/shard_map/ppermute | solution.py:449
  83.6 1.7 %collective-permute-done.5 = f32[32,128]{1,0:T(8,128)S(1)} collective-permute-done((f32[32,128]{1,0:T(8,128)S(1)}, f32[32,128]{1,0:T(8,128)S(1)}, u32[]{:S(2)}, u32[]{:S(2)}) %collective-permute-start.5) | collective-permute-done | bytes 16416 | tf_op jit(solution)/shard_map/ppermute | solution.py:449
  85.3 3.4 %collective-permute-start.6 = (f32[32,128]{1,0:T(8,128)S(1)}, f32[32,128]{1,0:T(8,128)S(1)}, u32[]{:S(2)}, u32[]{:S(2)}) collective-permute-start(f32[32,128]{1,0:T(8,128)S(1)} %add.13), channel_id=1, source_target_pairs={{0,4},{1,5},{2,6},{3,7},{4,0},{5,1},{6,2},{7,3},{8,12},{9,13},{10,... | collective-permute-start | bytes 49160 | tf_op jit(solution)/shard_map/ppermute | solution.py:449
  88.7 1.7 %collective-permute-done.6 = f32[32,128]{1,0:T(8,128)S(1)} collective-permute-done((f32[32,128]{1,0:T(8,128)S(1)}, f32[32,128]{1,0:T(8,128)S(1)}, u32[]{:S(2)}, u32[]{:S(2)}) %collective-permute-start.6) | collective-permute-done | bytes 16416 | tf_op jit(solution)/shard_map/ppermute | solution.py:449
  90.4 3.7 %collective-permute-start.7 = (f32[32,128]{1,0:T(8,128)S(1)}, f32[32,128]{1,0:T(8,128)S(1)}, u32[]{:S(2)}, u32[]{:S(2)}) collective-permute-start(f32[32,128]{1,0:T(8,128)S(1)} %add.14), channel_id=1, source_target_pairs={{0,8},{1,9},{2,10},{3,11},{4,12},{5,13},{6,14},{7,15},{8,0},{9,1},... | collective-permute-start | bytes 49160 | tf_op jit(solution)/shard_map/ppermute | solution.py:449
  94.2 1.7 %collective-permute-done.7 = f32[32,128]{1,0:T(8,128)S(1)} collective-permute-done((f32[32,128]{1,0:T(8,128)S(1)}, f32[32,128]{1,0:T(8,128)S(1)}, u32[]{:S(2)}, u32[]{:S(2)}) %collective-permute-start.7) | collective-permute-done | bytes 16416 | tf_op jit(solution)/shard_map/ppermute | solution.py:449
  95.9 4.1 %basis.1 = (f32[5,64,2048]{2,1,0:T(8,128)}, f32[64,64]{1,0:T(8,128)}) custom-call(f32[32,128]{1,0:T(8,128)S(1)} %add.15.gram_ref, bf16[640,2048]{1,0:T(8,128)(2,1)S(1)} %get-tuple-element.29.field_ref), custom_call_target="tpu_custom_call" | custom-call | tf_op jit(solution)/shard_map/basis/pallas_call | solution.py:37
  (4 shorter events, 0.0 us)
Async XLA Ops:
  0.6 11.9 %copy-start = (f32[5,5,2048]{2,1,0:T(8,128)S(1)}, f32[5,5,2048]{2,1,0:T(8,128)}, u32[]{:S(2)}) copy-start(f32[5,5,2048]{2,1,0:T(8,128)} %inv_ref.3) | copy-start | bytes 614404
  0.6 11.9 %copy-start.2 = (s32[6,2048]{1,0:T(8,128)S(1)}, s32[6,2048]{1,0:T(8,128)}, u32[]{:S(2)}) copy-start(s32[6,2048]{1,0:T(8,128)} %neighbours_ref.1) | copy-start | bytes 147460
  5.2 27.2 %all-to-all-start = ((f32[16,104,128]{2,1,0:T(8,128)}), f32[16,104,128]{2,1,0:T(8,128)S(1)}, u32[]{:S(2)}, u32[]{:S(2)}) async-start(f32[16,104,128]{2,1,0:T(8,128)} %bitcast.10), calls=%async_computation | async-start | bytes 1703936 | tf_op jit(solution)/shard_map/all_to_all | solution.py:395
  12.6 1.4 %copy-start.1 = (f32[6,5,5,2048]{3,0,2,1:T(8,128)S(1)}, f32[6,5,5,2048]{3,0,2,1:T(8,128)}, u32[]{:S(2)}) copy-start(f32[6,5,5,2048]{3,0,2,1:T(8,128)} %param.12) | copy-start | bytes 3686404
  37.7 14.4 %collective-permute-start = (f32[5,64,256]{2,1,0:T(8,128)S(1)}, f32[5,64,256]{2,1,0:T(8,128)S(1)}, u32[]{:S(2)}, u32[]{:S(2)}) collective-permute-start(f32[5,64,256]{2,1,0:T(8,128)S(1)} %get-tuple-element.18), channel_id=1, source_target_pairs={{0,1},{1,2},{2,3},{3,4},{4,5},{5,6},{6,7},{7,8},{8,9},{9,10},{10,1... | collective-permute-start | bytes 983048 | tf_op jit(solution)/shard_map/ppermute | solution.py:427
  39.9 12.1 %collective-permute-start.1 = (f32[5,64,256]{2,1,0:T(8,128)S(1)}, f32[5,64,256]{2,1,0:T(8,128)S(1)}, u32[]{:S(2)}, u32[]{:S(2)}) collective-permute-start(f32[5,64,256]{2,1,0:T(8,128)S(1)} %get-tuple-element.19), channel_id=1, source_target_pairs={{1,0},{2,1},{3,2},{4,3},{5,4},{6,5},{7,6},{8,7},{9,8},{10,9},{11,1... | collective-permute-start | bytes 983048 | tf_op jit(solution)/shard_map/ppermute | solution.py:428
  56.2 15.8 %collective-permute-start.2 = (f32[5,64,256]{2,1,0:T(8,128)S(1)}, f32[5,64,256]{2,1,0:T(8,128)S(1)}, u32[]{:S(2)}, u32[]{:S(2)}) collective-permute-start(f32[5,64,256]{2,1,0:T(8,128)S(1)} %get-tuple-element.26), channel_id=1, source_target_pairs={{0,1},{1,2},{2,3},{3,4},{4,5},{5,6},{6,7},{7,8},{8,9},{9,10},{10,1... | collective-permute-start | bytes 983048 | tf_op jit(solution)/shard_map/ppermute | solution.py:427
  59.8 12.2 %collective-permute-start.3 = (f32[5,64,256]{2,1,0:T(8,128)S(1)}, f32[5,64,256]{2,1,0:T(8,128)S(1)}, u32[]{:S(2)}, u32[]{:S(2)}) collective-permute-start(f32[5,64,256]{2,1,0:T(8,128)S(1)} %get-tuple-element.27), channel_id=1, source_target_pairs={{1,0},{2,1},{3,2},{4,3},{5,4},{6,5},{7,6},{8,7},{9,8},{10,9},{11,1... | collective-permute-start | bytes 983048 | tf_op jit(solution)/shard_map/ppermute | solution.py:428
  76.8 3.3 %collective-permute-start.4 = (f32[32,128]{1,0:T(8,128)S(1)}, f32[32,128]{1,0:T(8,128)S(1)}, u32[]{:S(2)}, u32[]{:S(2)}) collective-permute-start(f32[32,128]{1,0:T(8,128)S(1)} %get-tuple-element.28), channel_id=1, source_target_pairs={{0,1},{1,0},{2,3},{3,2},{4,5},{5,4},{6,7},{7,6},{8,9},{9,8},{10,11... | collective-permute-start | bytes 49160 | tf_op jit(solution)/shard_map/ppermute | solution.py:449
  80.1 5.2 %collective-permute-start.5 = (f32[32,128]{1,0:T(8,128)S(1)}, f32[32,128]{1,0:T(8,128)S(1)}, u32[]{:S(2)}, u32[]{:S(2)}) collective-permute-start(f32[32,128]{1,0:T(8,128)S(1)} %add.12), channel_id=1, source_target_pairs={{0,2},{1,3},{2,0},{3,1},{4,6},{5,7},{6,4},{7,5},{8,10},{9,11},{10,... | collective-permute-start | bytes 49160 | tf_op jit(solution)/shard_map/ppermute | solution.py:449
  85.3 5.1 %collective-permute-start.6 = (f32[32,128]{1,0:T(8,128)S(1)}, f32[32,128]{1,0:T(8,128)S(1)}, u32[]{:S(2)}, u32[]{:S(2)}) collective-permute-start(f32[32,128]{1,0:T(8,128)S(1)} %add.13), channel_id=1, source_target_pairs={{0,4},{1,5},{2,6},{3,7},{4,0},{5,1},{6,2},{7,3},{8,12},{9,13},{10,... | collective-permute-start | bytes 49160 | tf_op jit(solution)/shard_map/ppermute | solution.py:449
  90.4 5.5 %collective-permute-start.7 = (f32[32,128]{1,0:T(8,128)S(1)}, f32[32,128]{1,0:T(8,128)S(1)}, u32[]{:S(2)}, u32[]{:S(2)}) collective-permute-start(f32[32,128]{1,0:T(8,128)S(1)} %add.14), channel_id=1, source_target_pairs={{0,8},{1,9},{2,10},{3,11},{4,12},{5,13},{6,14},{7,15},{8,0},{9,1},... | collective-permute-start | bytes 49160 | tf_op jit(solution)/shard_map/ppermute | solution.py:449

commit v4 on v3

--- a/solution.py
+++ b/solution.py
@@ -11,8 +11,8 @@
 VARS = 5
 NBR = 6
 BY_LANES = 2
-ROWS = 16
-TOGETHER = 4
+ROWS = 32
+ORDER = (("F", 0), ("L", 0), ("F", 1), ("L", 1), ("D", 0), ("D", 1))
 LIMIT = 16
 MANY = 4
 STEP = 8
@@ -49,7 +49,7 @@
 def pack_body(cap, groups, rows, shapes_ref, weights_ref, dev_ref, cell_ref, out_ref, rows_ref, lhs_ref):
     width, nodes = shapes_ref.shape
     devices = out_ref.shape[0] // rows
-    rows16 = lhs_ref.shape[1] // 3
+    rows16 = lhs_ref.shape[1] // 2
     used = width + weights_ref.shape[0]
     rows_ref[used - used % 8 :, :] = jnp.zeros((rows_ref.shape[0] - used + used % 8, nodes), F32)
     rows_ref[:width, :] = shapes_ref[...]
@@ -57,12 +57,7 @@
     rows_ref[used : used + 1, :] = (cell_ref[...] + 1).astype(F32)
     for g in range(groups):
         x = rows_ref[g * rows : g * rows + rows16, :]
-        high = x.astype(BF16)
-        rest = x - high.astype(F32)
-        mid = rest.astype(BF16)
-        lhs_ref[g, :rows16, :] = high
-        lhs_ref[g, rows16 : 2 * rows16, :] = mid
-        lhs_ref[g, 2 * rows16 :, :] = (rest - mid.astype(F32)).astype(BF16)
+        lhs_ref[g, :rows16, :], lhs_ref[g, rows16:, :] = split2(x)
     dest = dev_ref[...]
     named = jnp.where(dest == lax.broadcasted_iota(I32, (devices, nodes), 0), 1.0, 0.0)
     earlier = jnp.where(
@@ -73,11 +68,11 @@
     slot = lax.broadcasted_iota(I32, (128 * MANY, nodes), 0)
 
     def several(step, _):
-        total = jnp.zeros((3 * rows16, 128 * MANY), F32)
+        total = jnp.zeros((2 * rows16, 128 * MANY), F32)
         for g in range(groups):
             hot = jnp.where(place + (g * cap - step * 128 * MANY) == slot, 1.0, 0.0).astype(BF16)
             total = total + lax.dot_general(lhs_ref[g], hot, (((1,), (1,)), ((), ())), preferred_element_type=F32)
-        total = total[:rows16] + total[rows16 : 2 * rows16] + total[2 * rows16 :]
+        total = total[:rows16] + total[rows16:]
         for h in range(MANY):
             at = pl.multiple_of((step * MANY + h) * rows, 8)
             out_ref[pl.ds(at, rows), :] = total[:rows, h * 128 : (h + 1) * 128]
@@ -128,98 +123,88 @@
     lane = lax.broadcasted_iota(I32, (slots, 128), 1) + 1
 
     def tile(t, _):
-        lo = pl.multiple_of(t * 512, 512)
-        hot = [jnp.where(tag_ref[...] == (lane + (lo + h * 128)).astype(F32), 1.0, 0.0).astype(BF16) for h in range(4)]
+        lo = pl.multiple_of(t * 1024, 1024)
+        hot = [jnp.where(tag_ref[...] == (lane + (lo + h * 128)).astype(F32), 1.0, 0.0).astype(BF16) for h in range(8)]
         both = dot(lhs_ref[...], jnp.concatenate(hot, axis=1))
         forcing = [both[u * 2 * modes : u * 2 * modes + modes] + both[u * 2 * modes + modes : (u + 1) * 2 * modes] for u in range(VARS)]
         for v in range(VARS):
-            total = inv_ref[v, 0:1, pl.ds(lo, 512)] * forcing[0]
+            total = inv_ref[v, 0:1, pl.ds(lo, 1024)] * forcing[0]
             for u in range(1, VARS):
-                total = total + inv_ref[v, u : u + 1, pl.ds(lo, 512)] * forcing[u]
-            out_ref[v, :, pl.ds(lo, 512)] = total
+                total = total + inv_ref[v, u : u + 1, pl.ds(lo, 1024)] * forcing[u]
+            out_ref[v, :, pl.ds(lo, 1024)] = total
             high, low = split2(total)
-            two_ref[2 * v * modes : (2 * v + 1) * modes, pl.ds(lo, 512)] = high
-            two_ref[(2 * v + 1) * modes : (2 * v + 2) * modes, pl.ds(lo, 512)] = low
+            two_ref[2 * v * modes : (2 * v + 1) * modes, pl.ds(lo, 1024)] = high
+            two_ref[(2 * v + 1) * modes : (2 * v + 2) * modes, pl.ds(lo, 1024)] = low
         return 0
 
-    lax.fori_loop(0, cells // 512, tile, 0)
+    lax.fori_loop(0, cells // 1024, tile, 0)
     first_ref[...] = out_ref[:, :, :rim]
     last_ref[...] = out_ref[:, :, cells - rim :]
 
 
-def fetch(out_ref, windows, place_ref, lo):
-    def step(slots):
-        total, at = None, 0
-        for two, start, width in windows:
-            row = lax.broadcasted_iota(I32, (width, 256), 0) + at
-            hot = [jnp.where(row == place_ref[j : j + 1, pl.ds(lo, 256)], 1.0, 0.0).astype(BF16) for j in slots]
-            part = dot(two[:, pl.ds(start, width)], jnp.concatenate(hot, axis=1))
-            total = part if total is None else total + part
-            at += width
-        out_ref[:, slots[0] * 256 : (slots[-1] + 1) * 256] = total
-
-    slots = list(range(NBR - BY_LANES))
-    return [functools.partial(step, slots[j : j + TOGETHER]) for j in range(0, len(slots), TOGETHER)]
-
-
-def relax(fetched_ref, source, start_ref, place_ref, blocks_ref, lo, store):
+def relax(fetched_ref, part_ref, two, source, start_ref, place_ref, blocks_ref, lo, store):
     modes = start_ref.shape[1]
     by_matmul = NBR - BY_LANES
     rows = range(0, ROWS, 8)
-
-    def step(m, h):
+    two_ref, first = two
+
+    def subtract(acc, at, j, u, values):
+        for v in range(VARS):
+            row = (v * VARS + u) * 8 + j
+            block = blocks_ref[row : row + 1, pl.ds(at, 128)]
+            acc[v] = [a - block * value for a, value in zip(acc[v], values)]
+
+    def fetch(h):
         at = pl.multiple_of(lo + h * 128, 128)
-        acc = [[start_ref[v, m + i : m + i + 8, pl.ds(at, 128)] for i in rows] for v in range(VARS)]
-
-        def subtract(j, u, values):
-            for v in range(VARS):
-                row = (v * VARS + u) * 8 + j
-                block = blocks_ref[row : row + 1, pl.ds(at, 128)]
-                acc[v] = [a - block * value for a, value in zip(acc[v], values)]
-
-        lanes, wheres = [], []
+        row = lax.broadcasted_iota(I32, (640, 128), 0) + h * 128
+        hot = [jnp.where(row == place_ref[j : j + 1, pl.ds(at, 128)], 1.0, 0.0).astype(BF16) for j in range(by_matmul)]
+        window = pl.ds(pl.multiple_of(first + h * 128, 128), 640)
+        fetched_ref[:, h * by_matmul * 128 : (h + 1) * by_matmul * 128] = dot(two_ref[:, window], jnp.concatenate(hot, axis=1))
+
+    def lanes(h):
+        at = pl.multiple_of(lo + h * 128, 128)
+        picks = []
         for j in range(by_matmul, NBR):
             place = jnp.broadcast_to(place_ref[j : j + 1, pl.ds(at, 128)] - h * 128, (8, 128))
-            lanes.append(place & 127)
-            wheres.append(place >> 7)
-        def by_lanes(u):
-            around = [[source(u, m + i, h + s) for s in range(5)] for i in rows]
-            taken = [
-                [[jnp.take_along_axis(x, lane, axis=1, mode="promise_in_bounds") for x in blocks] for blocks in around]
-                for lane in lanes
-            ]
-            for n, where in enumerate(wheres):
-                values = []
-                for x in taken[n]:
-                    value = x[0]
-                    for s in range(1, 5):
-                        value = jnp.where(where == s, x[s], value)
-                    values.append(value)
-                subtract(by_matmul + n, u, values)
-
-        def by_dots(u):
-            for j in range(by_matmul):
-                values = []
-                for i in rows:
-                    r, c = u * 2 * modes + m + i, j * 256 + h * 128
-                    values.append(
-                        fetched_ref[r : r + 8, c : c + 128] + fetched_ref[r + modes : r + modes + 8, c : c + 128]
-                    )
-                subtract(j, u, values)
-
-        for u in range(VARS):
-            by_lanes(u)
-        for u in range(VARS):
-            by_dots(u)
-        for v in range(VARS):
-            store(v, m, h, jnp.concatenate(acc[v], axis=0))
-
-    return [functools.partial(step, m, h) for m in range(0, modes, ROWS) for h in range(2)]
-
-
-def run(steps):
-    for step in steps:
-        step()
+            picks.append((j, place & 127, place >> 7))
+        for m in range(0, modes, ROWS):
+            acc = [[start_ref[v, m + i : m + i + 8, pl.ds(at, 128)] for i in rows] for v in range(VARS)]
+            for u in range(VARS):
+                around = [[source(u, m + i, h + s) for s in range(5)] for i in rows]
+                taken = [
+                    [[jnp.take_along_axis(x, lane, axis=1, mode="promise_in_bounds") for x in blocks] for blocks in around]
+                    for _, lane, _ in picks
+                ]
+                for (j, _, where), found in zip(picks, taken):
+                    values = []
+                    for x in found:
+                        value = x[0]
+                        for s in range(1, 5):
+                            value = jnp.where(where == s, x[s], value)
+                        values.append(value)
+                    subtract(acc, at, j, u, values)
+            for v in range(VARS):
+                for n, i in enumerate(rows):
+                    part_ref[h, v, m + i : m + i + 8, :] = acc[v][n]
+
+    def dots(h):
+        at = pl.multiple_of(lo + h * 128, 128)
+        for m in range(0, modes, ROWS):
+            acc = [[part_ref[h, v, m + i : m + i + 8, :] for i in rows] for v in range(VARS)]
+            for u in range(VARS):
+                for j in range(by_matmul):
+                    values = []
+                    for i in rows:
+                        r, c = u * 2 * modes + m + i, (h * by_matmul + j) * 128
+                        values.append(
+                            fetched_ref[r : r + 8, c : c + 128] + fetched_ref[r + modes : r + modes + 8, c : c + 128]
+                        )
+                    subtract(acc, at, j, u, values)
+            for v in range(VARS):
+                store(v, m, h, jnp.concatenate(acc[v], axis=0))
+
+    for step, h in ORDER:
+        {"F": fetch, "L": lanes, "D": dots}[step](h)
 
 
 def put_two(two_ref, modes, v, m, at, high, low):
@@ -230,17 +215,13 @@
 
 def inner_body(rim, last, x_ref, two_ref, start_ref, place_ref, blocks_ref, *refs):
     if last:
-        mid_two_ref, fetched_ref = refs
+        mid_two_ref, fetched_ref, part_ref = refs
     else:
-        mid_ref, mid_two_ref, fetched_ref = refs
+        mid_ref, mid_two_ref, fetched_ref, part_ref = refs
     modes, cells = x_ref.shape[1:]
     tiles = (cells - 2 * rim) // 256
 
-    def load(t, ref):
-        lo = pl.multiple_of(rim + t * 256, 256)
-        return fetch(ref, [(two_ref, pl.multiple_of(lo - rim, 256), 256 + 2 * rim)], place_ref, lo)
-
-    def work(t, ref):
+    def one_tile(t, _):
         lo = pl.multiple_of(rim + t * 256, 256)
 
         def store(v, m, h, value):
@@ -252,10 +233,8 @@
         def source(u, m, s):
             return x_ref[u, m : m + 8, pl.ds(pl.multiple_of(lo - rim + s * 128, 128), 128)]
 
-        return relax(ref, source, start_ref, place_ref, blocks_ref, lo, store)
-
-    def one_tile(t, _):
-        run(load(t, fetched_ref) + work(t, fetched_ref))
+        two = (two_ref, pl.multiple_of(lo - rim, 256))
+        relax(fetched_ref, part_ref, two, source, start_ref, place_ref, blocks_ref, lo, store)
         return 0
 
     lax.fori_loop(0, tiles, one_tile, 0)
@@ -263,9 +242,9 @@
 
 def outer_body(rim, last, x_ref, two_ref, before_ref, after_ref, start_ref, place_ref, blocks_ref, *refs):
     if last:
-        mid_two_ref, out_two_ref, gram_ref, window_ref, window_two_ref, fetched_ref = refs
+        mid_two_ref, out_two_ref, gram_ref, window_ref, window_two_ref, fetched_ref, part_ref = refs
     else:
-        mid_ref, mid_two_ref, out_ref, out_two_ref, first_ref, last_ref, window_ref, window_two_ref, fetched_ref = refs
+        mid_ref, mid_two_ref, out_ref, out_two_ref, first_ref, last_ref, window_ref, window_two_ref, fetched_ref, part_ref = refs
     modes, cells = x_ref.shape[1:]
     ends = cells - rim
     near = 256 + rim
@@ -296,10 +275,8 @@
                 out_ref[v, m : m + ROWS, at] = value
             put_two(out_two_ref, modes, v, m, at, *split2(value))
 
-        run(
-            fetch(fetched_ref, [(window_two_ref.at[t], 0, near + rim)], place_ref, lo)
-            + relax(fetched_ref, source, start_ref, place_ref, blocks_ref, lo, store)
-        )
+        two = (window_two_ref.at[t], 0)
+        relax(fetched_ref, part_ref, two, source, start_ref, place_ref, blocks_ref, lo, store)
         return 0
 
     lax.fori_loop(0, 2, one_side, 0)
@@ -389,7 +366,7 @@
         grid=(1,),
         in_specs=[pl.BlockSpec((n, nodes), lambda i: (0, 0)) for n in (3 * modes, 3 * VARS, 1, 1)],
         out_specs=pl.BlockSpec((devices * rows, 128), lambda i: (0, 0)),
-        scratch=[pltpu.VMEM(((groups - 1) * rows + rows16, nodes), F32), pltpu.VMEM((groups, 3 * rows16, nodes), BF16)],
+        scratch=[pltpu.VMEM(((groups - 1) * rows + rows16, nodes), F32), pltpu.VMEM((groups, 2 * rows16, nodes), BF16)],
         name="pack", limit=60,
     )
     arrived = lax.all_to_all(packed, "slab", split_axis=0, concat_axis=0, tiled=True)
@@ -421,7 +398,9 @@
     inner = cells - 2 * rim
     mid = jax.ShapeDtypeStruct((VARS, modes, inner), F32)
     mid_two = jax.ShapeDtypeStruct((VARS * 2 * modes, inner), BF16)
-    fetched = [pltpu.VMEM((VARS * 2 * modes, (NBR - BY_LANES) * 256), F32)]
+    fetched = [
+        pltpu.VMEM((VARS * 2 * modes, (NBR - BY_LANES) * 256), F32), pltpu.VMEM((2, VARS, modes, 128), F32)
+    ]
     cost = pl.CostEstimate(flops=10**10, bytes_accessed=3 * 10**7, transcendentals=0)
     for last in (False, True):
         before = lax.ppermute(final, "slab", up)

time: 100 us -> 98.8 us (0.988)
  Pallas kernels: 45.4 us -> 43.7 us
    pallas_call x8, Pallas kernels: 45.4 us -> 43.7 us  [call(): pl.pallas_call(body, out_shape=out_shape, in_specs=kw.pop('in_specs', [VM...]
where the time goes in v4:
time: 98.8 us; the launch traced here: 98.5 us
  Pallas kernels  43.7 us (44%)
  starting transfers between devices  29.1 us (29%)
  waiting for transfers between devices  23.3 us (24%)
  local copies, waits for them, and re-layouts  1.43 us (1%)
    pallas_call x8, Pallas kernels, call(): pl.pallas_call(body, out_shape=out_shape, in_specs=kw.pop('in_specs', [VM...  43.7 us
    all_to_all x1, waiting for transfers between devices, local(): lax.all_to_all(packed, 'slab', split_axis=0, concat_axis=0, tiled=True)  17.3 us
    ppermute x4, starting transfers between devices, local(): lax.ppermute(gram, 'slab', [(i, i ^ reach) for i in range(devices)])  13.1 us
    all_to_all x1, starting transfers between devices, local(): lax.all_to_all(packed, 'slab', split_axis=0, concat_axis=0, tiled=True)  7.38 us
    ppermute x4, waiting for transfers between devices, local(): lax.ppermute(gram, 'slab', [(i, i ^ reach) for i in range(devices)])  5.99 us
    ppermute x2, starting transfers between devices, local(): before = lax.ppermute(final, 'slab', up)  5.85 us
    ppermute x2, starting transfers between devices, local(): after = lax.ppermute(first, 'slab', down)  2.76 us
  transfers between devices with their start and end apart: 9, of which 5 were waited for; matrix products, arithmetic and copies ran while one was open for 0% of the time, Pallas kernels for 22%

profile of v4, /device:TPU:0, one launch (start us, length us, event | category | flops | bytes accessed | tf_op | source)
XLA Modules:
  0.0 98.5 jit_solution(9299886304882628849)
XLA Ops:
  0.6 0.0 copy-start
  0.6 0.0 copy-start.2
  0.7 4.2 %pack.1 = f32[1664,128]{1,0:T(8,128)} custom-call(f32[192,512]{1,0:T(8,128)} %bitcast.11, f32[15,512]{1,0:T(8,128)} %bitcast.12, s32[1,512]{1,0:T(1,128)} %bitcast.13, s32[1,512]{1,0:T(1,128)} %bitcast.14), custom_call_target="tpu_custom_call" | custom-call | tf_op jit(solution)/shard_map/pack/pallas_call | solution.py:37
  4.8 7.4 %all-to-all-start = ((f32[16,104,128]{2,1,0:T(8,128)}), f32[16,104,128]{2,1,0:T(8,128)S(1)}, u32[]{:S(2)}, u32[]{:S(2)}) async-start(f32[16,104,128]{2,1,0:T(8,128)} %bitcast.10), calls=%async_computation | async-start | bytes 1703936 | tf_op jit(solution)/shard_map/all_to_all | solution.py:372
  12.2 0.0 copy-done
  12.2 0.0 copy-done.2
  12.2 0.0 copy-start.1
  12.3 1.4 %copy-done.1 = f32[6,5,5,2048]{3,0,2,1:T(8,128)S(1)} copy-done((f32[6,5,5,2048]{3,0,2,1:T(8,128)S(1)}, f32[6,5,5,2048]{3,0,2,1:T(8,128)}, u32[]{:S(2)}) %copy-start.1) | copy-done | bytes 1228824
  13.7 1.0 %prepare.1 = (f32[200,2048]{1,0:T(8,128)S(1)}, s32[8,2048]{1,0:T(8,128)S(1)}) custom-call(s32[1]{0:T(128)} %bitcast.6.first_ref, s32[6,2048]{1,0:T(8,128)S(1)} %copy-done.2, f32[5,5,6,2048]{3,2,1,0:T(8,128)S(1)} %bitcast.9, f32[5,5,2048]{2,1,0:T(8,128)S(1)} %copy-done), custom_call_target="tpu_custom_call" | custom-call | flops 1000000000 | bytes 10000000 | tf_op jit(solution)/shard_map/prepare/pallas_call | solution.py:37
  14.7 17.3 %all-to-all-done = f32[16,104,128]{2,1,0:T(8,128)S(1)} async-done(((f32[16,104,128]{2,1,0:T(8,128)}), f32[16,104,128]{2,1,0:T(8,128)S(1)}, u32[]{:S(2)}, u32[]{:S(2)}) %all-to-all-start) | async-done | bytes 852000 | tf_op jit(solution)/shard_map/all_to_all | solution.py:372
  32.0 5.0 %forcing.1 = (f32[5,64,2048]{2,1,0:T(8,128)S(1)}, bf16[640,2048]{1,0:T(8,128)(2,1)S(1)}, f32[5,64,256]{2,1,0:T(8,128)S(1)}, f32[5,64,256]{2,1,0:T(8,128)S(1)}) custom-call(f32[1664,128]{1,0:T(8,128)S(1)} %bitcast.8, f32[5,5,2048]{2,1,0:T(8,128)S(1)} %copy-done), custom_call_target="tpu_custom_call" | custom-call | tf_op jit(solution)/shard_map/forcing/pallas_call | solution.py:37
  37.0 2.3 %collective-permute-start = (f32[5,64,256]{2,1,0:T(8,128)S(1)}, f32[5,64,256]{2,1,0:T(8,128)S(1)}, u32[]{:S(2)}, u32[]{:S(2)}) collective-permute-start(f32[5,64,256]{2,1,0:T(8,128)S(1)} %get-tuple-element.18), channel_id=1, source_target_pairs={{0,1},{1,2},{2,3},{3,4},{4,5},{5,6},{6,7},{7,8},{8,9},{9,10},{10,1... | collective-permute-start | bytes 983048 | tf_op jit(solution)/shard_map/ppermute | solution.py:406
  39.3 1.3 %collective-permute-start.1 = (f32[5,64,256]{2,1,0:T(8,128)S(1)}, f32[5,64,256]{2,1,0:T(8,128)S(1)}, u32[]{:S(2)}, u32[]{:S(2)}) collective-permute-start(f32[5,64,256]{2,1,0:T(8,128)S(1)} %get-tuple-element.19), channel_id=1, source_target_pairs={{1,0},{2,1},{3,2},{4,3},{5,4},{6,5},{7,6},{8,7},{9,8},{10,9},{11,1... | collective-permute-start | bytes 983048 | tf_op jit(solution)/shard_map/ppermute | solution.py:407
  40.6 10.5 %inner.1 = (f32[5,64,1536]{2,1,0:T(8,128)S(1)}, bf16[640,1536]{1,0:T(8,128)(2,1)S(1)}) custom-call(f32[5,64,2048]{2,1,0:T(8,128)S(1)} %get-tuple-element.16.x_ref.start_ref, bf16[640,2048]{1,0:T(8,128)(2,1)S(1)} %get-tuple-element.17.two_ref, f32[5,64,2048]{2,1,0:T(8,128)S(1)} %get-tuple-element.16.x_ref.start_ref, ...), custom_call_target="tpu_custom_call" | custom-call | flops 10000000000 | bytes 30000000 | tf_op jit(solution)/shard_map/inner/pallas_call | solution.py:37
  51.1 0.0 collective-permute-done.before_ref
  51.1 0.0 collective-permute-done.1.after_ref
  51.1 3.9 %outer.1 = (f32[5,64,2048]{2,1,0:T(8,128)S(1)}, bf16[640,2048]{1,0:T(8,128)(2,1)S(1)}, f32[5,64,256]{2,1,0:T(8,128)S(1)}, f32[5,64,256]{2,1,0:T(8,128)S(1)}) custom-call(f32[5,64,2048]{2,1,0:T(8,128)S(1)} %get-tuple-element.16.x_ref.start_ref, bf16[640,2048]{1,0:T(8,128)(2,1)S(1)} %get-tuple-element.17.two_ref, ...), custom_call_target="tpu_custom_call" | custom-call | tf_op jit(solution)/shard_map/outer/pallas_call | solution.py:37
  55.0 3.6 %collective-permute-start.2 = (f32[5,64,256]{2,1,0:T(8,128)S(1)}, f32[5,64,256]{2,1,0:T(8,128)S(1)}, u32[]{:S(2)}, u32[]{:S(2)}) collective-permute-start(f32[5,64,256]{2,1,0:T(8,128)S(1)} %get-tuple-element.26), channel_id=1, source_target_pairs={{0,1},{1,2},{2,3},{3,4},{4,5},{5,6},{6,7},{7,8},{8,9},{9,10},{10,1... | collective-permute-start | bytes 983048 | tf_op jit(solution)/shard_map/ppermute | solution.py:406
  58.6 1.5 %collective-permute-start.3 = (f32[5,64,256]{2,1,0:T(8,128)S(1)}, f32[5,64,256]{2,1,0:T(8,128)S(1)}, u32[]{:S(2)}, u32[]{:S(2)}) collective-permute-start(f32[5,64,256]{2,1,0:T(8,128)S(1)} %get-tuple-element.27), channel_id=1, source_target_pairs={{1,0},{2,1},{3,2},{4,3},{5,4},{6,5},{7,6},{8,7},{9,8},{10,9},{11,1... | collective-permute-start | bytes 983048 | tf_op jit(solution)/shard_map/ppermute | solution.py:407
  60.1 10.4 %inner_last.1.refs_0_ = bf16[640,1536]{1,0:T(8,128)(2,1)S(1)} custom-call(f32[5,64,2048]{2,1,0:T(8,128)S(1)} %get-tuple-element.24.x_ref, bf16[640,2048]{1,0:T(8,128)(2,1)S(1)} %get-tuple-element.25.two_ref, f32[5,64,2048]{2,1,0:T(8,128)S(1)} %get-tuple-element.16.x_ref.start_ref, s32[8,2048]{1,0:T(8,128)S(1)} %get-tuple-element.20.place_ref, ...), custom_call_target="tpu_custom_call" | custom-call | flops 10000000000 | bytes 30000000 | tf_op jit(solution)/shard_map/inner_last/pallas_call | solution.py:37
  70.5 0.0 collective-permute-done.2.before_ref
  70.5 0.0 collective-permute-done.3.after_ref
  70.5 4.6 %outer_last.1 = (bf16[640,2048]{1,0:T(8,128)(2,1)S(1)}, f32[32,128]{1,0:T(8,128)S(1)}) custom-call(f32[5,64,2048]{2,1,0:T(8,128)S(1)} %get-tuple-element.24.x_ref, bf16[640,2048]{1,0:T(8,128)(2,1)S(1)} %get-tuple-element.25.two_ref, f32[5,64,256]{2,1,0:T(8,128)S(1)} %collective-permute-done.2.before_ref, f32[5,64,256]{2,1,0:T(8,128)S(1)} %collective-permute-done.3.after_ref, ...), custom_call_target="tpu_custom_call" | custom-call | tf_op jit(solution)/shard_map/outer_last/pallas_call | solution.py:37
  75.2 2.4 %collective-permute-start.4 = (f32[32,128]{1,0:T(8,128)S(1)}, f32[32,128]{1,0:T(8,128)S(1)}, u32[]{:S(2)}, u32[]{:S(2)}) collective-permute-start(f32[32,128]{1,0:T(8,128)S(1)} %get-tuple-element.28), channel_id=1, source_target_pairs={{0,1},{1,0},{2,3},{3,2},{4,5},{5,4},{6,7},{7,6},{8,9},{9,8},{10,11... | collective-permute-start | bytes 49160 | tf_op jit(solution)/shard_map/ppermute | solution.py:428
  77.6 0.8 collective-permute-done.4
  78.4 3.5 %collective-permute-start.5 = (f32[32,128]{1,0:T(8,128)S(1)}, f32[32,128]{1,0:T(8,128)S(1)}, u32[]{:S(2)}, u32[]{:S(2)}) collective-permute-start(f32[32,128]{1,0:T(8,128)S(1)} %add.12), channel_id=1, source_target_pairs={{0,2},{1,3},{2,0},{3,1},{4,6},{5,7},{6,4},{7,5},{8,10},{9,11},{10,... | collective-permute-start | bytes 49160 | tf_op jit(solution)/shard_map/ppermute | solution.py:428
  81.9 1.7 %collective-permute-done.5 = f32[32,128]{1,0:T(8,128)S(1)} collective-permute-done((f32[32,128]{1,0:T(8,128)S(1)}, f32[32,128]{1,0:T(8,128)S(1)}, u32[]{:S(2)}, u32[]{:S(2)}) %collective-permute-start.5) | collective-permute-done | bytes 16416 | tf_op jit(solution)/shard_map/ppermute | solution.py:428
  83.7 3.4 %collective-permute-start.6 = (f32[32,128]{1,0:T(8,128)S(1)}, f32[32,128]{1,0:T(8,128)S(1)}, u32[]{:S(2)}, u32[]{:S(2)}) collective-permute-start(f32[32,128]{1,0:T(8,128)S(1)} %add.13), channel_id=1, source_target_pairs={{0,4},{1,5},{2,6},{3,7},{4,0},{5,1},{6,2},{7,3},{8,12},{9,13},{10,... | collective-permute-start | bytes 49160 | tf_op jit(solution)/shard_map/ppermute | solution.py:428
  87.1 1.7 %collective-permute-done.6 = f32[32,128]{1,0:T(8,128)S(1)} collective-permute-done((f32[32,128]{1,0:T(8,128)S(1)}, f32[32,128]{1,0:T(8,128)S(1)}, u32[]{:S(2)}, u32[]{:S(2)}) %collective-permute-start.6) | collective-permute-done | bytes 16416 | tf_op jit(solution)/shard_map/ppermute | solution.py:428
  88.8 3.7 %collective-permute-start.7 = (f32[32,128]{1,0:T(8,128)S(1)}, f32[32,128]{1,0:T(8,128)S(1)}, u32[]{:S(2)}, u32[]{:S(2)}) collective-permute-start(f32[32,128]{1,0:T(8,128)S(1)} %add.14), channel_id=1, source_target_pairs={{0,8},{1,9},{2,10},{3,11},{4,12},{5,13},{6,14},{7,15},{8,0},{9,1},... | collective-permute-start | bytes 49160 | tf_op jit(solution)/shard_map/ppermute | solution.py:428
  92.5 1.7 %collective-permute-done.7 = f32[32,128]{1,0:T(8,128)S(1)} collective-permute-done((f32[32,128]{1,0:T(8,128)S(1)}, f32[32,128]{1,0:T(8,128)S(1)}, u32[]{:S(2)}, u32[]{:S(2)}) %collective-permute-start.7) | collective-permute-done | bytes 16416 | tf_op jit(solution)/shard_map/ppermute | solution.py:428
  94.3 4.1 %basis.1 = (f32[5,64,2048]{2,1,0:T(8,128)}, f32[64,64]{1,0:T(8,128)}) custom-call(f32[32,128]{1,0:T(8,128)S(1)} %add.15.gram_ref, bf16[640,2048]{1,0:T(8,128)(2,1)S(1)} %get-tuple-element.29.field_ref), custom_call_target="tpu_custom_call" | custom-call | tf_op jit(solution)/shard_map/basis/pallas_call | solution.py:37
  (4 shorter events, 0.0 us)
Async XLA Ops:
  0.6 11.6 %copy-start = (f32[5,5,2048]{2,1,0:T(8,128)S(1)}, f32[5,5,2048]{2,1,0:T(8,128)}, u32[]{:S(2)}) copy-start(f32[5,5,2048]{2,1,0:T(8,128)} %inv_ref.3) | copy-start | bytes 614404
  0.6 11.6 %copy-start.2 = (s32[6,2048]{1,0:T(8,128)S(1)}, s32[6,2048]{1,0:T(8,128)}, u32[]{:S(2)}) copy-start(s32[6,2048]{1,0:T(8,128)} %neighbours_ref.1) | copy-start | bytes 147460
  4.8 27.1 %all-to-all-start = ((f32[16,104,128]{2,1,0:T(8,128)}), f32[16,104,128]{2,1,0:T(8,128)S(1)}, u32[]{:S(2)}, u32[]{:S(2)}) async-start(f32[16,104,128]{2,1,0:T(8,128)} %bitcast.10), calls=%async_computation | async-start | bytes 1703936 | tf_op jit(solution)/shard_map/all_to_all | solution.py:372
  12.2 1.4 %copy-start.1 = (f32[6,5,5,2048]{3,0,2,1:T(8,128)S(1)}, f32[6,5,5,2048]{3,0,2,1:T(8,128)}, u32[]{:S(2)}) copy-start(f32[6,5,5,2048]{3,0,2,1:T(8,128)} %param.12) | copy-start | bytes 3686404
  37.0 14.1 %collective-permute-start = (f32[5,64,256]{2,1,0:T(8,128)S(1)}, f32[5,64,256]{2,1,0:T(8,128)S(1)}, u32[]{:S(2)}, u32[]{:S(2)}) collective-permute-start(f32[5,64,256]{2,1,0:T(8,128)S(1)} %get-tuple-element.18), channel_id=1, source_target_pairs={{0,1},{1,2},{2,3},{3,4},{4,5},{5,6},{6,7},{7,8},{8,9},{9,10},{10,1... | collective-permute-start | bytes 983048 | tf_op jit(solution)/shard_map/ppermute | solution.py:406
  39.3 11.8 %collective-permute-start.1 = (f32[5,64,256]{2,1,0:T(8,128)S(1)}, f32[5,64,256]{2,1,0:T(8,128)S(1)}, u32[]{:S(2)}, u32[]{:S(2)}) collective-permute-start(f32[5,64,256]{2,1,0:T(8,128)S(1)} %get-tuple-element.19), channel_id=1, source_target_pairs={{1,0},{2,1},{3,2},{4,3},{5,4},{6,5},{7,6},{8,7},{9,8},{10,9},{11,1... | collective-permute-start | bytes 983048 | tf_op jit(solution)/shard_map/ppermute | solution.py:407
  55.0 15.5 %collective-permute-start.2 = (f32[5,64,256]{2,1,0:T(8,128)S(1)}, f32[5,64,256]{2,1,0:T(8,128)S(1)}, u32[]{:S(2)}, u32[]{:S(2)}) collective-permute-start(f32[5,64,256]{2,1,0:T(8,128)S(1)} %get-tuple-element.26), channel_id=1, source_target_pairs={{0,1},{1,2},{2,3},{3,4},{4,5},{5,6},{6,7},{7,8},{8,9},{9,10},{10,1... | collective-permute-start | bytes 983048 | tf_op jit(solution)/shard_map/ppermute | solution.py:406
  58.6 11.9 %collective-permute-start.3 = (f32[5,64,256]{2,1,0:T(8,128)S(1)}, f32[5,64,256]{2,1,0:T(8,128)S(1)}, u32[]{:S(2)}, u32[]{:S(2)}) collective-permute-start(f32[5,64,256]{2,1,0:T(8,128)S(1)} %get-tuple-element.27), channel_id=1, source_target_pairs={{1,0},{2,1},{3,2},{4,3},{5,4},{6,5},{7,6},{8,7},{9,8},{10,9},{11,1... | collective-permute-start | bytes 983048 | tf_op jit(solution)/shard_map/ppermute | solution.py:407
  75.2 3.3 %collective-permute-start.4 = (f32[32,128]{1,0:T(8,128)S(1)}, f32[32,128]{1,0:T(8,128)S(1)}, u32[]{:S(2)}, u32[]{:S(2)}) collective-permute-start(f32[32,128]{1,0:T(8,128)S(1)} %get-tuple-element.28), channel_id=1, source_target_pairs={{0,1},{1,0},{2,3},{3,2},{4,5},{5,4},{6,7},{7,6},{8,9},{9,8},{10,11... | collective-permute-start | bytes 49160 | tf_op jit(solution)/shard_map/ppermute | solution.py:428
  78.4 5.2 %collective-permute-start.5 = (f32[32,128]{1,0:T(8,128)S(1)}, f32[32,128]{1,0:T(8,128)S(1)}, u32[]{:S(2)}, u32[]{:S(2)}) collective-permute-start(f32[32,128]{1,0:T(8,128)S(1)} %add.12), channel_id=1, source_target_pairs={{0,2},{1,3},{2,0},{3,1},{4,6},{5,7},{6,4},{7,5},{8,10},{9,11},{10,... | collective-permute-start | bytes 49160 | tf_op jit(solution)/shard_map/ppermute | solution.py:428
  83.7 5.1 %collective-permute-start.6 = (f32[32,128]{1,0:T(8,128)S(1)}, f32[32,128]{1,0:T(8,128)S(1)}, u32[]{:S(2)}, u32[]{:S(2)}) collective-permute-start(f32[32,128]{1,0:T(8,128)S(1)} %add.13), channel_id=1, source_target_pairs={{0,4},{1,5},{2,6},{3,7},{4,0},{5,1},{6,2},{7,3},{8,12},{9,13},{10,... | collective-permute-start | bytes 49160 | tf_op jit(solution)/shard_map/ppermute | solution.py:428
  88.8 5.5 %collective-permute-start.7 = (f32[32,128]{1,0:T(8,128)S(1)}, f32[32,128]{1,0:T(8,128)S(1)}, u32[]{:S(2)}, u32[]{:S(2)}) collective-permute-start(f32[32,128]{1,0:T(8,128)S(1)} %add.14), channel_id=1, source_target_pairs={{0,8},{1,9},{2,10},{3,11},{4,12},{5,13},{6,14},{7,15},{8,0},{9,1},... | collective-permute-start | bytes 49160 | tf_op jit(solution)/shard_map/ppermute | solution.py:428

commit v5 on v4

--- a/solution.py
+++ b/solution.py
@@ -14,7 +14,7 @@
 ROWS = 32
 ORDER = (("F", 0), ("L", 0), ("F", 1), ("L", 1), ("D", 0), ("D", 1))
 LIMIT = 16
-MANY = 4
+MANY = 8
 STEP = 8
 F32, BF16, I32 = jnp.float32, jnp.bfloat16, jnp.int32
 VMEM = pl.BlockSpec(memory_space=pltpu.VMEM)
@@ -65,13 +65,18 @@
     )
     rank = jnp.sum(named * dot(named.astype(BF16), earlier.astype(BF16)), axis=0, keepdims=True).astype(I32)
     place = dest * 128 + rank
-    slot = lax.broadcasted_iota(I32, (128 * MANY, nodes), 0)
+    column = jnp.broadcast_to(place.astype(F32), (8, nodes)).T[:, :1]
+    place = jnp.broadcast_to(column, (nodes, 128)).astype(I32)
+    lane = lax.broadcasted_iota(I32, (nodes, 128), 1)
 
     def several(step, _):
         total = jnp.zeros((2 * rows16, 128 * MANY), F32)
         for g in range(groups):
-            hot = jnp.where(place + (g * cap - step * 128 * MANY) == slot, 1.0, 0.0).astype(BF16)
-            total = total + lax.dot_general(lhs_ref[g], hot, (((1,), (1,)), ((), ())), preferred_element_type=F32)
+            hot = [
+                jnp.where(place + (g * cap - (step * MANY + h) * 128) == lane, 1.0, 0.0).astype(BF16)
+                for h in range(MANY)
+            ]
+            total = total + dot(lhs_ref[g], jnp.concatenate(hot, axis=1))
         total = total[:rows16] + total[rows16:]
         for h in range(MANY):
             at = pl.multiple_of((step * MANY + h) * rows, 8)

time: 98.8 us -> 98.5 us (level)
  no operation moved by 1% of the time
where the time goes in v5:
time: 98.5 us; the launch traced here: 98.1 us
  Pallas kernels  43.3 us (44%)
  starting transfers between devices  29.1 us (30%)
  waiting for transfers between devices  23.3 us (24%)
  local copies, waits for them, and re-layouts  1.43 us (1%)
    pallas_call x8, Pallas kernels, call(): pl.pallas_call(body, out_shape=out_shape, in_specs=kw.pop('in_specs', [VM...  43.3 us
    all_to_all x1, waiting for transfers between devices, local(): lax.all_to_all(packed, 'slab', split_axis=0, concat_axis=0, tiled=True)  17.3 us
    ppermute x4, starting transfers between devices, local(): lax.ppermute(gram, 'slab', [(i, i ^ reach) for i in range(devices)])  13.1 us
    all_to_all x1, starting transfers between devices, local(): lax.all_to_all(packed, 'slab', split_axis=0, concat_axis=0, tiled=True)  7.39 us
    ppermute x4, waiting for transfers between devices, local(): lax.ppermute(gram, 'slab', [(i, i ^ reach) for i in range(devices)])  5.99 us
    ppermute x2, starting transfers between devices, local(): before = lax.ppermute(final, 'slab', up)  5.85 us
    ppermute x2, starting transfers between devices, local(): after = lax.ppermute(first, 'slab', down)  2.76 us
  transfers between devices with their start and end apart: 9, of which 5 were waited for; matrix products, arithmetic and copies ran while one was open for 0% of the time, Pallas kernels for 22%

profile of v5, /device:TPU:0, one launch (start us, length us, event | category | flops | bytes accessed | tf_op | source)
XLA Modules:
  0.0 98.1 jit_solution(17809839300836078500)
XLA Ops:
  0.6 0.0 copy-start
  0.6 0.0 copy-start.2
  0.7 3.8 %pack.1 = f32[1664,128]{1,0:T(8,128)} custom-call(f32[192,512]{1,0:T(8,128)} %bitcast.11, f32[15,512]{1,0:T(8,128)} %bitcast.12, s32[1,512]{1,0:T(1,128)} %bitcast.13, s32[1,512]{1,0:T(1,128)} %bitcast.14), custom_call_target="tpu_custom_call" | custom-call | tf_op jit(solution)/shard_map/pack/pallas_call | solution.py:37
  4.4 7.4 %all-to-all-start = ((f32[16,104,128]{2,1,0:T(8,128)}), f32[16,104,128]{2,1,0:T(8,128)S(1)}, u32[]{:S(2)}, u32[]{:S(2)}) async-start(f32[16,104,128]{2,1,0:T(8,128)} %bitcast.10), calls=%async_computation | async-start | bytes 1703936 | tf_op jit(solution)/shard_map/all_to_all | solution.py:377
  11.8 0.0 copy-done
  11.8 0.0 copy-done.2
  11.9 0.0 copy-start.1
  11.9 1.4 %copy-done.1 = f32[6,5,5,2048]{3,0,2,1:T(8,128)S(1)} copy-done((f32[6,5,5,2048]{3,0,2,1:T(8,128)S(1)}, f32[6,5,5,2048]{3,0,2,1:T(8,128)}, u32[]{:S(2)}) %copy-start.1) | copy-done | bytes 1228824
  13.3 1.0 %prepare.1 = (f32[200,2048]{1,0:T(8,128)S(1)}, s32[8,2048]{1,0:T(8,128)S(1)}) custom-call(s32[1]{0:T(128)} %bitcast.6.first_ref, s32[6,2048]{1,0:T(8,128)S(1)} %copy-done.2, f32[5,5,6,2048]{3,2,1,0:T(8,128)S(1)} %bitcast.9, f32[5,5,2048]{2,1,0:T(8,128)S(1)} %copy-done), custom_call_target="tpu_custom_call" | custom-call | flops 1000000000 | bytes 10000000 | tf_op jit(solution)/shard_map/prepare/pallas_call | solution.py:37
  14.3 17.3 %all-to-all-done = f32[16,104,128]{2,1,0:T(8,128)S(1)} async-done(((f32[16,104,128]{2,1,0:T(8,128)}), f32[16,104,128]{2,1,0:T(8,128)S(1)}, u32[]{:S(2)}, u32[]{:S(2)}) %all-to-all-start) | async-done | bytes 852000 | tf_op jit(solution)/shard_map/all_to_all | solution.py:377
  31.6 5.0 %forcing.1 = (f32[5,64,2048]{2,1,0:T(8,128)S(1)}, bf16[640,2048]{1,0:T(8,128)(2,1)S(1)}, f32[5,64,256]{2,1,0:T(8,128)S(1)}, f32[5,64,256]{2,1,0:T(8,128)S(1)}) custom-call(f32[1664,128]{1,0:T(8,128)S(1)} %bitcast.8, f32[5,5,2048]{2,1,0:T(8,128)S(1)} %copy-done), custom_call_target="tpu_custom_call" | custom-call | tf_op jit(solution)/shard_map/forcing/pallas_call | solution.py:37
  36.6 2.3 %collective-permute-start = (f32[5,64,256]{2,1,0:T(8,128)S(1)}, f32[5,64,256]{2,1,0:T(8,128)S(1)}, u32[]{:S(2)}, u32[]{:S(2)}) collective-permute-start(f32[5,64,256]{2,1,0:T(8,128)S(1)} %get-tuple-element.18), channel_id=1, source_target_pairs={{0,1},{1,2},{2,3},{3,4},{4,5},{5,6},{6,7},{7,8},{8,9},{9,10},{10,1... | collective-permute-start | bytes 983048 | tf_op jit(solution)/shard_map/ppermute | solution.py:411
  38.9 1.3 %collective-permute-start.1 = (f32[5,64,256]{2,1,0:T(8,128)S(1)}, f32[5,64,256]{2,1,0:T(8,128)S(1)}, u32[]{:S(2)}, u32[]{:S(2)}) collective-permute-start(f32[5,64,256]{2,1,0:T(8,128)S(1)} %get-tuple-element.19), channel_id=1, source_target_pairs={{1,0},{2,1},{3,2},{4,3},{5,4},{6,5},{7,6},{8,7},{9,8},{10,9},{11,1... | collective-permute-start | bytes 983048 | tf_op jit(solution)/shard_map/ppermute | solution.py:412
  40.2 10.5 %inner.1 = (f32[5,64,1536]{2,1,0:T(8,128)S(1)}, bf16[640,1536]{1,0:T(8,128)(2,1)S(1)}) custom-call(f32[5,64,2048]{2,1,0:T(8,128)S(1)} %get-tuple-element.16.x_ref.start_ref, bf16[640,2048]{1,0:T(8,128)(2,1)S(1)} %get-tuple-element.17.two_ref, f32[5,64,2048]{2,1,0:T(8,128)S(1)} %get-tuple-element.16.x_ref.start_ref, ...), custom_call_target="tpu_custom_call" | custom-call | flops 10000000000 | bytes 30000000 | tf_op jit(solution)/shard_map/inner/pallas_call | solution.py:37
  50.7 0.0 collective-permute-done.before_ref
  50.7 0.0 collective-permute-done.1.after_ref
  50.7 3.9 %outer.1 = (f32[5,64,2048]{2,1,0:T(8,128)S(1)}, bf16[640,2048]{1,0:T(8,128)(2,1)S(1)}, f32[5,64,256]{2,1,0:T(8,128)S(1)}, f32[5,64,256]{2,1,0:T(8,128)S(1)}) custom-call(f32[5,64,2048]{2,1,0:T(8,128)S(1)} %get-tuple-element.16.x_ref.start_ref, bf16[640,2048]{1,0:T(8,128)(2,1)S(1)} %get-tuple-element.17.two_ref, ...), custom_call_target="tpu_custom_call" | custom-call | tf_op jit(solution)/shard_map/outer/pallas_call | solution.py:37
  54.6 3.6 %collective-permute-start.2 = (f32[5,64,256]{2,1,0:T(8,128)S(1)}, f32[5,64,256]{2,1,0:T(8,128)S(1)}, u32[]{:S(2)}, u32[]{:S(2)}) collective-permute-start(f32[5,64,256]{2,1,0:T(8,128)S(1)} %get-tuple-element.26), channel_id=1, source_target_pairs={{0,1},{1,2},{2,3},{3,4},{4,5},{5,6},{6,7},{7,8},{8,9},{9,10},{10,1... | collective-permute-start | bytes 983048 | tf_op jit(solution)/shard_map/ppermute | solution.py:411
  58.2 1.5 %collective-permute-start.3 = (f32[5,64,256]{2,1,0:T(8,128)S(1)}, f32[5,64,256]{2,1,0:T(8,128)S(1)}, u32[]{:S(2)}, u32[]{:S(2)}) collective-permute-start(f32[5,64,256]{2,1,0:T(8,128)S(1)} %get-tuple-element.27), channel_id=1, source_target_pairs={{1,0},{2,1},{3,2},{4,3},{5,4},{6,5},{7,6},{8,7},{9,8},{10,9},{11,1... | collective-permute-start | bytes 983048 | tf_op jit(solution)/shard_map/ppermute | solution.py:412
  59.7 10.4 %inner_last.1.refs_0_ = bf16[640,1536]{1,0:T(8,128)(2,1)S(1)} custom-call(f32[5,64,2048]{2,1,0:T(8,128)S(1)} %get-tuple-element.24.x_ref, bf16[640,2048]{1,0:T(8,128)(2,1)S(1)} %get-tuple-element.25.two_ref, f32[5,64,2048]{2,1,0:T(8,128)S(1)} %get-tuple-element.16.x_ref.start_ref, s32[8,2048]{1,0:T(8,128)S(1)} %get-tuple-element.20.place_ref, ...), custom_call_target="tpu_custom_call" | custom-call | flops 10000000000 | bytes 30000000 | tf_op jit(solution)/shard_map/inner_last/pallas_call | solution.py:37
  70.1 0.0 collective-permute-done.2.before_ref
  70.2 0.0 collective-permute-done.3.after_ref
  70.2 4.6 %outer_last.1 = (bf16[640,2048]{1,0:T(8,128)(2,1)S(1)}, f32[32,128]{1,0:T(8,128)S(1)}) custom-call(f32[5,64,2048]{2,1,0:T(8,128)S(1)} %get-tuple-element.24.x_ref, bf16[640,2048]{1,0:T(8,128)(2,1)S(1)} %get-tuple-element.25.two_ref, f32[5,64,256]{2,1,0:T(8,128)S(1)} %collective-permute-done.2.before_ref, f32[5,64,256]{2,1,0:T(8,128)S(1)} %collective-permute-done.3.after_ref, ...), custom_call_target="tpu_custom_call" | custom-call | tf_op jit(solution)/shard_map/outer_last/pallas_call | solution.py:37
  74.8 2.4 %collective-permute-start.4 = (f32[32,128]{1,0:T(8,128)S(1)}, f32[32,128]{1,0:T(8,128)S(1)}, u32[]{:S(2)}, u32[]{:S(2)}) collective-permute-start(f32[32,128]{1,0:T(8,128)S(1)} %get-tuple-element.28), channel_id=1, source_target_pairs={{0,1},{1,0},{2,3},{3,2},{4,5},{5,4},{6,7},{7,6},{8,9},{9,8},{10,11... | collective-permute-start | bytes 49160 | tf_op jit(solution)/shard_map/ppermute | solution.py:433
  77.2 0.8 collective-permute-done.4
  78.0 3.5 %collective-permute-start.5 = (f32[32,128]{1,0:T(8,128)S(1)}, f32[32,128]{1,0:T(8,128)S(1)}, u32[]{:S(2)}, u32[]{:S(2)}) collective-permute-start(f32[32,128]{1,0:T(8,128)S(1)} %add.12), channel_id=1, source_target_pairs={{0,2},{1,3},{2,0},{3,1},{4,6},{5,7},{6,4},{7,5},{8,10},{9,11},{10,... | collective-permute-start | bytes 49160 | tf_op jit(solution)/shard_map/ppermute | solution.py:433
  81.6 1.7 %collective-permute-done.5 = f32[32,128]{1,0:T(8,128)S(1)} collective-permute-done((f32[32,128]{1,0:T(8,128)S(1)}, f32[32,128]{1,0:T(8,128)S(1)}, u32[]{:S(2)}, u32[]{:S(2)}) %collective-permute-start.5) | collective-permute-done | bytes 16416 | tf_op jit(solution)/shard_map/ppermute | solution.py:433
  83.3 3.4 %collective-permute-start.6 = (f32[32,128]{1,0:T(8,128)S(1)}, f32[32,128]{1,0:T(8,128)S(1)}, u32[]{:S(2)}, u32[]{:S(2)}) collective-permute-start(f32[32,128]{1,0:T(8,128)S(1)} %add.13), channel_id=1, source_target_pairs={{0,4},{1,5},{2,6},{3,7},{4,0},{5,1},{6,2},{7,3},{8,12},{9,13},{10,... | collective-permute-start | bytes 49160 | tf_op jit(solution)/shard_map/ppermute | solution.py:433
  86.7 1.7 %collective-permute-done.6 = f32[32,128]{1,0:T(8,128)S(1)} collective-permute-done((f32[32,128]{1,0:T(8,128)S(1)}, f32[32,128]{1,0:T(8,128)S(1)}, u32[]{:S(2)}, u32[]{:S(2)}) %collective-permute-start.6) | collective-permute-done | bytes 16416 | tf_op jit(solution)/shard_map/ppermute | solution.py:433
  88.4 3.7 %collective-permute-start.7 = (f32[32,128]{1,0:T(8,128)S(1)}, f32[32,128]{1,0:T(8,128)S(1)}, u32[]{:S(2)}, u32[]{:S(2)}) collective-permute-start(f32[32,128]{1,0:T(8,128)S(1)} %add.14), channel_id=1, source_target_pairs={{0,8},{1,9},{2,10},{3,11},{4,12},{5,13},{6,14},{7,15},{8,0},{9,1},... | collective-permute-start | bytes 49160 | tf_op jit(solution)/shard_map/ppermute | solution.py:433
  92.2 1.7 %collective-permute-done.7 = f32[32,128]{1,0:T(8,128)S(1)} collective-permute-done((f32[32,128]{1,0:T(8,128)S(1)}, f32[32,128]{1,0:T(8,128)S(1)}, u32[]{:S(2)}, u32[]{:S(2)}) %collective-permute-start.7) | collective-permute-done | bytes 16416 | tf_op jit(solution)/shard_map/ppermute | solution.py:433
  93.9 4.1 %basis.1 = (f32[5,64,2048]{2,1,0:T(8,128)}, f32[64,64]{1,0:T(8,128)}) custom-call(f32[32,128]{1,0:T(8,128)S(1)} %add.15.gram_ref, bf16[640,2048]{1,0:T(8,128)(2,1)S(1)} %get-tuple-element.29.field_ref), custom_call_target="tpu_custom_call" | custom-call | tf_op jit(solution)/shard_map/basis/pallas_call | solution.py:37
  (4 shorter events, 0.0 us)
Async XLA Ops:
  0.6 11.2 %copy-start = (f32[5,5,2048]{2,1,0:T(8,128)S(1)}, f32[5,5,2048]{2,1,0:T(8,128)}, u32[]{:S(2)}) copy-start(f32[5,5,2048]{2,1,0:T(8,128)} %inv_ref.3) | copy-start | bytes 614404
  0.6 11.2 %copy-start.2 = (s32[6,2048]{1,0:T(8,128)S(1)}, s32[6,2048]{1,0:T(8,128)}, u32[]{:S(2)}) copy-start(s32[6,2048]{1,0:T(8,128)} %neighbours_ref.1) | copy-start | bytes 147460
  4.4 27.2 %all-to-all-start = ((f32[16,104,128]{2,1,0:T(8,128)}), f32[16,104,128]{2,1,0:T(8,128)S(1)}, u32[]{:S(2)}, u32[]{:S(2)}) async-start(f32[16,104,128]{2,1,0:T(8,128)} %bitcast.10), calls=%async_computation | async-start | bytes 1703936 | tf_op jit(solution)/shard_map/all_to_all | solution.py:377
  11.9 1.4 %copy-start.1 = (f32[6,5,5,2048]{3,0,2,1:T(8,128)S(1)}, f32[6,5,5,2048]{3,0,2,1:T(8,128)}, u32[]{:S(2)}) copy-start(f32[6,5,5,2048]{3,0,2,1:T(8,128)} %param.12) | copy-start | bytes 3686404
  36.6 14.1 %collective-permute-start = (f32[5,64,256]{2,1,0:T(8,128)S(1)}, f32[5,64,256]{2,1,0:T(8,128)S(1)}, u32[]{:S(2)}, u32[]{:S(2)}) collective-permute-start(f32[5,64,256]{2,1,0:T(8,128)S(1)} %get-tuple-element.18), channel_id=1, source_target_pairs={{0,1},{1,2},{2,3},{3,4},{4,5},{5,6},{6,7},{7,8},{8,9},{9,10},{10,1... | collective-permute-start | bytes 983048 | tf_op jit(solution)/shard_map/ppermute | solution.py:411
  38.9 11.8 %collective-permute-start.1 = (f32[5,64,256]{2,1,0:T(8,128)S(1)}, f32[5,64,256]{2,1,0:T(8,128)S(1)}, u32[]{:S(2)}, u32[]{:S(2)}) collective-permute-start(f32[5,64,256]{2,1,0:T(8,128)S(1)} %get-tuple-element.19), channel_id=1, source_target_pairs={{1,0},{2,1},{3,2},{4,3},{5,4},{6,5},{7,6},{8,7},{9,8},{10,9},{11,1... | collective-permute-start | bytes 983048 | tf_op jit(solution)/shard_map/ppermute | solution.py:412
  54.6 15.5 %collective-permute-start.2 = (f32[5,64,256]{2,1,0:T(8,128)S(1)}, f32[5,64,256]{2,1,0:T(8,128)S(1)}, u32[]{:S(2)}, u32[]{:S(2)}) collective-permute-start(f32[5,64,256]{2,1,0:T(8,128)S(1)} %get-tuple-element.26), channel_id=1, source_target_pairs={{0,1},{1,2},{2,3},{3,4},{4,5},{5,6},{6,7},{7,8},{8,9},{9,10},{10,1... | collective-permute-start | bytes 983048 | tf_op jit(solution)/shard_map/ppermute | solution.py:411
  58.2 11.9 %collective-permute-start.3 = (f32[5,64,256]{2,1,0:T(8,128)S(1)}, f32[5,64,256]{2,1,0:T(8,128)S(1)}, u32[]{:S(2)}, u32[]{:S(2)}) collective-permute-start(f32[5,64,256]{2,1,0:T(8,128)S(1)} %get-tuple-element.27), channel_id=1, source_target_pairs={{1,0},{2,1},{3,2},{4,3},{5,4},{6,5},{7,6},{8,7},{9,8},{10,9},{11,1... | collective-permute-start | bytes 983048 | tf_op jit(solution)/shard_map/ppermute | solution.py:412
  74.8 3.2 %collective-permute-start.4 = (f32[32,128]{1,0:T(8,128)S(1)}, f32[32,128]{1,0:T(8,128)S(1)}, u32[]{:S(2)}, u32[]{:S(2)}) collective-permute-start(f32[32,128]{1,0:T(8,128)S(1)} %get-tuple-element.28), channel_id=1, source_target_pairs={{0,1},{1,0},{2,3},{3,2},{4,5},{5,4},{6,7},{7,6},{8,9},{9,8},{10,11... | collective-permute-start | bytes 49160 | tf_op jit(solution)/shard_map/ppermute | solution.py:433
  78.0 5.2 %collective-permute-start.5 = (f32[32,128]{1,0:T(8,128)S(1)}, f32[32,128]{1,0:T(8,128)S(1)}, u32[]{:S(2)}, u32[]{:S(2)}) collective-permute-start(f32[32,128]{1,0:T(8,128)S(1)} %add.12), channel_id=1, source_target_pairs={{0,2},{1,3},{2,0},{3,1},{4,6},{5,7},{6,4},{7,5},{8,10},{9,11},{10,... | collective-permute-start | bytes 49160 | tf_op jit(solution)/shard_map/ppermute | solution.py:433
  83.3 5.1 %collective-permute-start.6 = (f32[32,128]{1,0:T(8,128)S(1)}, f32[32,128]{1,0:T(8,128)S(1)}, u32[]{:S(2)}, u32[]{:S(2)}) collective-permute-start(f32[32,128]{1,0:T(8,128)S(1)} %add.13), channel_id=1, source_target_pairs={{0,4},{1,5},{2,6},{3,7},{4,0},{5,1},{6,2},{7,3},{8,12},{9,13},{10,... | collective-permute-start | bytes 49160 | tf_op jit(solution)/shard_map/ppermute | solution.py:433
  88.4 5.5 %collective-permute-start.7 = (f32[32,128]{1,0:T(8,128)S(1)}, f32[32,128]{1,0:T(8,128)S(1)}, u32[]{:S(2)}, u32[]{:S(2)}) collective-permute-start(f32[32,128]{1,0:T(8,128)S(1)} %add.14), channel_id=1, source_target_pairs={{0,8},{1,9},{2,10},{3,11},{4,12},{5,13},{6,14},{7,15},{8,0},{9,1},... | collective-permute-start | bytes 49160 | tf_op jit(solution)/shard_map/ppermute | solution.py:433

commit v6 on v5

--- a/solution.py
+++ b/solution.py
@@ -408,8 +408,13 @@
     ]
     cost = pl.CostEstimate(flops=10**10, bytes_accessed=3 * 10**7, transcendentals=0)
     for last in (False, True):
-        before = lax.ppermute(final, "slab", up)
-        after = lax.ppermute(first, "slab", down)
+        pairs = [(i, i ^ 1) for i in range(devices)]
+        shifted = [(i, i + 1) for i in range(1, devices - 1, 2)]
+        shifted = shifted + [(j, i) for i, j in shifted]
+        even = lax.axis_index("slab") % 2 == 0
+        one = lax.ppermute(jnp.where(even, final, first), "slab", pairs)
+        other = lax.ppermute(jnp.where(even, first, final), "slab", shifted)
+        before, after = jnp.where(even, other, one), jnp.where(even, one, other)
         middle = call(
             functools.partial(inner_body, rim, last), (mid_two,) if last else (mid, mid_two),
             x, two, start, place, blocks, scratch=fetched, cost_estimate=cost, name="inner_last" if last else "inner",

time: 98.5 us -> 93 us (0.944)
  starting transfers between devices: 29.1 us -> 21.3 us
  waiting for transfers between devices: 23.3 us -> 25.4 us
    ppermute x4, starting transfers between devices: 13.1 us -> 8.83 us  [local(): lax.ppermute(gram, 'slab', [(i, i ^ reach) for i in range(devices)])]
    ppermute x4, starting transfers between devices: 8.62 us -> 5.04 us  [the longest x2 3.53 us: local(): one = lax.ppermute(jnp.where(even, final, first), 'slab', pairs)]
    ppermute x4, waiting for transfers between devices: 5.99 us -> 8.12 us  [local(): lax.ppermute(gram, 'slab', [(i, i ^ reach) for i in range(devices)])]
  transfers between devices with their start and end apart: 9 -> 9, of which waited for: 5 -> 5; matrix products, arithmetic and copies ran while one was open for 0% -> 0% of each run, Pallas kernels for 22% -> 24%
where the time goes in v6:
time: 93 us; the launch traced here: 92.7 us
  Pallas kernels  43.3 us (47%)
  waiting for transfers between devices  25.4 us (27%)
  starting transfers between devices  21.3 us (23%)
  local copies, waits for them, and re-layouts  1.43 us (2%)
  between operations  0.98 us (1%)
    pallas_call x8, Pallas kernels, call(): pl.pallas_call(body, out_shape=out_shape, in_specs=kw.pop('in_specs', [VM...  43.3 us
    all_to_all x1, waiting for transfers between devices, local(): lax.all_to_all(packed, 'slab', split_axis=0, concat_axis=0, tiled=True)  17.3 us
    ppermute x4, starting transfers between devices, local(): lax.ppermute(gram, 'slab', [(i, i ^ reach) for i in range(devices)])  8.83 us
    ppermute x4, waiting for transfers between devices, local(): lax.ppermute(gram, 'slab', [(i, i ^ reach) for i in range(devices)])  8.12 us
    all_to_all x1, starting transfers between devices, local(): lax.all_to_all(packed, 'slab', split_axis=0, concat_axis=0, tiled=True)  7.39 us
    ppermute x2, starting transfers between devices, local(): one = lax.ppermute(jnp.where(even, final, first), 'slab', pairs)  3.53 us
  transfers between devices with their start and end apart: 9, of which 5 were waited for; matrix products, arithmetic and copies ran while one was open for 0% of the time, Pallas kernels for 24%

profile of v6, /device:TPU:0, one launch (start us, length us, event | category | flops | bytes accessed | tf_op | source)
XLA Modules:
  0.0 92.7 jit_solution(17739069128014109471)
XLA Ops:
  0.7 3.8 %pack.1 = f32[1664,128]{1,0:T(8,128)} custom-call(f32[192,512]{1,0:T(8,128)} %bitcast.11, f32[15,512]{1,0:T(8,128)} %bitcast.12, s32[1,512]{1,0:T(1,128)} %bitcast.13, s32[1,512]{1,0:T(1,128)} %bitcast.14), custom_call_target="tpu_custom_call" | custom-call | tf_op jit(solution)/shard_map/pack/pallas_call | solution.py:37
  4.4 7.4 %all-to-all-start = ((f32[16,104,128]{2,1,0:T(8,128)}), f32[16,104,128]{2,1,0:T(8,128)S(1)}, u32[]{:S(2)}, u32[]{:S(2)}) async-start(f32[16,104,128]{2,1,0:T(8,128)} %bitcast.10), calls=%async_computation | async-start | bytes 1703936 | tf_op jit(solution)/shard_map/all_to_all | solution.py:377
  11.9 0.0 copy-start.1
  11.9 1.4 %copy-done.1 = f32[6,5,5,2048]{3,0,2,1:T(8,128)S(1)} copy-done((f32[6,5,5,2048]{3,0,2,1:T(8,128)S(1)}, f32[6,5,5,2048]{3,0,2,1:T(8,128)}, u32[]{:S(2)}) %copy-start.1) | copy-done | bytes 1228824
  13.3 1.0 %prepare.1 = (f32[200,2048]{1,0:T(8,128)S(1)}, s32[8,2048]{1,0:T(8,128)S(1)}) custom-call(s32[1]{0:T(128)} %bitcast.6.first_ref, s32[6,2048]{1,0:T(8,128)S(1)} %copy-done.2, f32[5,5,6,2048]{3,2,1,0:T(8,128)S(1)} %bitcast.9, f32[5,5,2048]{2,1,0:T(8,128)S(1)} %copy-done), custom_call_target="tpu_custom_call" | custom-call | flops 1000000000 | bytes 10000000 | tf_op jit(solution)/shard_map/prepare/pallas_call | solution.py:37
  14.3 17.3 %all-to-all-done = f32[16,104,128]{2,1,0:T(8,128)S(1)} async-done(((f32[16,104,128]{2,1,0:T(8,128)}), f32[16,104,128]{2,1,0:T(8,128)S(1)}, u32[]{:S(2)}, u32[]{:S(2)}) %all-to-all-start) | async-done | bytes 852000 | tf_op jit(solution)/shard_map/all_to_all | solution.py:377
  31.6 5.0 %forcing.1 = (f32[5,64,2048]{2,1,0:T(8,128)S(1)}, bf16[640,2048]{1,0:T(8,128)(2,1)S(1)}, f32[5,64,256]{2,1,0:T(8,128)S(1)}, f32[5,64,256]{2,1,0:T(8,128)S(1)}) custom-call(f32[1664,128]{1,0:T(8,128)S(1)} %bitcast.8, f32[5,5,2048]{2,1,0:T(8,128)S(1)} %copy-done), custom_call_target="tpu_custom_call" | custom-call | tf_op jit(solution)/shard_map/forcing/pallas_call | solution.py:37
  36.6 0.1 broadcast_select_fusion.6
  36.7 0.4 collective-permute-start.1
  37.1 0.7 collective-permute-start
  37.8 10.5 %inner.1 = (f32[5,64,1536]{2,1,0:T(8,128)S(1)}, bf16[640,1536]{1,0:T(8,128)(2,1)S(1)}) custom-call(f32[5,64,2048]{2,1,0:T(8,128)S(1)} %get-tuple-element.16.x_ref.start_ref, bf16[640,2048]{1,0:T(8,128)(2,1)S(1)} %get-tuple-element.17.two_ref, f32[5,64,2048]{2,1,0:T(8,128)S(1)} %get-tuple-element.16.x_ref.start_ref, ...), custom_call_target="tpu_custom_call" | custom-call | flops 10000000000 | bytes 30000000 | tf_op jit(solution)/shard_map/inner/pallas_call | solution.py:37
  48.3 0.0 collective-permute-done.1
  48.3 0.0 collective-permute-done
  48.3 0.1 broadcast_select_fusion.4
  48.4 3.9 %outer.1 = (f32[5,64,2048]{2,1,0:T(8,128)S(1)}, bf16[640,2048]{1,0:T(8,128)(2,1)S(1)}, f32[5,64,256]{2,1,0:T(8,128)S(1)}, f32[5,64,256]{2,1,0:T(8,128)S(1)}) custom-call(f32[5,64,2048]{2,1,0:T(8,128)S(1)} %get-tuple-element.16.x_ref.start_ref, bf16[640,2048]{1,0:T(8,128)(2,1)S(1)} %get-tuple-element.17.two_ref, ...), custom_call_target="tpu_custom_call" | custom-call | tf_op jit(solution)/shard_map/outer/pallas_call | solution.py:37
  52.3 0.1 broadcast_select_fusion.2
  52.3 3.1 %collective-permute-start.3 = (f32[5,64,256]{2,1,0:T(8,128)S(1)}, f32[5,64,256]{2,1,0:T(8,128)S(1)}, u32[]{:S(2)}, u32[]{:S(2)}) collective-permute-start(f32[5,64,256]{2,1,0:T(8,128)S(1)} %get-tuple-element.32), channel_id=1, source_target_pairs={{0,1},{1,0},{2,3},{3,2},{4,5},{5,4},{6,7},{7,6},{8,9},{9,8},{10,11... | collective-permute-start | bytes 983048 | tf_op jit(solution)/shard_map/ppermute | solution.py:415
  55.4 0.8 collective-permute-start.2
  56.3 10.4 %inner_last.1.refs_0_ = bf16[640,1536]{1,0:T(8,128)(2,1)S(1)} custom-call(f32[5,64,2048]{2,1,0:T(8,128)S(1)} %get-tuple-element.24.x_ref, bf16[640,2048]{1,0:T(8,128)(2,1)S(1)} %get-tuple-element.25.two_ref, f32[5,64,2048]{2,1,0:T(8,128)S(1)} %get-tuple-element.16.x_ref.start_ref, s32[8,2048]{1,0:T(8,128)S(1)} %get-tuple-element.20.place_ref, ...), custom_call_target="tpu_custom_call" | custom-call | flops 10000000000 | bytes 30000000 | tf_op jit(solution)/shard_map/inner_last/pallas_call | solution.py:37
  66.7 0.0 collective-permute-done.3
  66.7 0.0 collective-permute-done.2
  66.8 0.1 broadcast_select_fusion
  66.8 4.6 %outer_last.1 = (bf16[640,2048]{1,0:T(8,128)(2,1)S(1)}, f32[32,128]{1,0:T(8,128)S(1)}) custom-call(f32[5,64,2048]{2,1,0:T(8,128)S(1)} %get-tuple-element.24.x_ref, bf16[640,2048]{1,0:T(8,128)(2,1)S(1)} %get-tuple-element.25.two_ref, f32[5,64,256]{2,1,0:T(8,128)S(1)} %get-tuple-element.31.before_ref, f32[5,64,256]{2,1,0:T(8,128)S(1)} %get-tuple-element.30.after_ref, ...), custom_call_target="tpu_custom_call" | custom-call | tf_op jit(solution)/shard_map/outer_last/pallas_call | solution.py:37
  71.5 4.0 %collective-permute-start.4 = (f32[32,128]{1,0:T(8,128)S(1)}, f32[32,128]{1,0:T(8,128)S(1)}, u32[]{:S(2)}, u32[]{:S(2)}) collective-permute-start(f32[32,128]{1,0:T(8,128)S(1)} %get-tuple-element.28), channel_id=1, source_target_pairs={{0,1},{1,0},{2,3},{3,2},{4,5},{5,4},{6,7},{7,6},{8,9},{9,8},{10,11... | collective-permute-start | bytes 49160 | tf_op jit(solution)/shard_map/ppermute | solution.py:438
  75.5 0.8 collective-permute-done.4
  76.3 1.2 %collective-permute-start.5 = (f32[32,128]{1,0:T(8,128)S(1)}, f32[32,128]{1,0:T(8,128)S(1)}, u32[]{:S(2)}, u32[]{:S(2)}) collective-permute-start(f32[32,128]{1,0:T(8,128)S(1)} %add.18), channel_id=1, source_target_pairs={{0,2},{1,3},{2,0},{3,1},{4,6},{5,7},{6,4},{7,5},{8,10},{9,11},{10,... | collective-permute-start | bytes 49160 | tf_op jit(solution)/shard_map/ppermute | solution.py:438
  77.5 2.5 %collective-permute-done.5 = f32[32,128]{1,0:T(8,128)S(1)} collective-permute-done((f32[32,128]{1,0:T(8,128)S(1)}, f32[32,128]{1,0:T(8,128)S(1)}, u32[]{:S(2)}, u32[]{:S(2)}) %collective-permute-start.5) | collective-permute-done | bytes 16416 | tf_op jit(solution)/shard_map/ppermute | solution.py:438
  80.0 1.4 %collective-permute-start.6 = (f32[32,128]{1,0:T(8,128)S(1)}, f32[32,128]{1,0:T(8,128)S(1)}, u32[]{:S(2)}, u32[]{:S(2)}) collective-permute-start(f32[32,128]{1,0:T(8,128)S(1)} %add.19), channel_id=1, source_target_pairs={{0,4},{1,5},{2,6},{3,7},{4,0},{5,1},{6,2},{7,3},{8,12},{9,13},{10,... | collective-permute-start | bytes 49160 | tf_op jit(solution)/shard_map/ppermute | solution.py:438
  81.5 2.3 %collective-permute-done.6 = f32[32,128]{1,0:T(8,128)S(1)} collective-permute-done((f32[32,128]{1,0:T(8,128)S(1)}, f32[32,128]{1,0:T(8,128)S(1)}, u32[]{:S(2)}, u32[]{:S(2)}) %collective-permute-start.6) | collective-permute-done | bytes 16416 | tf_op jit(solution)/shard_map/ppermute | solution.py:438
  83.8 2.2 %collective-permute-start.7 = (f32[32,128]{1,0:T(8,128)S(1)}, f32[32,128]{1,0:T(8,128)S(1)}, u32[]{:S(2)}, u32[]{:S(2)}) collective-permute-start(f32[32,128]{1,0:T(8,128)S(1)} %add.20), channel_id=1, source_target_pairs={{0,8},{1,9},{2,10},{3,11},{4,12},{5,13},{6,14},{7,15},{8,0},{9,1},... | collective-permute-start | bytes 49160 | tf_op jit(solution)/shard_map/ppermute | solution.py:438
  86.0 2.5 %collective-permute-done.7 = f32[32,128]{1,0:T(8,128)S(1)} collective-permute-done((f32[32,128]{1,0:T(8,128)S(1)}, f32[32,128]{1,0:T(8,128)S(1)}, u32[]{:S(2)}, u32[]{:S(2)}) %collective-permute-start.7) | collective-permute-done | bytes 16416 | tf_op jit(solution)/shard_map/ppermute | solution.py:438
  88.4 4.1 %basis.1 = (f32[5,64,2048]{2,1,0:T(8,128)}, f32[64,64]{1,0:T(8,128)}) custom-call(f32[32,128]{1,0:T(8,128)S(1)} %add.21.gram_ref, bf16[640,2048]{1,0:T(8,128)(2,1)S(1)} %get-tuple-element.29.field_ref), custom_call_target="tpu_custom_call" | custom-call | tf_op jit(solution)/shard_map/basis/pallas_call | solution.py:37
  (8 shorter events, 0.0 us)
Async XLA Ops:
  0.6 11.2 %copy-start = (f32[5,5,2048]{2,1,0:T(8,128)S(1)}, f32[5,5,2048]{2,1,0:T(8,128)}, u32[]{:S(2)}) copy-start(f32[5,5,2048]{2,1,0:T(8,128)} %inv_ref.3) | copy-start | bytes 614404
  0.6 11.2 %copy-start.2 = (s32[6,2048]{1,0:T(8,128)S(1)}, s32[6,2048]{1,0:T(8,128)}, u32[]{:S(2)}) copy-start(s32[6,2048]{1,0:T(8,128)} %neighbours_ref.1) | copy-start | bytes 147460
  4.4 27.2 %all-to-all-start = ((f32[16,104,128]{2,1,0:T(8,128)}), f32[16,104,128]{2,1,0:T(8,128)S(1)}, u32[]{:S(2)}, u32[]{:S(2)}) async-start(f32[16,104,128]{2,1,0:T(8,128)} %bitcast.10), calls=%async_computation | async-start | bytes 1703936 | tf_op jit(solution)/shard_map/all_to_all | solution.py:377
  11.9 1.4 %copy-start.1 = (f32[6,5,5,2048]{3,0,2,1:T(8,128)S(1)}, f32[6,5,5,2048]{3,0,2,1:T(8,128)}, u32[]{:S(2)}) copy-start(f32[6,5,5,2048]{3,0,2,1:T(8,128)} %param.12) | copy-start | bytes 3686404
  36.7 11.6 %collective-permute-start.1 = (f32[5,64,256]{2,1,0:T(8,128)S(1)}, f32[5,64,256]{2,1,0:T(8,128)S(1)}, u32[]{:S(2)}, u32[]{:S(2)}) collective-permute-start(f32[5,64,256]{2,1,0:T(8,128)S(1)} %get-tuple-element.36), channel_id=1, source_target_pairs={{0,1},{1,0},{2,3},{3,2},{4,5},{5,4},{6,7},{7,6},{8,9},{9,8},{10,11... | collective-permute-start | bytes 983048 | tf_op jit(solution)/shard_map/ppermute | solution.py:415
  37.1 11.2 %collective-permute-start = (f32[5,64,256]{2,1,0:T(8,128)S(1)}, f32[5,64,256]{2,1,0:T(8,128)S(1)}, u32[]{:S(2)}, u32[]{:S(2)}) collective-permute-start(f32[5,64,256]{2,1,0:T(8,128)S(1)} %get-tuple-element.37), channel_id=1, source_target_pairs={{1,2},{3,4},{5,6},{7,8},{9,10},{11,12},{13,14},{2,1},{4,3},{6,5},{... | collective-permute-start | bytes 983048 | tf_op jit(solution)/shard_map/ppermute | solution.py:416
  52.3 14.4 %collective-permute-start.3 = (f32[5,64,256]{2,1,0:T(8,128)S(1)}, f32[5,64,256]{2,1,0:T(8,128)S(1)}, u32[]{:S(2)}, u32[]{:S(2)}) collective-permute-start(f32[5,64,256]{2,1,0:T(8,128)S(1)} %get-tuple-element.32), channel_id=1, source_target_pairs={{0,1},{1,0},{2,3},{3,2},{4,5},{5,4},{6,7},{7,6},{8,9},{9,8},{10,11... | collective-permute-start | bytes 983048 | tf_op jit(solution)/shard_map/ppermute | solution.py:415
  55.4 11.3 %collective-permute-start.2 = (f32[5,64,256]{2,1,0:T(8,128)S(1)}, f32[5,64,256]{2,1,0:T(8,128)S(1)}, u32[]{:S(2)}, u32[]{:S(2)}) collective-permute-start(f32[5,64,256]{2,1,0:T(8,128)S(1)} %get-tuple-element.33), channel_id=1, source_target_pairs={{1,2},{3,4},{5,6},{7,8},{9,10},{11,12},{13,14},{2,1},{4,3},{6,5},{... | collective-permute-start | bytes 983048 | tf_op jit(solution)/shard_map/ppermute | solution.py:416
  71.5 4.8 %collective-permute-start.4 = (f32[32,128]{1,0:T(8,128)S(1)}, f32[32,128]{1,0:T(8,128)S(1)}, u32[]{:S(2)}, u32[]{:S(2)}) collective-permute-start(f32[32,128]{1,0:T(8,128)S(1)} %get-tuple-element.28), channel_id=1, source_target_pairs={{0,1},{1,0},{2,3},{3,2},{4,5},{5,4},{6,7},{7,6},{8,9},{9,8},{10,11... | collective-permute-start | bytes 49160 | tf_op jit(solution)/shard_map/ppermute | solution.py:438
  76.3 3.7 %collective-permute-start.5 = (f32[32,128]{1,0:T(8,128)S(1)}, f32[32,128]{1,0:T(8,128)S(1)}, u32[]{:S(2)}, u32[]{:S(2)}) collective-permute-start(f32[32,128]{1,0:T(8,128)S(1)} %add.18), channel_id=1, source_target_pairs={{0,2},{1,3},{2,0},{3,1},{4,6},{5,7},{6,4},{7,5},{8,10},{9,11},{10,... | collective-permute-start | bytes 49160 | tf_op jit(solution)/shard_map/ppermute | solution.py:438
  80.0 3.7 %collective-permute-start.6 = (f32[32,128]{1,0:T(8,128)S(1)}, f32[32,128]{1,0:T(8,128)S(1)}, u32[]{:S(2)}, u32[]{:S(2)}) collective-permute-start(f32[32,128]{1,0:T(8,128)S(1)} %add.19), channel_id=1, source_target_pairs={{0,4},{1,5},{2,6},{3,7},{4,0},{5,1},{6,2},{7,3},{8,12},{9,13},{10,... | collective-permute-start | bytes 49160 | tf_op jit(solution)/shard_map/ppermute | solution.py:438
  83.8 4.6 %collective-permute-start.7 = (f32[32,128]{1,0:T(8,128)S(1)}, f32[32,128]{1,0:T(8,128)S(1)}, u32[]{:S(2)}, u32[]{:S(2)}) collective-permute-start(f32[32,128]{1,0:T(8,128)S(1)} %add.20), channel_id=1, source_target_pairs={{0,8},{1,9},{2,10},{3,11},{4,12},{5,13},{6,14},{7,15},{8,0},{9,1},... | collective-permute-start | bytes 49160 | tf_op jit(solution)/shard_map/ppermute | solution.py:438
